TPU v7x, 512 devices: a whole 4x4x16 slice. The times are simulated.
512 devices in a mesh: row: 16 (over z_lo, core), col: 32 (over y, x, z_hi).
Axes of the slice: x: 4, y: 4, z: 16 (z_hi: 2, z_lo: 8; z = z_hi * 8 + z_lo), core: 2. Of those that a mesh axis runs over, the one named last changes fastest.
Arguments:
- tokens: bfloat16 [1280, 12288], P('col', 'row'), may hold values from -6 to 6
- inner_weight: bfloat16 [12288, 24576], P('row', 'col'), may hold values from -0.0546875 to 0.0546875
- inner_bias: bfloat16 [24576], P('col'), may hold values from -3 to 3
- outer_weight: bfloat16 [24576, 12288], P('col', 'row'), may hold values from -0.0390625 to 0.0390625
- outer_bias: bfloat16 [12288], P('row'), may hold values from -3 to 3
Outputs:
- block_output: bfloat16 [1280, 12288], P('col', 'row')
All inputs are finite; a program needn't handle non-finite values.
Results may differ from a plain program's by a relative error of at most 0.028.
Values may be sent and summed in bfloat16 or wider, within the bound.
No kernel may reach another device: no remote copies, remote signals or barrier semaphores. Data moves between devices by JAX's collectives and lax.ppermute only.
A program may use at most 64 MiB of HBM per device.

v0:
```python
import jax
import jax.numpy as jnp
from jax import lax
from jax.sharding import PartitionSpec as P


def shards(tokens, inner_weight, inner_bias, outer_weight, outer_bias):
    partial_value = jnp.dot(
        lax.all_gather(tokens, "col", axis=0, tiled=True),
        inner_weight,
        preferred_element_type=jnp.float32,
    )
    bias_wide = inner_bias.astype(jnp.float32)
    preact = lax.psum(partial_value.astype(jnp.bfloat16), "row").astype(jnp.float32)
    hidden = jax.nn.gelu(preact + bias_wide, approximate=True).astype(jnp.bfloat16)
    summed = lax.psum_scatter(
        jnp.dot(hidden, outer_weight, preferred_element_type=jnp.float32).astype(jnp.bfloat16),
        "col",
        scatter_dimension=0,
        tiled=True,
    ).astype(jnp.float32)
    return (summed + outer_bias.astype(jnp.float32)).astype(jnp.bfloat16)


def solution(mesh):
    in_specs = (P("col", "row"), P("row", "col"), P("col"), P("col", "row"), P("row"))
    out_specs = P("col", "row")
    return jax.shard_map(shards, mesh=mesh, in_specs=in_specs, out_specs=out_specs, check_vma=False)
```

profile of v0, /device:TPU:1, one launch (start us, length us, event | category | flops | bytes accessed | tf_op | source)
XLA Modules:
  0.0 678.4 jit_solution(2317913726141311824)
XLA Ops:
  6.5 0.0 copy-start
  6.5 0.0 all-gather.2.cloned.1.call-start
  6.5 0.7 all-gather.2.cloned.1.call-update
  7.3 0.0 all-reduce.2.cloned.1.call-start
  7.3 136.0 %all-gather.2.cloned.1.call-done = bf16[1280,768]{1,0:T(8,128)(2,1)} async-done(((bf16[40,768]{1,0:T(8,128)(2,1)}), bf16[1280,768]{1,0:T(8,128)(2,1)}) %all-gather.2.cloned.1.call-update) | async-done | bytes 1966096 | tf_op jit(solution)/shard_map/all_gather | solution.py:9
  143.3 0.0 copy-done
  143.3 4.5 convolution_convert_fusion.1
  147.8 0.0 copy-start.1
  147.8 0.0 copy-start.3
  147.8 0.0 all-reduce.2.cloned.1.call-update
  147.8 0.0 reduce-scatter.2.cloned.1.call-start
  147.9 0.6 copy-done.1
  148.5 195.6 %all-reduce.2.cloned.1.call-done = bf16[1280,768]{1,0:T(8,128)(2,1)} async-done(((bf16[1280,768]{1,0:T(8,128)(2,1)}), bf16[1280,768]{1,0:T(8,128)(2,1)}) %all-reduce.2.cloned.1.call-update) | async-done | bytes 1966096 | tf_op jit(solution)/shard_map/psum | solution.py:14
  344.1 0.0 copy-done.3
  344.1 5.5 convolution_convert_fusion
  349.6 0.0 copy-start.2
  349.6 0.0 reduce-scatter.2.cloned.1.call-update
  349.6 0.7 copy-done.2
  350.3 320.1 %reduce-scatter.2.cloned.1.call-done = bf16[40,768]{1,0:T(8,128)(2,1)} async-done(((bf16[1280,768]{1,0:T(8,128)(2,1)}), bf16[40,768]{1,0:T(8,128)(2,1)}) %reduce-scatter.2.cloned.1.call-update) | async-done | bytes 61456 | tf_op jit(solution)/shard_map/reduce_scatter | solution.py:16
  670.4 1.5 add_convert_fusion
  (2 shorter events, 0.0 us)
Async XLA Ops:
  6.5 136.7 %copy-start = (bf16[768,768]{1,0:T(8,128)(2,1)S(1)}, bf16[768,768]{1,0:T(8,128)(2,1)}, u32[]{:S(2)}) copy-start(bf16[768,768]{1,0:T(8,128)(2,1)} %param.6) | copy-start | bytes 3538948
  6.5 136.7 %all-gather.2.cloned.1.call-start = ((), (), s32[]{:S(2)}) async-start(), calls=%async_computation.1 | async-start | bytes 2027520 | tf_op jit(solution)/shard_map/all_gather | solution.py:9
  7.3 336.8 %all-reduce.2.cloned.1.call-start = ((), (), s32[]{:S(2)}) async-start(), calls=%async_computation.2 | async-start | bytes 3932160 | tf_op jit(solution)/shard_map/psum | solution.py:14
  147.8 0.7 copy-start.1
  147.8 196.3 %copy-start.3 = (bf16[768,768]{1,0:T(8,128)(2,1)S(1)}, bf16[768,768]{1,0:T(8,128)(2,1)}, u32[]{:S(2)}) copy-start(bf16[768,768]{1,0:T(8,128)(2,1)} %param.8) | copy-start | bytes 3538948
  147.8 522.6 %reduce-scatter.2.cloned.1.call-start = ((), (), s32[]{:S(2)}) async-start(), calls=%async_computation.3 | async-start | bytes 2027520 | tf_op jit(solution)/shard_map/reduce_scatter | solution.py:16
  349.6 0.7 copy-start.2
Sparse Core Ops, SparseCore 0:
  11.7 131.5 all-gather.1
  147.9 196.0 all-reduce.1
  351.4 318.9 reduce-scatter.1
where the time goes:
time: 679 us; the launch traced here: 678 us
  waiting for transfers between devices  652 us (96%)
  between operations  13.1 us (2%)
  matrix products  10 us (1%)
    reduce_scatter x1, waiting for transfers between devices, shards(): lax.psum_scatter(jnp.dot(hidden, outer_weight, preferred_element_type=jnp...  320 us
    psum x1, waiting for transfers between devices, shards(): lax.psum(partial_value.astype(jnp.bfloat16), 'row').astype(jnp.float32)  196 us
    all_gather x1, waiting for transfers between devices, shards(): lax.all_gather(tokens, 'col', axis=0, tiled=True)  136 us
  transfers between devices with their start and end apart: 3, of which 3 were waited for; matrix products, arithmetic and copies ran while one was open for 0% of the time, Pallas kernels for 0%

commit v1 on v0

v1 whole, which is shorter than its diff:
```python
import jax
import jax.numpy as jnp
from jax import lax
from jax.sharding import Mesh
from jax.sharding import PartitionSpec as P

ROW = ("zq", "zb", "c")
COL = ("y", "x", "zh")
SIZES = (4, 2, 2, 4, 4, 2)

F32 = jnp.float32
BF16 = jnp.bfloat16


def gather_by_exchange(block, axes, n):
    return lax.all_to_all(jnp.broadcast_to(block[None], (n, *block.shape)), axes, 0, 0, tiled=True)


def scatter_by_exchange(parts, axes):
    return lax.all_to_all(parts, axes, 0, 0, tiled=True).astype(F32).sum(axis=0)


def shards(tokens, w1, b1, w2, b2):
    zb, zh = lax.axis_index("zb"), lax.axis_index("zh")
    pairs = [(a, b) for a in range(2) for b in range(2)]
    straight = [(a * 2 + b, b * 2 + a) for a, b in pairs]
    crossed = [(a * 2 + b, b * 2 + 1 - a) for a, b in pairs]
    swap = [(0, 1), (1, 0)]

    got_zh = lax.ppermute(tokens, ("zb", "zh"), straight)
    got_other = lax.ppermute(tokens, ("zb", "zh"), crossed)
    mine = jnp.where(zb == zh, got_zh, got_other)
    other = jnp.where(zb == zh, got_other, got_zh)
    tok = jnp.concatenate([mine, other], axis=1)

    w1_in, tok = lax.optimization_barrier((w1, tok))
    w1_other = lax.ppermute(w1_in, "zb", swap)
    all_tok = gather_by_exchange(tok, ("y", "x"), 16).reshape(640, 1536)
    w2_in, w1_other, all_tok = lax.optimization_barrier((w2, w1_other, all_tok))
    w2_other = lax.ppermute(w2_in, "zb", swap)

    w1_pair = jnp.concatenate([w1, w1_other], axis=0)
    part = jnp.dot(all_tok, w1_pair, preferred_element_type=F32).astype(BF16)
    half = scatter_by_exchange(part.reshape(2, 320, 768), "c").astype(BF16)
    preact = scatter_by_exchange(half.reshape(4, 80, 768), "zq") + b1.astype(F32)
    hidden = jax.nn.gelu(preact, approximate=True).astype(BF16)

    hidden = gather_by_exchange(hidden, "zq", 4).reshape(320, 768)
    hidden = gather_by_exchange(hidden, "c", 2).reshape(640, 768)
    w2_pair = jnp.concatenate([w2, w2_other], axis=1)
    out = jnp.dot(hidden, w2_pair, preferred_element_type=F32).astype(BF16)
    out = scatter_by_exchange(out.reshape(16, 40, 1536), ("y", "x")).astype(BF16)

    mine, other = out[:, :768], out[:, 768:]
    back = [(b * 2 + a, (1 - a) * 2 + b) for a, b in pairs]
    to_zh = lax.ppermute(jnp.where(zb == zh, mine, other), ("zb", "zh"), straight)
    to_other = lax.ppermute(jnp.where(zb == zh, other, mine), ("zb", "zh"), back)
    return (to_zh.astype(F32) + to_other.astype(F32) + b2.astype(F32)).astype(BF16)


def solution(mesh):
    fine = Mesh(mesh.devices.reshape(SIZES), ROW + COL)
    in_specs = (P(COL, ROW), P(ROW, COL), P(COL), P(COL, ROW), P(ROW))
    return jax.shard_map(shards, mesh=fine, in_specs=in_specs, out_specs=P(COL, ROW), check_vma=False)
```

time: 679 us -> 210 us (0.31)
  the two profiles are of different devices: /device:TPU:1 before, /device:TPU:64 now
where the time goes in v1:
time: 210 us; the launch traced here: 209 us
  waiting for transfers between devices  87.8 us (42%)
  starting transfers between devices  73.3 us (35%)
  blocking collectives  37.4 us (18%)
  matrix products  4.65 us (2%)
  local copies, waits for them, and re-layouts  3.27 us (2%)
  other arithmetic  2.24 us (1%)
    all_to_all x2, blocking collectives, scatter_by_exchange(): return lax.all_to_all(parts, axes, 0, 0, tiled=True).astype(F32).sum(axis=0)  37.4 us
    ppermute x1, waiting for transfers between devices, shards(): w1_other = lax.ppermute(w1_in, 'zb', swap)  22.2 us
    all_to_all x1, waiting for transfers between devices, scatter_by_exchange(): return lax.all_to_all(parts, axes, 0, 0, tiled=True).astype(F32).sum(axis=0)  22 us
    ppermute x1, waiting for transfers between devices, shards(): w2_other = lax.ppermute(w2_in, 'zb', swap)  20.2 us
    all_to_all x3, starting transfers between devices, gather_by_exchange(): lax.all_to_all(jnp.broadcast_to(block[None], (n, *block.shape)), axes, 0,...  19.8 us
    all_to_all x3, waiting for transfers between devices, gather_by_exchange(): lax.all_to_all(jnp.broadcast_to(block[None], (n, *block.shape)), axes, 0,...  17.5 us
    ppermute x1, starting transfers between devices, shards(): w1_other = lax.ppermute(w1_in, 'zb', swap)  14.6 us
    ppermute x1, starting transfers between devices, shards(): got_other = lax.ppermute(tokens, ('zb', 'zh'), crossed)  14.4 us
  transfers between devices with their start and end apart: 10, of which 6 were waited for; matrix products, arithmetic and copies ran while one was open for 0% of the time, Pallas kernels for 0%

profile of v1, /device:TPU:64, one launch (start us, length us, event | category | flops | bytes accessed | tf_op | source)
XLA Modules:
  0.0 208.9 jit_solution(13707987164681082301)
XLA Ops:
  0.0 1.5 collective-permute-start
  1.5 14.4 %collective-permute-start.1 = (bf16[40,768]{1,0:T(8,128)(2,1)}, bf16[40,768]{1,0:T(8,128)(2,1)S(1)}, u32[]{:S(2)}, u32[]{:S(2)}) collective-permute-start(bf16[40,768]{1,0:T(8,128)(2,1)} %param.5), channel_id=1, source_target_pairs={{0,1},{1,65},{64,0},{65,64},{2,3},{3,67},{66,2},{67,66},{4,5},{5,6... | collective-permute-start | bytes 184328 | tf_op jit(solution)/shard_map/ppermute | solution.py:31
  15.9 3.1 %collective-permute-done.1 = bf16[40,768]{1,0:T(8,128)(2,1)S(1)} collective-permute-done((bf16[40,768]{1,0:T(8,128)(2,1)}, bf16[40,768]{1,0:T(8,128)(2,1)S(1)}, u32[]{:S(2)}, u32[]{:S(2)}) %collective-permute-start.1) | collective-permute-done | bytes 61472 | tf_op jit(solution)/shard_map/ppermute | solution.py:31
  19.0 1.4 broadcast_in_dim.8
  20.4 7.2 %all-to-all-start = ((bf16[16,40,1536]{2,1,0:T(8,128)(2,1)}), bf16[16,40,1536]{2,1,0:T(8,128)(2,1)S(1)}, u32[]{:S(2)}, u32[]{:S(2)}) async-start(bf16[16,40,1536]{2,1,0:T(8,128)(2,1)} %broadcast_in_dim.8), calls=%async_computation | async-start | bytes 3932160 | tf_op jit(solution)/shard_map/all_to_all | solution.py:16
  27.6 14.6 %collective-permute-start.2 = (bf16[768,768]{1,0:T(8,128)(2,1)S(1)}, bf16[768,768]{1,0:T(8,128)(2,1)}, u32[]{:S(2)}, u32[]{:S(2)}) collective-permute-start(bf16[768,768]{1,0:T(8,128)(2,1)S(1)} %copy-done.2), channel_id=1, source_target_pairs={{0,64},{64,0},{1,65},{65,1},{2,66},{66,2},{3,67},{67,3},{4,68},{68... | collective-permute-start | bytes 3538952 | tf_op jit(solution)/shard_map/ppermute | solution.py:37
  42.2 22.2 %collective-permute-done.2 = bf16[768,768]{1,0:T(8,128)(2,1)} collective-permute-done((bf16[768,768]{1,0:T(8,128)(2,1)S(1)}, bf16[768,768]{1,0:T(8,128)(2,1)}, u32[]{:S(2)}, u32[]{:S(2)}) %collective-permute-start.2) | collective-permute-done | bytes 1179680 | tf_op jit(solution)/shard_map/ppermute | solution.py:37
  64.4 3.0 %fusion.7 = bf16[640,768]{1,0:T(8,128)(2,1)S(1)} fusion(bf16[640,1536]{1,0:T(8,128)(2,1)S(1)} %bitcast.8, bf16[768,768]{1,0:T(8,128)(2,1)} %collective-permute-done.2, bf16[768,768]{1,0:T(8,128)(2,1)S(1)} %copy-done.2), kind=kOutput, calls=%fused_computation.8 | convolution fusion | flops 1515159552 | bytes 5308416 | tf_op jit(solution)/shard_map/dot_general | solution.py:43
  67.4 4.5 %all_to_all.30 = bf16[2,320,768]{2,1,0:T(8,128)(2,1)S(1)} all-to-all(bf16[2,320,768]{2,1,0:T(8,128)(2,1)S(1)} %bitcast.12), channel_id=1, replica_groups=mesh['zq'=4,'zb'=2,'c'=2,'y'=4,'x'=4,'zh'=2] {'c'}, dimensions={0} | all-to-all | bytes 1966080 | tf_op jit(solution)/shard_map/all_to_all | solution.py:20
  71.9 1.1 reduce_sum.33
  73.0 6.1 %all-to-all-start.2 = ((bf16[4,80,768]{2,1,0:T(8,128)(2,1)}), bf16[4,80,768]{2,1,0:T(8,128)(2,1)S(1)}, u32[]{:S(2)}, u32[]{:S(2)}) async-start(bf16[4,80,768]{2,1,0:T(8,128)(2,1)} %bitcast.2), calls=%async_computation.2 | async-start | bytes 983040 | tf_op jit(solution)/shard_map/all_to_all | solution.py:20
  79.2 22.0 %all-to-all-done.2 = bf16[4,80,768]{2,1,0:T(8,128)(2,1)S(1)} async-done(((bf16[4,80,768]{2,1,0:T(8,128)(2,1)}), bf16[4,80,768]{2,1,0:T(8,128)(2,1)S(1)}, u32[]{:S(2)}, u32[]{:S(2)}) %all-to-all-start.2) | async-done | bytes 491552 | tf_op jit(solution)/shard_map/all_to_all | solution.py:20
  101.3 0.8 broadcast_in_dim.9
  102.2 9.1 %all-to-all-start.3 = ((bf16[4,80,768]{2,1,0:T(8,128)(2,1)}), bf16[4,80,768]{2,1,0:T(8,128)(2,1)S(1)}, u32[]{:S(2)}, u32[]{:S(2)}) async-start(bf16[4,80,768]{2,1,0:T(8,128)(2,1)} %broadcast_in_dim.9), calls=%async_computation.3 | async-start | bytes 983040 | tf_op jit(solution)/shard_map/all_to_all | solution.py:16
  111.2 3.6 %collective-permute-start.3 = (bf16[768,768]{1,0:T(8,128)(2,1)S(1)}, bf16[768,768]{1,0:T(8,128)(2,1)S(1)}, u32[]{:S(2)}, u32[]{:S(2)}) collective-permute-start(bf16[768,768]{1,0:T(8,128)(2,1)S(1)} %copy-done.3), channel_id=1, source_target_pairs={{0,64},{64,0},{1,65},{65,1},{2,66},{66,2},{3,67},{67,3},{4,68},{68... | collective-permute-start | bytes 3538952 | tf_op jit(solution)/shard_map/ppermute | solution.py:40
  114.8 17.5 %all-to-all-done.3 = bf16[4,80,768]{2,1,0:T(8,128)(2,1)S(1)} async-done(((bf16[4,80,768]{2,1,0:T(8,128)(2,1)}), bf16[4,80,768]{2,1,0:T(8,128)(2,1)S(1)}, u32[]{:S(2)}, u32[]{:S(2)}) %all-to-all-start.3) | async-done | bytes 491552 | tf_op jit(solution)/shard_map/all_to_all | solution.py:16
  132.3 1.0 broadcast_in_dim.11
  133.3 3.6 %all-to-all-start.4 = ((bf16[2,320,768]{2,1,0:T(8,128)(2,1)}), bf16[2,320,768]{2,1,0:T(8,128)(2,1)S(1)}, u32[]{:S(2)}, u32[]{:S(2)}) async-start(bf16[2,320,768]{2,1,0:T(8,128)(2,1)} %broadcast_in_dim.11), calls=%async_computation.4 | async-start | bytes 1966080 | tf_op jit(solution)/shard_map/all_to_all | solution.py:16
  136.9 20.2 %collective-permute-done.3 = bf16[768,768]{1,0:T(8,128)(2,1)S(1)} collective-permute-done((bf16[768,768]{1,0:T(8,128)(2,1)S(1)}, bf16[768,768]{1,0:T(8,128)(2,1)S(1)}, u32[]{:S(2)}, u32[]{:S(2)}) %collective-permute-start.3) | collective-permute-done | bytes 1179680 | tf_op jit(solution)/shard_map/ppermute | solution.py:40
  157.1 1.7 convolution_convert_fusion
  158.8 32.9 %all_to_all.31 = bf16[16,40,1536]{2,1,0:T(8,128)(2,1)S(1)} all-to-all(bf16[16,40,1536]{2,1,0:T(8,128)(2,1)S(1)} %bitcast.9), channel_id=1, replica_groups=mesh['zq'=4,'zb'=2,'c'=2,'y'=4,'x'=4,'zh'=2] {'y','x'}, dimensions={0} | all-to-all | bytes 3932160 | tf_op jit(solution)/shard_map/all_to_all | solution.py:20
  192.1 0.7 collective-permute-start.4
  192.8 12.7 %collective-permute-start.5 = (bf16[40,768]{1,0:T(8,128)(2,1)S(1)}, bf16[40,768]{1,0:T(8,128)(2,1)S(1)}, u32[]{:S(2)}, u32[]{:S(2)}) collective-permute-start(bf16[40,768]{1,0:T(8,128)(2,1)S(1)} %get-tuple-element.16), channel_id=1, source_target_pairs={{0,64},{64,65},{1,0},{65,1},{2,66},{66,67},{3,2},{67,3},{4,68},{68... | collective-permute-start | bytes 184328 | tf_op jit(solution)/shard_map/ppermute | solution.py:57
  205.5 2.7 %collective-permute-done.5 = bf16[40,768]{1,0:T(8,128)(2,1)S(1)} collective-permute-done((bf16[40,768]{1,0:T(8,128)(2,1)S(1)}, bf16[40,768]{1,0:T(8,128)(2,1)S(1)}, u32[]{:S(2)}, u32[]{:S(2)}) %collective-permute-start.5) | collective-permute-done | bytes 61472 | tf_op jit(solution)/shard_map/ppermute | solution.py:57
  (21 shorter events, 1.2 us)
Async XLA Ops:
  0.0 15.9 %collective-permute-start = (bf16[40,768]{1,0:T(8,128)(2,1)}, bf16[40,768]{1,0:T(8,128)(2,1)S(1)}, u32[]{:S(2)}, u32[]{:S(2)}) collective-permute-start(bf16[40,768]{1,0:T(8,128)(2,1)} %param.5), channel_id=1, source_target_pairs={{0,0},{1,64},{64,1},{65,65},{2,2},{3,66},{66,3},{67,67},{4,4},{5,6... | collective-permute-start | bytes 184328 | tf_op jit(solution)/shard_map/ppermute | solution.py:30
  1.5 17.5 %collective-permute-start.1 = (bf16[40,768]{1,0:T(8,128)(2,1)}, bf16[40,768]{1,0:T(8,128)(2,1)S(1)}, u32[]{:S(2)}, u32[]{:S(2)}) collective-permute-start(bf16[40,768]{1,0:T(8,128)(2,1)} %param.5), channel_id=1, source_target_pairs={{0,1},{1,65},{64,0},{65,64},{2,3},{3,67},{66,2},{67,66},{4,5},{5,6... | collective-permute-start | bytes 184328 | tf_op jit(solution)/shard_map/ppermute | solution.py:31
  20.4 7.2 %copy-start.2 = (bf16[768,768]{1,0:T(8,128)(2,1)S(1)}, bf16[768,768]{1,0:T(8,128)(2,1)}, u32[]{:S(2)}) copy-start(bf16[768,768]{1,0:T(8,128)(2,1)} %param.6) | copy-start | bytes 3538948
  20.4 44.0 %all-to-all-start = ((bf16[16,40,1536]{2,1,0:T(8,128)(2,1)}), bf16[16,40,1536]{2,1,0:T(8,128)(2,1)S(1)}, u32[]{:S(2)}, u32[]{:S(2)}) async-start(bf16[16,40,1536]{2,1,0:T(8,128)(2,1)} %broadcast_in_dim.8), calls=%async_computation | async-start | bytes 3932160 | tf_op jit(solution)/shard_map/all_to_all | solution.py:16
  27.6 36.8 %collective-permute-start.2 = (bf16[768,768]{1,0:T(8,128)(2,1)S(1)}, bf16[768,768]{1,0:T(8,128)(2,1)}, u32[]{:S(2)}, u32[]{:S(2)}) collective-permute-start(bf16[768,768]{1,0:T(8,128)(2,1)S(1)} %copy-done.2), channel_id=1, source_target_pairs={{0,64},{64,0},{1,65},{65,1},{2,66},{66,2},{3,67},{67,3},{4,68},{68... | collective-permute-start | bytes 3538952 | tf_op jit(solution)/shard_map/ppermute | solution.py:37
  67.4 11.8 %copy-start = (bf16[768]{0:T(1024)(128)(2,1)S(1)}, bf16[768]{0:T(1024)(128)(2,1)}, u32[]{:S(2)}) copy-start(bf16[768]{0:T(1024)(128)(2,1)} %param.7) | copy-start | bytes 4612
  73.0 38.2 %copy-start.3 = (bf16[768,768]{1,0:T(8,128)(2,1)S(1)}, bf16[768,768]{1,0:T(8,128)(2,1)}, u32[]{:S(2)}) copy-start(bf16[768,768]{1,0:T(8,128)(2,1)} %param.8) | copy-start | bytes 3538948
  73.0 28.1 %all-to-all-start.2 = ((bf16[4,80,768]{2,1,0:T(8,128)(2,1)}), bf16[4,80,768]{2,1,0:T(8,128)(2,1)S(1)}, u32[]{:S(2)}, u32[]{:S(2)}) async-start(bf16[4,80,768]{2,1,0:T(8,128)(2,1)} %bitcast.2), calls=%async_computation.2 | async-start | bytes 983040 | tf_op jit(solution)/shard_map/all_to_all | solution.py:20
  102.2 30.2 %all-to-all-start.3 = ((bf16[4,80,768]{2,1,0:T(8,128)(2,1)}), bf16[4,80,768]{2,1,0:T(8,128)(2,1)S(1)}, u32[]{:S(2)}, u32[]{:S(2)}) async-start(bf16[4,80,768]{2,1,0:T(8,128)(2,1)} %broadcast_in_dim.9), calls=%async_computation.3 | async-start | bytes 983040 | tf_op jit(solution)/shard_map/all_to_all | solution.py:16
  111.2 45.9 %collective-permute-start.3 = (bf16[768,768]{1,0:T(8,128)(2,1)S(1)}, bf16[768,768]{1,0:T(8,128)(2,1)S(1)}, u32[]{:S(2)}, u32[]{:S(2)}) collective-permute-start(bf16[768,768]{1,0:T(8,128)(2,1)S(1)} %copy-done.3), channel_id=1, source_target_pairs={{0,64},{64,0},{1,65},{65,1},{2,66},{66,2},{3,67},{67,3},{4,68},{68... | collective-permute-start | bytes 3538952 | tf_op jit(solution)/shard_map/ppermute | solution.py:40
  133.3 23.8 %all-to-all-start.4 = ((bf16[2,320,768]{2,1,0:T(8,128)(2,1)}), bf16[2,320,768]{2,1,0:T(8,128)(2,1)S(1)}, u32[]{:S(2)}, u32[]{:S(2)}) async-start(bf16[2,320,768]{2,1,0:T(8,128)(2,1)} %broadcast_in_dim.11), calls=%async_computation.4 | async-start | bytes 1966080 | tf_op jit(solution)/shard_map/all_to_all | solution.py:16
  191.8 13.7 %copy-start.1 = (bf16[768]{0:T(1024)(128)(2,1)S(1)}, bf16[768]{0:T(1024)(128)(2,1)}, u32[]{:S(2)}) copy-start(bf16[768]{0:T(1024)(128)(2,1)} %param.9) | copy-start | bytes 4612
  192.1 13.4 %collective-permute-start.4 = (bf16[40,768]{1,0:T(8,128)(2,1)S(1)}, bf16[40,768]{1,0:T(8,128)(2,1)S(1)}, u32[]{:S(2)}, u32[]{:S(2)}) collective-permute-start(bf16[40,768]{1,0:T(8,128)(2,1)S(1)} %get-tuple-element.15), channel_id=1, source_target_pairs={{0,0},{1,64},{64,1},{65,65},{2,2},{3,66},{66,3},{67,67},{4,4},{5,6... | collective-permute-start | bytes 184328 | tf_op jit(solution)/shard_map/ppermute | solution.py:56
  192.8 15.5 %collective-permute-start.5 = (bf16[40,768]{1,0:T(8,128)(2,1)S(1)}, bf16[40,768]{1,0:T(8,128)(2,1)S(1)}, u32[]{:S(2)}, u32[]{:S(2)}) collective-permute-start(bf16[40,768]{1,0:T(8,128)(2,1)S(1)} %get-tuple-element.16), channel_id=1, source_target_pairs={{0,64},{64,65},{1,0},{65,1},{2,66},{66,67},{3,2},{67,3},{4,68},{68... | collective-permute-start | bytes 184328 | tf_op jit(solution)/shard_map/ppermute | solution.py:57

commit v2 on v0

v2 whole, which is shorter than its diff:
```python
import jax
import jax.numpy as jnp
from jax import lax
from jax.experimental import pallas as pl
from jax.experimental.pallas import tpu as pltpu
from jax.sharding import Mesh
from jax.sharding import PartitionSpec as P

ROW = ("zq", "zb", "c")
COL = ("yp", "y0", "xp", "x0", "zh")
SIZES = (4, 2, 2, 2, 2, 2, 2, 2)
PLANE = ("yp", "y0", "xp", "x0")
CORNER = ("zb", "c", "y0", "x0", "zh")
SWAP = [(0, 1), (1, 0)]
VMEM = pl.BlockSpec(memory_space=pltpu.VMEM)

F32 = jnp.float32
BF16 = jnp.bfloat16
barrier = lax.optimization_barrier


def corner_pairs(other_zh):
    return [(i, ((i >> 1) & 3) << 3 | (i >> 3) << 1 | ((i & 1) ^ other_zh)) for i in range(32)]


def slot(block, dz, dc):
    y0 = jnp.bitwise_xor(lax.axis_index("zb"), dz)
    x0 = jnp.bitwise_xor(lax.axis_index("c"), dc)
    return (block & 2) * 4 + y0 * 4 + (block & 1) * 2 + x0


def cost(flops, nbytes):
    return pl.CostEstimate(flops=flops, bytes_accessed=nbytes, transcendentals=0)


def first_kernel(got, w00, w01, w10, w11, p0, p1, p2, p3, total):
    for k, w in enumerate((w00, w01, w10, w11)):
        left = jnp.concatenate([got[slot(b, k // 2, k % 2)] for b in range(4)], axis=0)
        part = jnp.dot(left, w[...], preferred_element_type=F32).reshape(4, 40, 768)
        total[...] = part if k == 0 else total[...] + part
    zq = lax.axis_index("zq")
    for k, p in enumerate((p0, p1, p2, p3)):
        p[...] = total[jnp.bitwise_xor(zq, k)].astype(BF16)


def first(got, ws):
    return pl.pallas_call(
        first_kernel,
        out_shape=[jax.ShapeDtypeStruct((40, 768), BF16)] * 4,
        in_specs=[VMEM] * 5,
        out_specs=[VMEM] * 4,
        scratch_shapes=[pltpu.VMEM((4, 40, 768), F32)],
        compiler_params=pltpu.CompilerParams(vmem_limit_bytes=8 << 20),
        cost_estimate=cost(2 * 160 * 3072 * 768, 6 << 20),
        name="first_product",
    )(got, *ws)


def second_kernel(h0, h1, h2, h3, w00, w01, w10, w11, out):
    zq = lax.axis_index("zq")
    left = jnp.concatenate([h[...] for h in (h0, h1, h2, h3)], axis=0)
    for k, w in enumerate((w00, w01, w10, w11)):
        part = jnp.dot(left, w[...], preferred_element_type=F32)
        for j in range(4):
            at = slot(jnp.bitwise_xor(zq, j), k // 2, k % 2)
            out[at] = part[j * 40 : (j + 1) * 40].astype(BF16)


def second(hs, ws):
    return pl.pallas_call(
        second_kernel,
        out_shape=jax.ShapeDtypeStruct((16, 40, 768), BF16),
        in_specs=[VMEM] * 8,
        out_specs=VMEM,
        compiler_params=pltpu.CompilerParams(vmem_limit_bytes=8 << 20),
        cost_estimate=cost(2 * 160 * 3072 * 768, 6 << 20),
        name="second_product",
    )(*hs, *ws)


def across(block, k):
    return lax.ppermute(block, "zq", [(i, i ^ k) for i in range(4)])


def middle_kernel(p0, p1, p2, p3, bias, h):
    preact = bias[...].astype(F32)
    for p in (p0, p1, p2, p3):
        preact = preact + p[...].astype(F32)
    h[...] = jax.nn.gelu(preact, approximate=True).astype(BF16)


def middle(ps, bias):
    return pl.pallas_call(
        middle_kernel,
        out_shape=jax.ShapeDtypeStruct((40, 768), BF16),
        in_specs=[VMEM] * 5,
        out_specs=VMEM,
        compiler_params=pltpu.CompilerParams(vmem_limit_bytes=4 << 20),
        cost_estimate=cost(20 * 40 * 768, 5 * 40 * 768 * 2),
        name="sum_gelu",
    )(*ps, bias)


def across(block, k):
    return lax.ppermute(block, "zq", [(i, i ^ k) for i in range(4)])


def shards(tokens, w1, b1, w2, b2):
    tok = [lax.ppermute(tokens, CORNER, corner_pairs(1 - k)) for k in range(2)]

    got = []
    for k in range(2):
        if k:
            tok[k], got[0] = barrier((tok[k], got[0]))
        spread = jnp.broadcast_to(tok[k][None], (16, 40, 768))
        got.append(lax.all_to_all(spread, PLANE, 0, 0, tiled=True))

    w1_z, got[0] = barrier((lax.ppermute(w1, "zb", SWAP), got[0]))
    w1_all = [w1, lax.ppermute(w1, "c", SWAP), w1_z, lax.ppermute(w1_z, "c", SWAP)]
    w2_own, w1_z = barrier((w2, w1_z))
    w2_z = lax.ppermute(w2_own, "zb", SWAP)

    bias = b1.reshape(1, 768)
    parts = [first(g, w1_all) for g in got]
    sums = [[p[0]] + [across(p[i], i) for i in range(1, 4)] for p in parts]
    sums[0], parts[1] = barrier((sums[0], parts[1]))
    sums[1], w2_z = barrier((sums[1], w2_z))
    w2_all = [w2, lax.ppermute(w2, "c", SWAP), w2_z, lax.ppermute(w2_z, "c", SWAP)]
    hidden = [middle(s, bias) for s in sums]
    rows = [[h] + [across(h, i) for i in range(1, 4)] for h in hidden]
    rows[0], hidden[1] = barrier((rows[0], hidden[1]))
    outs = [second(r, w2_all) for r in rows]
    back = []
    for k in range(2):
        if k:
            outs[k], out = barrier((outs[k], out))
        out = lax.all_to_all(outs[k], PLANE, 0, 0, tiled=True)
        total = out.astype(F32).sum(axis=0).astype(BF16)
        back.append(lax.ppermute(total, CORNER, corner_pairs(1 - k)))
    return (back[0].astype(F32) + back[1].astype(F32) + b2.astype(F32)).astype(BF16)


def solution(mesh):
    fine = Mesh(mesh.devices.reshape(SIZES), ROW + COL)
    in_specs = (P(COL, ROW), P(ROW, COL), P(COL), P(COL, ROW), P(ROW))
    return jax.shard_map(shards, mesh=fine, in_specs=in_specs, out_specs=P(COL, ROW), check_vma=False)
```

time: 679 us -> 241 us (0.35)
  the two profiles are of different devices: /device:TPU:1 before, /device:TPU:38 now
where the time goes in v2:
time: 241 us; the launch traced here: 240 us
  starting transfers between devices  153 us (63%)
  waiting for transfers between devices  66.6 us (28%)
  Pallas kernels  10.3 us (4%)
  local copies, waits for them, and re-layouts  8.44 us (4%)
    ppermute x12, starting transfers between devices, across(): return lax.ppermute(block, 'zq', [(i, i ^ k) for i in range(4)])  56.1 us
    all_to_all x2, starting transfers between devices, shards(): got.append(lax.all_to_all(spread, PLANE, 0, 0, tiled=True))  38.3 us
    ppermute x12, waiting for transfers between devices, across(): return lax.ppermute(block, 'zq', [(i, i ^ k) for i in range(4)])  22.9 us
    ppermute x2, starting transfers between devices, shards(): tok = [lax.ppermute(tokens, CORNER, corner_pairs(1 - k)) for k in range(2)]  22.6 us
    all_to_all x2, waiting for transfers between devices, shards(): got.append(lax.all_to_all(spread, PLANE, 0, 0, tiled=True))  19.4 us
    all_to_all x2, starting transfers between devices, shards(): out = lax.all_to_all(outs[k], PLANE, 0, 0, tiled=True)  15.2 us
    ppermute x2, waiting for transfers between devices, shards(): back.append(lax.ppermute(total, CORNER, corner_pairs(1 - k)))  10.1 us
    all_to_all x2, waiting for transfers between devices, shards(): out = lax.all_to_all(outs[k], PLANE, 0, 0, tiled=True)  8.55 us
  transfers between devices with their start and end apart: 26, of which 11 were waited for; matrix products, arithmetic and copies ran while one was open for 1% of the time, Pallas kernels for 4%

profile of v2, /device:TPU:38, one launch (start us, length us, event | category | flops | bytes accessed | tf_op | source)
XLA Modules:
  0.0 239.6 jit_solution(15277826978888985143)
XLA Ops:
  2.0 15.7 %collective-permute-start.2 = (bf16[40,768]{1,0:T(8,128)(2,1)}, bf16[40,768]{1,0:T(8,128)(2,1)S(1)}, u32[]{:S(2)}, u32[]{:S(2)}) collective-permute-start(bf16[40,768]{1,0:T(8,128)(2,1)} %param.5), channel_id=1, source_target_pairs={{0,1},{1,0},{2,33},{3,32},{8,65},{9,64},{10,97},{11,96},{32,3},{33... | collective-permute-start | bytes 184328 | tf_op jit(solution)/shard_map/ppermute | solution.py:109
  17.7 4.9 %collective-permute-done.2 = bf16[40,768]{1,0:T(8,128)(2,1)S(1)} collective-permute-done((bf16[40,768]{1,0:T(8,128)(2,1)}, bf16[40,768]{1,0:T(8,128)(2,1)S(1)}, u32[]{:S(2)}, u32[]{:S(2)}) %collective-permute-start.2) | collective-permute-done | bytes 61472 | tf_op jit(solution)/shard_map/ppermute | solution.py:109
  23.7 31.9 %all-to-all-start = ((bf16[16,40,768]{2,1,0:T(8,128)(2,1)}), bf16[16,40,768]{2,1,0:T(8,128)(2,1)S(1)}, u32[]{:S(2)}, u32[]{:S(2)}) async-start(bf16[16,40,768]{2,1,0:T(8,128)(2,1)} %broadcast_in_dim.4), calls=%async_computation | async-start | bytes 1966080 | tf_op jit(solution)/shard_map/all_to_all | solution.py:116
  55.6 6.9 %collective-permute-start.1 = (bf16[40,768]{1,0:T(8,128)(2,1)S(1)}, bf16[40,768]{1,0:T(8,128)(2,1)S(1)}, u32[]{:S(2)}, u32[]{:S(2)}) collective-permute-start(bf16[40,768]{1,0:T(8,128)(2,1)S(1)} %copy-done.11), channel_id=1, source_target_pairs={{0,0},{1,1},{2,32},{3,33},{8,64},{9,65},{10,96},{11,97},{32,2},{33... | collective-permute-start | bytes 184328 | tf_op jit(solution)/shard_map/ppermute | solution.py:109
  65.2 5.3 %all-to-all-done.got = bf16[16,40,768]{2,1,0:T(8,128)(2,1)S(1)} async-done(((bf16[16,40,768]{2,1,0:T(8,128)(2,1)}), bf16[16,40,768]{2,1,0:T(8,128)(2,1)S(1)}, u32[]{:S(2)}, u32[]{:S(2)}) %all-to-all-start) | async-done | bytes 983072 | tf_op jit(solution)/shard_map/all_to_all | solution.py:116
  73.3 7.1 %collective-permute-start.14 = (bf16[768,768]{1,0:T(8,128)(2,1)S(1)}, bf16[768,768]{1,0:T(8,128)(2,1)S(1)}, u32[]{:S(2)}, u32[]{:S(2)}) collective-permute-start(bf16[768,768]{1,0:T(8,128)(2,1)S(1)} %copy-done.1), channel_id=1, source_target_pairs={{0,64},{64,0},{1,65},{65,1},{2,66},{66,2},{3,67},{67,3},{4,68},{68... | collective-permute-start | bytes 3538952 | tf_op jit(solution)/shard_map/ppermute | solution.py:121
  82.3 6.4 %all-to-all-start.1 = ((bf16[16,40,768]{2,1,0:T(8,128)(2,1)}), bf16[16,40,768]{2,1,0:T(8,128)(2,1)}, u32[]{:S(2)}, u32[]{:S(2)}) async-start(bf16[16,40,768]{2,1,0:T(8,128)(2,1)} %broadcast_in_dim.5), calls=%async_computation.1 | async-start | bytes 1966080 | tf_op jit(solution)/shard_map/all_to_all | solution.py:116
  88.7 14.1 %all-to-all-done.1.got = bf16[16,40,768]{2,1,0:T(8,128)(2,1)} async-done(((bf16[16,40,768]{2,1,0:T(8,128)(2,1)}), bf16[16,40,768]{2,1,0:T(8,128)(2,1)}, u32[]{:S(2)}, u32[]{:S(2)}) %all-to-all-start.1) | async-done | bytes 983072 | tf_op jit(solution)/shard_map/all_to_all | solution.py:116
  108.6 6.7 %collective-permute-start.12 = (bf16[40,768]{1,0:T(8,128)(2,1)S(1)}, bf16[40,768]{1,0:T(8,128)(2,1)S(1)}, u32[]{:S(2)}, u32[]{:S(2)}) collective-permute-start(bf16[40,768]{1,0:T(8,128)(2,1)S(1)} %get-tuple-element.42), channel_id=1, source_target_pairs={{0,256},{128,384},{256,0},{384,128},{1,257},{129,385},{257,1},{385... | collective-permute-start | bytes 184328 | tf_op jit(solution)/shard_map/ppermute | solution.py:105
  115.3 4.9 %collective-permute-start.13 = (bf16[40,768]{1,0:T(8,128)(2,1)S(1)}, bf16[40,768]{1,0:T(8,128)(2,1)S(1)}, u32[]{:S(2)}, u32[]{:S(2)}) collective-permute-start(bf16[40,768]{1,0:T(8,128)(2,1)S(1)} %get-tuple-element.43), channel_id=1, source_target_pairs={{0,384},{128,256},{256,128},{384,0},{1,385},{129,257},{257,129},{3... | collective-permute-start | bytes 184328 | tf_op jit(solution)/shard_map/ppermute | solution.py:105
  122.2 5.0 %collective-permute-done.13.p3 = bf16[40,768]{1,0:T(8,128)(2,1)S(1)} collective-permute-done((bf16[40,768]{1,0:T(8,128)(2,1)S(1)}, bf16[40,768]{1,0:T(8,128)(2,1)S(1)}, u32[]{:S(2)}, u32[]{:S(2)}) %collective-permute-start.13) | collective-permute-done | bytes 61472 | tf_op jit(solution)/shard_map/ppermute | solution.py:105
  134.1 6.4 %collective-permute-start.6 = (bf16[40,768]{1,0:T(8,128)(2,1)S(1)}, bf16[40,768]{1,0:T(8,128)(2,1)S(1)}, u32[]{:S(2)}, u32[]{:S(2)}) collective-permute-start(bf16[40,768]{1,0:T(8,128)(2,1)S(1)} %get-tuple-element.37), channel_id=1, source_target_pairs={{0,256},{128,384},{256,0},{384,128},{1,257},{129,385},{257,1},{385... | collective-permute-start | bytes 184328 | tf_op jit(solution)/shard_map/ppermute | solution.py:105
  140.5 5.7 %collective-permute-start.7 = (bf16[40,768]{1,0:T(8,128)(2,1)S(1)}, bf16[40,768]{1,0:T(8,128)(2,1)S(1)}, u32[]{:S(2)}, u32[]{:S(2)}) collective-permute-start(bf16[40,768]{1,0:T(8,128)(2,1)S(1)} %get-tuple-element.38), channel_id=1, source_target_pairs={{0,384},{128,256},{256,128},{384,0},{1,385},{129,257},{257,129},{3... | collective-permute-start | bytes 184328 | tf_op jit(solution)/shard_map/ppermute | solution.py:105
  146.3 6.1 %collective-permute-done.7.p3 = bf16[40,768]{1,0:T(8,128)(2,1)S(1)} collective-permute-done((bf16[40,768]{1,0:T(8,128)(2,1)S(1)}, bf16[40,768]{1,0:T(8,128)(2,1)S(1)}, u32[]{:S(2)}, u32[]{:S(2)}) %collective-permute-start.7) | collective-permute-done | bytes 61472 | tf_op jit(solution)/shard_map/ppermute | solution.py:105
  152.4 6.4 %collective-permute-start.10 = (bf16[40,768]{1,0:T(8,128)(2,1)S(1)}, bf16[40,768]{1,0:T(8,128)(2,1)S(1)}, u32[]{:S(2)}, u32[]{:S(2)}) collective-permute-start(bf16[40,768]{1,0:T(8,128)(2,1)S(1)} %sum_gelu.2.h0), channel_id=1, source_target_pairs={{0,384},{128,256},{256,128},{384,0},{1,385},{129,257},{257,129},{3... | collective-permute-start | bytes 184328 | tf_op jit(solution)/shard_map/ppermute | solution.py:105
  160.7 5.7 %collective-permute-start.9 = (bf16[40,768]{1,0:T(8,128)(2,1)S(1)}, bf16[40,768]{1,0:T(8,128)(2,1)S(1)}, u32[]{:S(2)}, u32[]{:S(2)}) collective-permute-start(bf16[40,768]{1,0:T(8,128)(2,1)S(1)} %sum_gelu.2.h0), channel_id=1, source_target_pairs={{0,256},{128,384},{256,0},{384,128},{1,257},{129,385},{257,1},{385... | collective-permute-start | bytes 184328 | tf_op jit(solution)/shard_map/ppermute | solution.py:105
  166.6 4.6 %collective-permute-done.9.h2 = bf16[40,768]{1,0:T(8,128)(2,1)S(1)} collective-permute-done((bf16[40,768]{1,0:T(8,128)(2,1)S(1)}, bf16[40,768]{1,0:T(8,128)(2,1)S(1)}, u32[]{:S(2)}, u32[]{:S(2)}) %collective-permute-start.9) | collective-permute-done | bytes 61472 | tf_op jit(solution)/shard_map/ppermute | solution.py:105
  175.2 8.0 %all-to-all-start.2 = ((bf16[16,40,768]{2,1,0:T(8,128)(2,1)}), bf16[16,40,768]{2,1,0:T(8,128)(2,1)S(1)}, u32[]{:S(2)}, u32[]{:S(2)}) async-start(bf16[16,40,768]{2,1,0:T(8,128)(2,1)} %second_product.2), calls=%async_computation.2 | async-start | bytes 1966080 | tf_op jit(solution)/shard_map/all_to_all | solution.py:137
  187.4 5.1 %collective-permute-start.19 = (bf16[40,768]{1,0:T(8,128)(2,1)S(1)}, bf16[40,768]{1,0:T(8,128)(2,1)S(1)}, u32[]{:S(2)}, u32[]{:S(2)}) collective-permute-start(bf16[40,768]{1,0:T(8,128)(2,1)S(1)} %sum_gelu.3.h0), channel_id=1, source_target_pairs={{0,256},{128,384},{256,0},{384,128},{1,257},{129,385},{257,1},{385... | collective-permute-start | bytes 184328 | tf_op jit(solution)/shard_map/ppermute | solution.py:105
  192.6 4.6 %collective-permute-start.20 = (bf16[40,768]{1,0:T(8,128)(2,1)S(1)}, bf16[40,768]{1,0:T(8,128)(2,1)S(1)}, u32[]{:S(2)}, u32[]{:S(2)}) collective-permute-start(bf16[40,768]{1,0:T(8,128)(2,1)S(1)} %sum_gelu.3.h0), channel_id=1, source_target_pairs={{0,384},{128,256},{256,128},{384,0},{1,385},{129,257},{257,129},{3... | collective-permute-start | bytes 184328 | tf_op jit(solution)/shard_map/ppermute | solution.py:105
  199.6 4.8 %collective-permute-done.20.h3 = bf16[40,768]{1,0:T(8,128)(2,1)S(1)} collective-permute-done((bf16[40,768]{1,0:T(8,128)(2,1)S(1)}, bf16[40,768]{1,0:T(8,128)(2,1)S(1)}, u32[]{:S(2)}, u32[]{:S(2)}) %collective-permute-start.20) | collective-permute-done | bytes 61472 | tf_op jit(solution)/shard_map/ppermute | solution.py:105
  208.9 7.2 %all-to-all-start.3 = ((bf16[16,40,768]{2,1,0:T(8,128)(2,1)}), bf16[16,40,768]{2,1,0:T(8,128)(2,1)S(1)}, u32[]{:S(2)}, u32[]{:S(2)}) async-start(bf16[16,40,768]{2,1,0:T(8,128)(2,1)} %second_product.3), calls=%async_computation.3 | async-start | bytes 1966080 | tf_op jit(solution)/shard_map/all_to_all | solution.py:137
  218.2 8.6 %all-to-all-done.3 = bf16[16,40,768]{2,1,0:T(8,128)(2,1)S(1)} async-done(((bf16[16,40,768]{2,1,0:T(8,128)(2,1)}), bf16[16,40,768]{2,1,0:T(8,128)(2,1)S(1)}, u32[]{:S(2)}, u32[]{:S(2)}) %all-to-all-start.3) | async-done | bytes 983072 | tf_op jit(solution)/shard_map/all_to_all | solution.py:137
  228.8 10.1 %collective-permute-done.17 = bf16[40,768]{1,0:T(8,128)(2,1)S(1)} collective-permute-done((bf16[40,768]{1,0:T(8,128)(2,1)S(1)}, bf16[40,768]{1,0:T(8,128)(2,1)S(1)}, u32[]{:S(2)}, u32[]{:S(2)}) %collective-permute-start.17) | collective-permute-done | bytes 61472 | tf_op jit(solution)/shard_map/ppermute | solution.py:139
  (65 shorter events, 47.1 us)
Async XLA Ops:
  0.0 71.4 %collective-permute-start = (bf16[768,768]{1,0:T(8,128)(2,1)}, bf16[768,768]{1,0:T(8,128)(2,1)}, u32[]{:S(2)}, u32[]{:S(2)}) collective-permute-start(bf16[768,768]{1,0:T(8,128)(2,1)} %w00.5), channel_id=1, source_target_pairs={{0,64},{64,0},{1,65},{65,1},{2,66},{66,2},{3,67},{67,3},{4,68},{68... | collective-permute-start | bytes 3538952 | tf_op jit(solution)/shard_map/ppermute | solution.py:118
  2.0 20.6 %collective-permute-start.2 = (bf16[40,768]{1,0:T(8,128)(2,1)}, bf16[40,768]{1,0:T(8,128)(2,1)S(1)}, u32[]{:S(2)}, u32[]{:S(2)}) collective-permute-start(bf16[40,768]{1,0:T(8,128)(2,1)} %param.5), channel_id=1, source_target_pairs={{0,1},{1,0},{2,33},{3,32},{8,65},{9,64},{10,97},{11,96},{32,3},{33... | collective-permute-start | bytes 184328 | tf_op jit(solution)/shard_map/ppermute | solution.py:109
  23.7 46.8 %all-to-all-start = ((bf16[16,40,768]{2,1,0:T(8,128)(2,1)}), bf16[16,40,768]{2,1,0:T(8,128)(2,1)S(1)}, u32[]{:S(2)}, u32[]{:S(2)}) async-start(bf16[16,40,768]{2,1,0:T(8,128)(2,1)} %broadcast_in_dim.4), calls=%async_computation | async-start | bytes 1966080 | tf_op jit(solution)/shard_map/all_to_all | solution.py:116
  62.5 26.2 %collective-permute-start.3 = (bf16[768,768]{1,0:T(8,128)(2,1)S(1)}, bf16[768,768]{1,0:T(8,128)(2,1)}, u32[]{:S(2)}, u32[]{:S(2)}) collective-permute-start(bf16[768,768]{1,0:T(8,128)(2,1)S(1)} %copy-done), channel_id=1, source_target_pairs={{0,32},{32,0},{1,33},{33,1},{2,34},{34,2},{3,35},{35,3},{4,36},{36... | collective-permute-start | bytes 3538952 | tf_op jit(solution)/shard_map/ppermute | solution.py:119
  71.4 31.4 %collective-permute-start.4 = (bf16[768,768]{1,0:T(8,128)(2,1)}, bf16[768,768]{1,0:T(8,128)(2,1)}, u32[]{:S(2)}, u32[]{:S(2)}) collective-permute-start(bf16[768,768]{1,0:T(8,128)(2,1)} %collective-permute-done.w10), channel_id=1, source_target_pairs={{0,32},{32,0},{1,33},{33,1},{2,34},{34,2},{3,35},{35,3},{4,36},{36... | collective-permute-start | bytes 3538952 | tf_op jit(solution)/shard_map/ppermute | solution.py:119
  73.3 48.8 %collective-permute-start.14 = (bf16[768,768]{1,0:T(8,128)(2,1)S(1)}, bf16[768,768]{1,0:T(8,128)(2,1)S(1)}, u32[]{:S(2)}, u32[]{:S(2)}) collective-permute-start(bf16[768,768]{1,0:T(8,128)(2,1)S(1)} %copy-done.1), channel_id=1, source_target_pairs={{0,64},{64,0},{1,65},{65,1},{2,66},{66,2},{3,67},{67,3},{4,68},{68... | collective-permute-start | bytes 3538952 | tf_op jit(solution)/shard_map/ppermute | solution.py:121
  82.3 20.5 %all-to-all-start.1 = ((bf16[16,40,768]{2,1,0:T(8,128)(2,1)}), bf16[16,40,768]{2,1,0:T(8,128)(2,1)}, u32[]{:S(2)}, u32[]{:S(2)}) async-start(bf16[16,40,768]{2,1,0:T(8,128)(2,1)} %broadcast_in_dim.5), calls=%async_computation.1 | async-start | bytes 1966080 | tf_op jit(solution)/shard_map/all_to_all | solution.py:116
  106.2 16.0 %collective-permute-start.11 = (bf16[40,768]{1,0:T(8,128)(2,1)S(1)}, bf16[40,768]{1,0:T(8,128)(2,1)S(1)}, u32[]{:S(2)}, u32[]{:S(2)}) collective-permute-start(bf16[40,768]{1,0:T(8,128)(2,1)S(1)} %get-tuple-element.41), channel_id=1, source_target_pairs={{0,128},{128,0},{256,384},{384,256},{1,129},{129,1},{257,385},{385... | collective-permute-start | bytes 184328 | tf_op jit(solution)/shard_map/ppermute | solution.py:105
  108.6 13.6 %collective-permute-start.12 = (bf16[40,768]{1,0:T(8,128)(2,1)S(1)}, bf16[40,768]{1,0:T(8,128)(2,1)S(1)}, u32[]{:S(2)}, u32[]{:S(2)}) collective-permute-start(bf16[40,768]{1,0:T(8,128)(2,1)S(1)} %get-tuple-element.42), channel_id=1, source_target_pairs={{0,256},{128,384},{256,0},{384,128},{1,257},{129,385},{257,1},{385... | collective-permute-start | bytes 184328 | tf_op jit(solution)/shard_map/ppermute | solution.py:105
  115.3 11.9 %collective-permute-start.13 = (bf16[40,768]{1,0:T(8,128)(2,1)S(1)}, bf16[40,768]{1,0:T(8,128)(2,1)S(1)}, u32[]{:S(2)}, u32[]{:S(2)}) collective-permute-start(bf16[40,768]{1,0:T(8,128)(2,1)S(1)} %get-tuple-element.43), channel_id=1, source_target_pairs={{0,384},{128,256},{256,128},{384,0},{1,385},{129,257},{257,129},{3... | collective-permute-start | bytes 184328 | tf_op jit(solution)/shard_map/ppermute | solution.py:105
  120.2 51.0 %collective-permute-start.15 = (bf16[768,768]{1,0:T(8,128)(2,1)S(1)}, bf16[768,768]{1,0:T(8,128)(2,1)S(1)}, u32[]{:S(2)}, u32[]{:S(2)}) collective-permute-start(bf16[768,768]{1,0:T(8,128)(2,1)S(1)} %copy-done.1), channel_id=1, source_target_pairs={{0,32},{32,0},{1,33},{33,1},{2,34},{34,2},{3,35},{35,3},{4,36},{36... | collective-permute-start | bytes 3538952 | tf_op jit(solution)/shard_map/ppermute | solution.py:128
  127.2 44.0 %collective-permute-start.16 = (bf16[768,768]{1,0:T(8,128)(2,1)S(1)}, bf16[768,768]{1,0:T(8,128)(2,1)S(1)}, u32[]{:S(2)}, u32[]{:S(2)}) collective-permute-start(bf16[768,768]{1,0:T(8,128)(2,1)S(1)} %collective-permute-done.14.w10), channel_id=1, source_target_pairs={{0,32},{32,0},{1,33},{33,1},{2,34},{34,2},{3,35},{35,3},{4,36},{36... | collective-permute-start | bytes 3538952 | tf_op jit(solution)/shard_map/ppermute | solution.py:128
  132.2 14.1 %collective-permute-start.5 = (bf16[40,768]{1,0:T(8,128)(2,1)S(1)}, bf16[40,768]{1,0:T(8,128)(2,1)S(1)}, u32[]{:S(2)}, u32[]{:S(2)}) collective-permute-start(bf16[40,768]{1,0:T(8,128)(2,1)S(1)} %get-tuple-element.36), channel_id=1, source_target_pairs={{0,128},{128,0},{256,384},{384,256},{1,129},{129,1},{257,385},{385... | collective-permute-start | bytes 184328 | tf_op jit(solution)/shard_map/ppermute | solution.py:105
  134.1 12.2 %collective-permute-start.6 = (bf16[40,768]{1,0:T(8,128)(2,1)S(1)}, bf16[40,768]{1,0:T(8,128)(2,1)S(1)}, u32[]{:S(2)}, u32[]{:S(2)}) collective-permute-start(bf16[40,768]{1,0:T(8,128)(2,1)S(1)} %get-tuple-element.37), channel_id=1, source_target_pairs={{0,256},{128,384},{256,0},{384,128},{1,257},{129,385},{257,1},{385... | collective-permute-start | bytes 184328 | tf_op jit(solution)/shard_map/ppermute | solution.py:105
  140.5 11.8 %collective-permute-start.7 = (bf16[40,768]{1,0:T(8,128)(2,1)S(1)}, bf16[40,768]{1,0:T(8,128)(2,1)S(1)}, u32[]{:S(2)}, u32[]{:S(2)}) collective-permute-start(bf16[40,768]{1,0:T(8,128)(2,1)S(1)} %get-tuple-element.38), channel_id=1, source_target_pairs={{0,384},{128,256},{256,128},{384,0},{1,385},{129,257},{257,129},{3... | collective-permute-start | bytes 184328 | tf_op jit(solution)/shard_map/ppermute | solution.py:105
  152.4 14.1 %collective-permute-start.10 = (bf16[40,768]{1,0:T(8,128)(2,1)S(1)}, bf16[40,768]{1,0:T(8,128)(2,1)S(1)}, u32[]{:S(2)}, u32[]{:S(2)}) collective-permute-start(bf16[40,768]{1,0:T(8,128)(2,1)S(1)} %sum_gelu.2.h0), channel_id=1, source_target_pairs={{0,384},{128,256},{256,128},{384,0},{1,385},{129,257},{257,129},{3... | collective-permute-start | bytes 184328 | tf_op jit(solution)/shard_map/ppermute | solution.py:105
  160.7 10.4 %collective-permute-start.9 = (bf16[40,768]{1,0:T(8,128)(2,1)S(1)}, bf16[40,768]{1,0:T(8,128)(2,1)S(1)}, u32[]{:S(2)}, u32[]{:S(2)}) collective-permute-start(bf16[40,768]{1,0:T(8,128)(2,1)S(1)} %sum_gelu.2.h0), channel_id=1, source_target_pairs={{0,256},{128,384},{256,0},{384,128},{1,257},{129,385},{257,1},{385... | collective-permute-start | bytes 184328 | tf_op jit(solution)/shard_map/ppermute | solution.py:105
  175.2 33.7 %all-to-all-start.2 = ((bf16[16,40,768]{2,1,0:T(8,128)(2,1)}), bf16[16,40,768]{2,1,0:T(8,128)(2,1)S(1)}, u32[]{:S(2)}, u32[]{:S(2)}) async-start(bf16[16,40,768]{2,1,0:T(8,128)(2,1)} %second_product.2), calls=%async_computation.2 | async-start | bytes 1966080 | tf_op jit(solution)/shard_map/all_to_all | solution.py:137
  183.1 14.0 %collective-permute-start.18 = (bf16[40,768]{1,0:T(8,128)(2,1)S(1)}, bf16[40,768]{1,0:T(8,128)(2,1)S(1)}, u32[]{:S(2)}, u32[]{:S(2)}) collective-permute-start(bf16[40,768]{1,0:T(8,128)(2,1)S(1)} %sum_gelu.3.h0), channel_id=1, source_target_pairs={{0,128},{128,0},{256,384},{384,256},{1,129},{129,1},{257,385},{385... | collective-permute-start | bytes 184328 | tf_op jit(solution)/shard_map/ppermute | solution.py:105
  187.4 12.2 %collective-permute-start.19 = (bf16[40,768]{1,0:T(8,128)(2,1)S(1)}, bf16[40,768]{1,0:T(8,128)(2,1)S(1)}, u32[]{:S(2)}, u32[]{:S(2)}) collective-permute-start(bf16[40,768]{1,0:T(8,128)(2,1)S(1)} %sum_gelu.3.h0), channel_id=1, source_target_pairs={{0,256},{128,384},{256,0},{384,128},{1,257},{129,385},{257,1},{385... | collective-permute-start | bytes 184328 | tf_op jit(solution)/shard_map/ppermute | solution.py:105
  192.6 11.8 %collective-permute-start.20 = (bf16[40,768]{1,0:T(8,128)(2,1)S(1)}, bf16[40,768]{1,0:T(8,128)(2,1)S(1)}, u32[]{:S(2)}, u32[]{:S(2)}) collective-permute-start(bf16[40,768]{1,0:T(8,128)(2,1)S(1)} %sum_gelu.3.h0), channel_id=1, source_target_pairs={{0,384},{128,256},{256,128},{384,0},{1,385},{129,257},{257,129},{3... | collective-permute-start | bytes 184328 | tf_op jit(solution)/shard_map/ppermute | solution.py:105
  208.9 17.9 %all-to-all-start.3 = ((bf16[16,40,768]{2,1,0:T(8,128)(2,1)}), bf16[16,40,768]{2,1,0:T(8,128)(2,1)S(1)}, u32[]{:S(2)}, u32[]{:S(2)}) async-start(bf16[16,40,768]{2,1,0:T(8,128)(2,1)} %second_product.3), calls=%async_computation.3 | async-start | bytes 1966080 | tf_op jit(solution)/shard_map/all_to_all | solution.py:137
  216.3 22.7 %collective-permute-start.17 = (bf16[40,768]{1,0:T(8,128)(2,1)S(1)}, bf16[40,768]{1,0:T(8,128)(2,1)S(1)}, u32[]{:S(2)}, u32[]{:S(2)}) collective-permute-start(bf16[40,768]{1,0:T(8,128)(2,1)S(1)} %reduce_sum.24), channel_id=1, source_target_pairs={{0,1},{1,0},{2,33},{3,32},{8,65},{9,64},{10,97},{11,96},{32,3},{33... | collective-permute-start | bytes 184328 | tf_op jit(solution)/shard_map/ppermute | solution.py:139
  226.9 12.1 %collective-permute-start.21 = (bf16[40,768]{1,0:T(8,128)(2,1)S(1)}, bf16[40,768]{1,0:T(8,128)(2,1)S(1)}, u32[]{:S(2)}, u32[]{:S(2)}) collective-permute-start(bf16[40,768]{1,0:T(8,128)(2,1)S(1)} %reduce_sum.25), channel_id=1, source_target_pairs={{0,0},{1,1},{2,32},{3,33},{8,64},{9,65},{10,96},{11,97},{32,2},{33... | collective-permute-start | bytes 184328 | tf_op jit(solution)/shard_map/ppermute | solution.py:139
  (14 other events, 208.8 us)

commit v3 on v0

v3 whole, which is shorter than its diff:
```python
import jax
import jax.numpy as jnp
from jax import lax
from jax.experimental import pallas as pl
from jax.experimental.pallas import tpu as pltpu
from jax.sharding import Mesh
from jax.sharding import PartitionSpec as P

ROW = ("zq", "zb", "c")
COL = ("yp", "y0", "xp", "x0", "zh")
SIZES = (4, 2, 2, 2, 2, 2, 2, 2)
PLANE = ("yp", "y0", "xp", "x0")
CORNER = ("zb", "c", "y0", "x0", "zh")
SWAP = [(0, 1), (1, 0)]
VMEM = pl.BlockSpec(memory_space=pltpu.VMEM)

F32 = jnp.float32
BF16 = jnp.bfloat16
barrier = lax.optimization_barrier


def corner_pairs(other_zh):
    return [(i, ((i >> 1) & 3) << 3 | (i >> 3) << 1 | ((i & 1) ^ other_zh)) for i in range(32)]


def slot(block, dz, dc):
    y0 = jnp.bitwise_xor(lax.axis_index("zb"), dz)
    x0 = jnp.bitwise_xor(lax.axis_index("c"), dc)
    return (block & 2) * 4 + y0 * 4 + (block & 1) * 2 + x0


def kernel_call(kernel, shape, n_in, flops, nbytes, scratch=()):
    return pl.pallas_call(
        kernel,
        out_shape=jax.ShapeDtypeStruct(shape, BF16),
        in_specs=[VMEM] * n_in,
        out_specs=VMEM,
        scratch_shapes=scratch,
        compiler_params=pltpu.CompilerParams(vmem_limit_bytes=12 << 20),
        cost_estimate=pl.CostEstimate(flops=flops, bytes_accessed=nbytes, transcendentals=0),
    )


def first_kernel(got, w00, w01, w10, w11, part, total):
    for k, w in enumerate((w00, w01, w10, w11)):
        left = jnp.concatenate([got[slot(b, k // 2, k % 2)] for b in range(4)], axis=0)
        product = jnp.dot(left, w[...], preferred_element_type=F32)
        total[...] = product if k == 0 else total[...] + product
    part[...] = total[...].astype(BF16).reshape(4, 80, 768)


def middle_kernel(parts, bias, h):
    preact = bias[...].astype(F32)
    for k in range(4):
        preact = preact + parts[k].astype(F32)
    h[...] = jax.nn.gelu(preact, approximate=True).astype(BF16)


def second_kernel(hidden, w00, w01, w10, w11, out):
    left = hidden[...].reshape(320, 768)
    for k, w in enumerate((w00, w01, w10, w11)):
        product = jnp.dot(left, w[...], preferred_element_type=F32).astype(BF16)
        for b in range(4):
            out[slot(b, k // 2, k % 2)] = product[b * 80 : (b + 1) * 80]


def shards(tokens, w1, b1, w2, b2):
    tok = jnp.concatenate([lax.ppermute(tokens, CORNER, corner_pairs(k)) for k in range(2)], axis=0)
    w1_in, w2_in, tok = barrier((w1, w2, tok))

    def weights(w):
        w_z = lax.ppermute(w, "zb", SWAP)
        return [w, lax.ppermute(w, "c", SWAP), w_z, lax.ppermute(w_z, "c", SWAP)]

    w1_all = weights(w1_in)
    w2_all = weights(w2_in)

    spread = jnp.broadcast_to(tok[None], (16, 80, 768))
    got = lax.all_to_all(spread, PLANE, 0, 0, tiled=True)
    flops = 2 * 320 * 3072 * 768
    scratch = [pltpu.VMEM((320, 768), F32)]
    part = kernel_call(first_kernel, (4, 80, 768), 5, flops, 8 << 20, scratch)(got, *w1_all)
    part = lax.all_to_all(part, "zq", 0, 0, tiled=True)
    h = kernel_call(middle_kernel, (80, 768), 2, 20 * 80 * 768, 1 << 20)(part, b1.reshape(1, 768))
    hidden = lax.all_gather(h, "zq", axis=0, tiled=False)
    out = kernel_call(second_kernel, (16, 80, 768), 5, flops, 8 << 20)(hidden, *w2_all)
    out = lax.all_to_all(out, PLANE, 0, 0, tiled=True).astype(F32).sum(axis=0).astype(BF16)

    back = [lax.ppermute(out[k * 40 : (k + 1) * 40], CORNER, corner_pairs(k)) for k in range(2)]
    return (back[0].astype(F32) + back[1].astype(F32) + b2.astype(F32)).astype(BF16)


def solution(mesh):
    fine = Mesh(mesh.devices.reshape(SIZES), ROW + COL)
    in_specs = (P(COL, ROW), P(ROW, COL), P(COL), P(COL, ROW), P(ROW))
    return jax.shard_map(shards, mesh=fine, in_specs=in_specs, out_specs=P(COL, ROW), check_vma=False)
```

time: 679 us -> 190 us (0.28)
  the two profiles are of different devices: /device:TPU:1 before, /device:TPU:32 now
where the time goes in v3:
time: 190 us; the launch traced here: 189 us
  waiting for transfers between devices  61.2 us (32%)
  starting transfers between devices  60.5 us (32%)
  blocking collectives  55.2 us (29%)
  Pallas kernels  7.59 us (4%)
  local copies, waits for them, and re-layouts  3.75 us (2%)
    all_to_all x1, blocking collectives, shards(): lax.all_to_all(out, PLANE, 0, 0, tiled=True).astype(F32).sum(axis=0)  31.6 us
    ppermute x2, waiting for transfers between devices, weights(): w_z = lax.ppermute(w, 'zb', SWAP)  30.7 us
    all_gather x1, blocking collectives, shards(): hidden = lax.all_gather(h, 'zq', axis=0, tiled=False)  23.6 us
    ppermute x2, starting transfers between devices, shards(): lax.ppermute(tokens, CORNER, corner_pairs(k))  18.2 us
    ppermute x2, starting transfers between devices, shards(): lax.ppermute(out[k * 40:(k + 1) * 40], CORNER, corner_pairs(k))  17.9 us
    all_to_all x1, waiting for transfers between devices, shards(): part = lax.all_to_all(part, 'zq', 0, 0, tiled=True)  10.6 us
    ppermute x2, waiting for transfers between devices, shards(): lax.ppermute(tokens, CORNER, corner_pairs(k))  8.69 us
    ppermute x4, starting transfers between devices, weights(): return [w, lax.ppermute(w, 'c', SWAP), w_z, lax.ppermute(w_z, 'c', SWAP)]  7.83 us
  transfers between devices with their start and end apart: 12, of which 6 were waited for; matrix products, arithmetic and copies ran while one was open for 1% of the time, Pallas kernels for 2%

profile of v3, /device:TPU:32, one launch (start us, length us, event | category | flops | bytes accessed | tf_op | source)
XLA Modules:
  0.0 189.4 jit_solution(17061760873297722506)
XLA Ops:
  0.0 15.4 %collective-permute-start.1 = (bf16[40,768]{1,0:T(8,128)(2,1)}, bf16[40,768]{1,0:T(8,128)(2,1)S(1)}, u32[]{:S(2)}, u32[]{:S(2)}) collective-permute-start(bf16[40,768]{1,0:T(8,128)(2,1)} %param.5), channel_id=1, source_target_pairs={{0,1},{1,0},{2,33},{3,32},{8,65},{9,64},{10,97},{11,96},{32,3},{33... | collective-permute-start | bytes 184328 | tf_op jit(solution)/shard_map/ppermute | solution.py:68
  15.4 2.8 %collective-permute-start = (bf16[40,768]{1,0:T(8,128)(2,1)}, bf16[40,768]{1,0:T(8,128)(2,1)S(1)}, u32[]{:S(2)}, u32[]{:S(2)}) collective-permute-start(bf16[40,768]{1,0:T(8,128)(2,1)} %param.5), channel_id=1, source_target_pairs={{0,0},{1,1},{2,32},{3,33},{8,64},{9,65},{10,96},{11,97},{32,2},{33... | collective-permute-start | bytes 184328 | tf_op jit(solution)/shard_map/ppermute | solution.py:68
  18.2 8.7 %collective-permute-done.1 = bf16[40,768]{1,0:T(8,128)(2,1)S(1)} collective-permute-done((bf16[40,768]{1,0:T(8,128)(2,1)}, bf16[40,768]{1,0:T(8,128)(2,1)S(1)}, u32[]{:S(2)}, u32[]{:S(2)}) %collective-permute-start.1) | collective-permute-done | bytes 61472 | tf_op jit(solution)/shard_map/ppermute | solution.py:68
  26.9 1.9 %collective-permute-start.3 = (bf16[768,768]{1,0:T(8,128)(2,1)}, bf16[768,768]{1,0:T(8,128)(2,1)}, u32[]{:S(2)}, u32[]{:S(2)}) collective-permute-start(bf16[768,768]{1,0:T(8,128)(2,1)} %w00), channel_id=1, source_target_pairs={{0,64},{64,0},{1,65},{65,1},{2,66},{66,2},{3,67},{67,3},{4,68},{68... | collective-permute-start | bytes 3538952 | tf_op jit(solution)/shard_map/ppermute | solution.py:72
  28.8 1.4 broadcast_in_dim.2
  30.3 6.9 %all-to-all-start = ((bf16[16,80,768]{2,1,0:T(8,128)(2,1)}), bf16[16,80,768]{2,1,0:T(8,128)(2,1)S(1)}, u32[]{:S(2)}, u32[]{:S(2)}) async-start(bf16[16,80,768]{2,1,0:T(8,128)(2,1)} %broadcast_in_dim.2), calls=%async_computation | async-start | bytes 3932160 | tf_op jit(solution)/shard_map/all_to_all | solution.py:79
  37.2 2.1 %collective-permute-start.2 = (bf16[768,768]{1,0:T(8,128)(2,1)S(1)}, bf16[768,768]{1,0:T(8,128)(2,1)S(1)}, u32[]{:S(2)}, u32[]{:S(2)}) collective-permute-start(bf16[768,768]{1,0:T(8,128)(2,1)S(1)} %copy-done), channel_id=1, source_target_pairs={{0,32},{32,0},{1,33},{33,1},{2,34},{34,2},{3,35},{35,3},{4,36},{36... | collective-permute-start | bytes 3538952 | tf_op jit(solution)/shard_map/ppermute | solution.py:73
  39.3 18.3 %collective-permute-done.3.w10 = bf16[768,768]{1,0:T(8,128)(2,1)} collective-permute-done((bf16[768,768]{1,0:T(8,128)(2,1)}, bf16[768,768]{1,0:T(8,128)(2,1)}, u32[]{:S(2)}, u32[]{:S(2)}) %collective-permute-start.3) | collective-permute-done | bytes 1179680 | tf_op jit(solution)/shard_map/ppermute | solution.py:72
  57.7 1.9 %collective-permute-start.4 = (bf16[768,768]{1,0:T(8,128)(2,1)}, bf16[768,768]{1,0:T(8,128)(2,1)}, u32[]{:S(2)}, u32[]{:S(2)}) collective-permute-start(bf16[768,768]{1,0:T(8,128)(2,1)} %collective-permute-done.3.w10), channel_id=1, source_target_pairs={{0,32},{32,0},{1,33},{33,1},{2,34},{34,2},{3,35},{35,3},{4,36},{36... | collective-permute-start | bytes 3538952 | tf_op jit(solution)/shard_map/ppermute | solution.py:73
  59.6 2.3 %collective-permute-start.6 = (bf16[768,768]{1,0:T(8,128)(2,1)}, bf16[768,768]{1,0:T(8,128)(2,1)}, u32[]{:S(2)}, u32[]{:S(2)}) collective-permute-start(bf16[768,768]{1,0:T(8,128)(2,1)} %w00.1), channel_id=1, source_target_pairs={{0,64},{64,0},{1,65},{65,1},{2,66},{66,2},{3,67},{67,3},{4,68},{68... | collective-permute-start | bytes 3538952 | tf_op jit(solution)/shard_map/ppermute | solution.py:72
  63.0 6.6 %all-to-all-done.got = bf16[16,80,768]{2,1,0:T(8,128)(2,1)S(1)} async-done(((bf16[16,80,768]{2,1,0:T(8,128)(2,1)}), bf16[16,80,768]{2,1,0:T(8,128)(2,1)S(1)}, u32[]{:S(2)}, u32[]{:S(2)}) %all-to-all-start) | async-done | bytes 1966112 | tf_op jit(solution)/shard_map/all_to_all | solution.py:79
  69.5 1.3 copy-done.3
  70.8 4.1 %shard_map.55 = bf16[4,80,768]{2,1,0:T(8,128)(2,1)} custom-call(bf16[16,80,768]{2,1,0:T(8,128)(2,1)S(1)} %all-to-all-done.got, bf16[768,768]{1,0:T(8,128)(2,1)S(1)} %copy-done, bf16[768,768]{1,0:T(8,128)(2,1)S(1)} %copy-done.3, bf16[768,768]{1,0:T(8,128)(2,1)} %collective-permute-done.3.w10, bf16[768,768]{1,0:T(8,128)(2,1)} %collective-permute-done.4.w11), custom_call_target="tpu_custom_call" | custom-call | flops 1509949440 | bytes 8388608 | tf_op jit(solution)/shard_map/pallas_call | solution.py:82
  74.9 5.4 %all-to-all-start.1 = ((bf16[4,80,768]{2,1,0:T(8,128)(2,1)}), bf16[4,80,768]{2,1,0:T(8,128)(2,1)S(1)}, u32[]{:S(2)}, u32[]{:S(2)}) async-start(bf16[4,80,768]{2,1,0:T(8,128)(2,1)} %shard_map.55), calls=%async_computation.1 | async-start | bytes 983040 | tf_op jit(solution)/shard_map/all_to_all | solution.py:83
  80.3 1.9 %collective-permute-start.5 = (bf16[768,768]{1,0:T(8,128)(2,1)}, bf16[768,768]{1,0:T(8,128)(2,1)S(1)}, u32[]{:S(2)}, u32[]{:S(2)}) collective-permute-start(bf16[768,768]{1,0:T(8,128)(2,1)} %w00.1), channel_id=1, source_target_pairs={{0,32},{32,0},{1,33},{33,1},{2,34},{34,2},{3,35},{35,3},{4,36},{36... | collective-permute-start | bytes 3538952 | tf_op jit(solution)/shard_map/ppermute | solution.py:73
  82.2 12.4 %collective-permute-done.6.w10 = bf16[768,768]{1,0:T(8,128)(2,1)} collective-permute-done((bf16[768,768]{1,0:T(8,128)(2,1)}, bf16[768,768]{1,0:T(8,128)(2,1)}, u32[]{:S(2)}, u32[]{:S(2)}) %collective-permute-start.6) | collective-permute-done | bytes 1179680 | tf_op jit(solution)/shard_map/ppermute | solution.py:72
  94.6 1.9 %collective-permute-start.7 = (bf16[768,768]{1,0:T(8,128)(2,1)}, bf16[768,768]{1,0:T(8,128)(2,1)}, u32[]{:S(2)}, u32[]{:S(2)}) collective-permute-start(bf16[768,768]{1,0:T(8,128)(2,1)} %collective-permute-done.6.w10), channel_id=1, source_target_pairs={{0,32},{32,0},{1,33},{33,1},{2,34},{34,2},{3,35},{35,3},{4,36},{36... | collective-permute-start | bytes 3538952 | tf_op jit(solution)/shard_map/ppermute | solution.py:73
  96.5 10.6 %all-to-all-done.1.parts = bf16[4,80,768]{2,1,0:T(8,128)(2,1)S(1)} async-done(((bf16[4,80,768]{2,1,0:T(8,128)(2,1)}), bf16[4,80,768]{2,1,0:T(8,128)(2,1)S(1)}, u32[]{:S(2)}, u32[]{:S(2)}) %all-to-all-start.1) | async-done | bytes 491552 | tf_op jit(solution)/shard_map/all_to_all | solution.py:83
  107.3 23.6 %all-gather = bf16[320,768]{1,0:T(8,128)(2,1)S(1)} all-gather(bf16[80,768]{1,0:T(8,128)(2,1)S(1)} %shard_map.56), channel_id=2, replica_groups=mesh['zq'=4,'zb'=2,'c'=2,'yp'=2,'y0'=2,'xp'=2,'x0'=2,'zh'=2] {'zq'}, dimensions={0}, use_global_device_ids=true | all-gather | bytes 614400 | tf_op jit(solution)/shard_map/all_gather | solution.py:85
  130.9 3.3 %shard_map.57 = bf16[16,80,768]{2,1,0:T(8,128)(2,1)S(1)} custom-call(bf16[4,80,768]{2,1,0:T(8,128)(2,1)S(1)} %bitcast.1, bf16[768,768]{1,0:T(8,128)(2,1)S(1)} %copy-done.1, bf16[768,768]{1,0:T(8,128)(2,1)S(1)} %collective-permute-done.5.w01, bf16[768,768]{1,0:T(8,128)(2,1)} %collective-permute-done.6.w10, bf16[768,768]{1,0:T(8,128)(2,1)} %collective-permute-done.7.w11), custom_call_target="tpu_custom_call" | custom-call | flops 1509949440 | bytes 8388608 | tf_op jit(solution)/shard_map/pallas_call | solution.py:86
  134.3 31.6 %all_to_all.15 = bf16[16,80,768]{2,1,0:T(8,128)(2,1)S(1)} all-to-all(bf16[16,80,768]{2,1,0:T(8,128)(2,1)S(1)} %shard_map.57), channel_id=1, replica_groups=mesh['zq'=4,'zb'=2,'c'=2,'yp'=2,'y0'=2,'xp'=2,'x0'=2,'zh'=2] {'yp','y0',..., dimensions={0} | all-to-all | bytes 3932160 | tf_op jit(solution)/shard_map/all_to_all | solution.py:87
  166.1 9.3 %collective-permute-start.9 = (bf16[40,768]{1,0:T(8,128)(2,1)S(1)}, bf16[40,768]{1,0:T(8,128)(2,1)S(1)}, u32[]{:S(2)}, u32[]{:S(2)}) collective-permute-start(bf16[40,768]{1,0:T(8,128)(2,1)S(1)} %get-tuple-element.12), channel_id=1, source_target_pairs={{0,1},{1,0},{2,33},{3,32},{8,65},{9,64},{10,97},{11,96},{32,3},{33... | collective-permute-start | bytes 184328 | tf_op jit(solution)/shard_map/ppermute | solution.py:89
  175.5 8.6 %collective-permute-start.8 = (bf16[40,768]{1,0:T(8,128)(2,1)S(1)}, bf16[40,768]{1,0:T(8,128)(2,1)S(1)}, u32[]{:S(2)}, u32[]{:S(2)}) collective-permute-start(bf16[40,768]{1,0:T(8,128)(2,1)S(1)} %get-tuple-element.11), channel_id=1, source_target_pairs={{0,0},{1,1},{2,32},{3,33},{8,64},{9,65},{10,96},{11,97},{32,2},{33... | collective-permute-start | bytes 184328 | tf_op jit(solution)/shard_map/ppermute | solution.py:89
  184.1 4.7 %collective-permute-done.9 = bf16[40,768]{1,0:T(8,128)(2,1)S(1)} collective-permute-done((bf16[40,768]{1,0:T(8,128)(2,1)S(1)}, bf16[40,768]{1,0:T(8,128)(2,1)S(1)}, u32[]{:S(2)}, u32[]{:S(2)}) %collective-permute-start.9) | collective-permute-done | bytes 61472 | tf_op jit(solution)/shard_map/ppermute | solution.py:89
  (24 shorter events, 2.2 us)
Async XLA Ops:
  0.0 26.9 %collective-permute-start.1 = (bf16[40,768]{1,0:T(8,128)(2,1)}, bf16[40,768]{1,0:T(8,128)(2,1)S(1)}, u32[]{:S(2)}, u32[]{:S(2)}) collective-permute-start(bf16[40,768]{1,0:T(8,128)(2,1)} %param.5), channel_id=1, source_target_pairs={{0,1},{1,0},{2,33},{3,32},{8,65},{9,64},{10,97},{11,96},{32,3},{33... | collective-permute-start | bytes 184328 | tf_op jit(solution)/shard_map/ppermute | solution.py:68
  15.4 11.5 %collective-permute-start = (bf16[40,768]{1,0:T(8,128)(2,1)}, bf16[40,768]{1,0:T(8,128)(2,1)S(1)}, u32[]{:S(2)}, u32[]{:S(2)}) collective-permute-start(bf16[40,768]{1,0:T(8,128)(2,1)} %param.5), channel_id=1, source_target_pairs={{0,0},{1,1},{2,32},{3,33},{8,64},{9,65},{10,96},{11,97},{32,2},{33... | collective-permute-start | bytes 184328 | tf_op jit(solution)/shard_map/ppermute | solution.py:68
  26.9 30.8 %collective-permute-start.3 = (bf16[768,768]{1,0:T(8,128)(2,1)}, bf16[768,768]{1,0:T(8,128)(2,1)}, u32[]{:S(2)}, u32[]{:S(2)}) collective-permute-start(bf16[768,768]{1,0:T(8,128)(2,1)} %w00), channel_id=1, source_target_pairs={{0,64},{64,0},{1,65},{65,1},{2,66},{66,2},{3,67},{67,3},{4,68},{68... | collective-permute-start | bytes 3538952 | tf_op jit(solution)/shard_map/ppermute | solution.py:72
  30.3 7.0 %copy-start = (bf16[768,768]{1,0:T(8,128)(2,1)S(1)}, bf16[768,768]{1,0:T(8,128)(2,1)}, u32[]{:S(2)}) copy-start(bf16[768,768]{1,0:T(8,128)(2,1)} %w00) | copy-start | bytes 3538948
  30.3 66.3 %copy-start.5 = (bf16[768]{0:T(1024)(128)(2,1)S(1)}, bf16[768]{0:T(1024)(128)(2,1)}, u32[]{:S(2)}) copy-start(bf16[768]{0:T(1024)(128)(2,1)} %param.7) | copy-start | bytes 4612
  30.3 39.2 %all-to-all-start = ((bf16[16,80,768]{2,1,0:T(8,128)(2,1)}), bf16[16,80,768]{2,1,0:T(8,128)(2,1)S(1)}, u32[]{:S(2)}, u32[]{:S(2)}) async-start(bf16[16,80,768]{2,1,0:T(8,128)(2,1)} %broadcast_in_dim.2), calls=%async_computation | async-start | bytes 3932160 | tf_op jit(solution)/shard_map/all_to_all | solution.py:79
  37.2 24.7 %collective-permute-start.2 = (bf16[768,768]{1,0:T(8,128)(2,1)S(1)}, bf16[768,768]{1,0:T(8,128)(2,1)S(1)}, u32[]{:S(2)}, u32[]{:S(2)}) collective-permute-start(bf16[768,768]{1,0:T(8,128)(2,1)S(1)} %copy-done), channel_id=1, source_target_pairs={{0,32},{32,0},{1,33},{33,1},{2,34},{34,2},{3,35},{35,3},{4,36},{36... | collective-permute-start | bytes 3538952 | tf_op jit(solution)/shard_map/ppermute | solution.py:73
  57.7 11.8 %collective-permute-start.4 = (bf16[768,768]{1,0:T(8,128)(2,1)}, bf16[768,768]{1,0:T(8,128)(2,1)}, u32[]{:S(2)}, u32[]{:S(2)}) collective-permute-start(bf16[768,768]{1,0:T(8,128)(2,1)} %collective-permute-done.3.w10), channel_id=1, source_target_pairs={{0,32},{32,0},{1,33},{33,1},{2,34},{34,2},{3,35},{35,3},{4,36},{36... | collective-permute-start | bytes 3538952 | tf_op jit(solution)/shard_map/ppermute | solution.py:73
  59.6 35.0 %collective-permute-start.6 = (bf16[768,768]{1,0:T(8,128)(2,1)}, bf16[768,768]{1,0:T(8,128)(2,1)}, u32[]{:S(2)}, u32[]{:S(2)}) collective-permute-start(bf16[768,768]{1,0:T(8,128)(2,1)} %w00.1), channel_id=1, source_target_pairs={{0,64},{64,0},{1,65},{65,1},{2,66},{66,2},{3,67},{67,3},{4,68},{68... | collective-permute-start | bytes 3538952 | tf_op jit(solution)/shard_map/ppermute | solution.py:72
  61.9 1.0 copy-start.2
  69.5 1.3 copy-start.3
  74.9 56.0 %copy-start.1 = (bf16[768,768]{1,0:T(8,128)(2,1)S(1)}, bf16[768,768]{1,0:T(8,128)(2,1)}, u32[]{:S(2)}) copy-start(bf16[768,768]{1,0:T(8,128)(2,1)} %w00.1) | copy-start | bytes 3538948
  74.9 32.3 %all-to-all-start.1 = ((bf16[4,80,768]{2,1,0:T(8,128)(2,1)}), bf16[4,80,768]{2,1,0:T(8,128)(2,1)S(1)}, u32[]{:S(2)}, u32[]{:S(2)}) async-start(bf16[4,80,768]{2,1,0:T(8,128)(2,1)} %shard_map.55), calls=%async_computation.1 | async-start | bytes 983040 | tf_op jit(solution)/shard_map/all_to_all | solution.py:83
  80.3 50.6 %collective-permute-start.5 = (bf16[768,768]{1,0:T(8,128)(2,1)}, bf16[768,768]{1,0:T(8,128)(2,1)S(1)}, u32[]{:S(2)}, u32[]{:S(2)}) collective-permute-start(bf16[768,768]{1,0:T(8,128)(2,1)} %w00.1), channel_id=1, source_target_pairs={{0,32},{32,0},{1,33},{33,1},{2,34},{34,2},{3,35},{35,3},{4,36},{36... | collective-permute-start | bytes 3538952 | tf_op jit(solution)/shard_map/ppermute | solution.py:73
  94.6 36.3 %collective-permute-start.7 = (bf16[768,768]{1,0:T(8,128)(2,1)}, bf16[768,768]{1,0:T(8,128)(2,1)}, u32[]{:S(2)}, u32[]{:S(2)}) collective-permute-start(bf16[768,768]{1,0:T(8,128)(2,1)} %collective-permute-done.6.w10), channel_id=1, source_target_pairs={{0,32},{32,0},{1,33},{33,1},{2,34},{34,2},{3,35},{35,3},{4,36},{36... | collective-permute-start | bytes 3538952 | tf_op jit(solution)/shard_map/ppermute | solution.py:73
  165.8 18.2 %copy-start.4 = (bf16[768]{0:T(1024)(128)(2,1)S(1)}, bf16[768]{0:T(1024)(128)(2,1)}, u32[]{:S(2)}) copy-start(bf16[768]{0:T(1024)(128)(2,1)} %param.9) | copy-start | bytes 4612
  166.1 22.6 %collective-permute-start.9 = (bf16[40,768]{1,0:T(8,128)(2,1)S(1)}, bf16[40,768]{1,0:T(8,128)(2,1)S(1)}, u32[]{:S(2)}, u32[]{:S(2)}) collective-permute-start(bf16[40,768]{1,0:T(8,128)(2,1)S(1)} %get-tuple-element.12), channel_id=1, source_target_pairs={{0,1},{1,0},{2,33},{3,32},{8,65},{9,64},{10,97},{11,96},{32,3},{33... | collective-permute-start | bytes 184328 | tf_op jit(solution)/shard_map/ppermute | solution.py:89
  175.5 13.3 %collective-permute-start.8 = (bf16[40,768]{1,0:T(8,128)(2,1)S(1)}, bf16[40,768]{1,0:T(8,128)(2,1)S(1)}, u32[]{:S(2)}, u32[]{:S(2)}) collective-permute-start(bf16[40,768]{1,0:T(8,128)(2,1)S(1)} %get-tuple-element.11), channel_id=1, source_target_pairs={{0,0},{1,1},{2,32},{3,33},{8,64},{9,65},{10,96},{11,97},{32,2},{33... | collective-permute-start | bytes 184328 | tf_op jit(solution)/shard_map/ppermute | solution.py:89

commit v4 on v3

v4 whole, which is shorter than its diff:
```python
import jax
import jax.numpy as jnp
from jax import lax
from jax.experimental import pallas as pl
from jax.experimental.pallas import tpu as pltpu
from jax.sharding import Mesh
from jax.sharding import PartitionSpec as P

ROW = ("zq", "zb", "c")
COL = ("yp", "y0", "xp", "x0", "zh")
SIZES = (4, 2, 2, 2, 2, 2, 2, 2)
PLANE = ("yp", "y0", "xp", "x0")
CORNER = ("zb", "c", "y0", "x0", "zh")
SWAP = [(0, 1), (1, 0)]
EARLY = 256
VMEM = pl.BlockSpec(memory_space=pltpu.VMEM)
ANY = pl.BlockSpec(memory_space=pl.ANY)

F32 = jnp.float32
BF16 = jnp.bfloat16
barrier = lax.optimization_barrier


def corner_pairs(other_zh):
    return [(i, ((i >> 1) & 3) << 3 | (i >> 3) << 1 | ((i & 1) ^ other_zh)) for i in range(32)]


def slot(block, dz, dc):
    y0 = jnp.bitwise_xor(lax.axis_index("zb"), dz)
    x0 = jnp.bitwise_xor(lax.axis_index("c"), dc)
    return (block & 2) * 4 + y0 * 4 + (block & 1) * 2 + x0


def kernel_call(kernel, shapes, specs, flops, nbytes, scratch=(), limit=16):
    return pl.pallas_call(
        kernel,
        out_shape=shapes,
        in_specs=specs,
        out_specs=[VMEM] * len(shapes),
        scratch_shapes=scratch,
        compiler_params=pltpu.CompilerParams(vmem_limit_bytes=limit << 20),
        cost_estimate=pl.CostEstimate(flops=flops, bytes_accessed=nbytes, transcendentals=0),
    )


def fetch(pairs, sems):
    copies = [pltpu.make_async_copy(src, dst, sems.at[i]) for i, (src, dst) in enumerate(pairs)]
    for copy in copies:
        copy.start()
    return copies


def parts_of(blocks, held):
    if not isinstance(blocks, tuple):
        return [(blocks, held)]
    return [(blocks[0], held.at[:EARLY]), (blocks[1], held.at[EARLY:])]


def held_blocks(n):
    return [pltpu.VMEM((n, 768, 768), BF16), pltpu.SemaphoreType.DMA((n, 2))]


def left_blocks(n):
    return [pltpu.VMEM((n, 320, 768), BF16), pltpu.SemaphoreType.DMA((n, 4))]


def products(got, ks, blocks, left, left_sems, held, sems):
    copies = []
    for i, k in enumerate(ks):
        rows = [(got.at[slot(b, k // 2, k % 2)], left.at[i, b * 80 : (b + 1) * 80]) for b in range(4)]
        copies.append(fetch(rows, left_sems.at[i]) + fetch(parts_of(blocks[i], held.at[i]), sems.at[i]))
    for i in range(len(ks)):
        for copy in copies[i]:
            copy.wait()
        yield jnp.dot(left[i], held[i], preferred_element_type=F32)


def first_kernel(got, w00, w01, w10a, w10b, total, *scratch):
    for k, product in enumerate(products(got, (0, 1, 2), (w00, w01, (w10a, w10b)), *scratch)):
        total[...] = product if k == 0 else total[...] + product


def first_rest_kernel(got, w11a, w11b, total, part, *scratch):
    (product,) = products(got, (3,), ((w11a, w11b),), *scratch)
    part[...] = (total[...] + product).astype(BF16).reshape(4, 80, 768)


def middle_kernel(parts, bias, here, other):
    preact = bias[...].astype(F32)
    for k in range(4):
        preact = preact + parts[k].astype(F32)
    h = jax.nn.gelu(preact, approximate=True).astype(BF16)
    here[...] = h[:40]
    other[...] = h[40:]


def spread_product(left, first_block, blocks, out, held, sems):
    copies = [fetch(parts_of(block, held.at[k]), sems.at[k]) for k, block in enumerate(blocks)]
    for k in range(4):
        for copy in copies[k]:
            copy.wait()
        product = jnp.dot(left, held[k], preferred_element_type=F32)
        for j in range(4):
            rows = product[j * 40 : (j + 1) * 40]
            out[slot(jnp.bitwise_xor(first_block, j), k // 2, k % 2)] = rows.astype(BF16)


def second_kernel(h0, h1, h2, h3, w00, w01, w10, w11, out, held, sems):
    left = jnp.concatenate([h[...] for h in (h0, h1, h2, h3)], axis=0)
    spread_product(left, lax.axis_index("zq"), (w00, w01, w10, w11), out, held, sems)


def second_gathered_kernel(hidden, w00, w01, w10, w11, out, held, sems):
    left = jnp.concatenate([hidden[j] for j in range(4)], axis=0)
    spread_product(left, 0, (w00, w01, w10, w11), out, held, sems)


def shards(tokens, w1, b1, w2, b2):
    here, other = (lax.ppermute(tokens, CORNER, corner_pairs(k)) for k in range(2))
    w1_za = lax.ppermute(w1[:EARLY], "zb", SWAP)
    here, other, w1_za = barrier((here, other, w1_za))
    w1_in, here = barrier((w1, here))
    w1_zb = lax.ppermute(w1_in[EARLY:], "zb", SWAP)
    w1_c = lax.ppermute(w1_in, "c", SWAP)
    w1_zca = lax.ppermute(w1_za, "c", SWAP)

    tok = jnp.concatenate([here, other], axis=0)
    spread = jnp.broadcast_to(tok[None], (16, 80, 768))
    got = lax.all_to_all(spread, PLANE, 0, 0, tiled=True)
    w2_in, w1_zca = barrier((w2, w1_zca))
    w1_zb, w1_zca, w1_c, got = barrier((w1_zb, w1_zca, w1_c, got))
    w1_zcb = lax.ppermute(w1_zb, "c", SWAP)
    w2_z = lax.ppermute(w2_in, "zb", SWAP)

    flops = 2 * 320 * 768 * 768
    shapes = [jax.ShapeDtypeStruct((320, 768), F32)]
    scratch = left_blocks(3) + held_blocks(3)
    first = kernel_call(first_kernel, shapes, [ANY] * 5, 3 * flops, 8 << 20, scratch, 60)
    (total,) = first(got, w1, w1_c, w1_za, w1_zb)
    shapes = [jax.ShapeDtypeStruct((4, 80, 768), BF16)]
    scratch = left_blocks(1) + held_blocks(1)
    first_rest = kernel_call(first_rest_kernel, shapes, [ANY] * 3 + [VMEM], flops, 3 << 20, scratch, 60)
    (part,) = first_rest(got, w1_zca, w1_zcb, total)
    w2_all = [w2, lax.ppermute(w2_in, "c", SWAP), w2_z, lax.ppermute(w2_z, "c", SWAP)]

    part = lax.all_to_all(part, "zq", 0, 0, tiled=True)
    shapes = [jax.ShapeDtypeStruct((40, 768), BF16)] * 2
    here, other = kernel_call(middle_kernel, shapes, [VMEM] * 2, 20 * 80 * 768, 1 << 20)(part, b1.reshape(1, 768))

    flops = 2 * 160 * 3072 * 768
    shapes = [jax.ShapeDtypeStruct((16, 40, 768), BF16)]
    hidden = lax.all_gather(other, "zq", axis=0, tiled=False)
    here, hidden = barrier((here, hidden))
    rows = [here] + [lax.ppermute(here, "zq", [(i, i ^ k) for i in range(4)]) for k in range(1, 4)]
    specs = [VMEM] + [ANY] * 4
    (out,) = kernel_call(second_gathered_kernel, shapes, specs, flops, 6 << 20, held_blocks(4))(hidden, *w2_all)
    other = lax.all_to_all(out, PLANE, 0, 0, tiled=True)
    specs = [VMEM] * 4 + [ANY] * 4
    (out,) = kernel_call(second_kernel, shapes, specs, flops, 6 << 20, held_blocks(4))(*rows, *w2_all)
    out, other = barrier((out, other))
    here = lax.all_to_all(out, PLANE, 0, 0, tiled=True)

    total = b2.astype(F32)
    for k, out in ((1, other), (0, here)):
        out = out.astype(F32).sum(axis=0).astype(BF16)
        total = total + lax.ppermute(out, CORNER, corner_pairs(k)).astype(F32)
    return total.astype(BF16)


def solution(mesh):
    fine = Mesh(mesh.devices.reshape(SIZES), ROW + COL)
    in_specs = (P(COL, ROW), P(ROW, COL), P(COL), P(COL, ROW), P(ROW))
    return jax.shard_map(shards, mesh=fine, in_specs=in_specs, out_specs=P(COL, ROW), check_vma=False)
```

time: 190 us -> 218 us (1.15)
  the two profiles are of different devices: /device:TPU:32 before, /device:TPU:14 now
where the time goes in v4:
time: 218 us; the launch traced here: 217 us
  starting transfers between devices  92.7 us (43%)
  waiting for transfers between devices  70.7 us (32%)
  blocking collectives  27.1 us (12%)
  Pallas kernels  15 us (7%)
  local copies, waits for them, and re-layouts  9.21 us (4%)
    all_gather x1, blocking collectives, shards(): hidden = lax.all_gather(other, 'zq', axis=0, tiled=False)  27.1 us
    ppermute x1, waiting for transfers between devices, shards(): w2_z = lax.ppermute(w2_in, 'zb', SWAP)  19.4 us
    ppermute x2, starting transfers between devices, shards(): lax.ppermute(tokens, CORNER, corner_pairs(k))  18.8 us
    ppermute x3, starting transfers between devices, shards(): lax.ppermute(here, 'zq', [(i, i ^ k) for i in range(4)])  14.3 us
    ppermute x1, waiting for transfers between devices, shards(): w1_zb = lax.ppermute(w1_in[EARLY:], 'zb', SWAP)  14.1 us
    ppermute x3, waiting for transfers between devices, shards(): lax.ppermute(here, 'zq', [(i, i ^ k) for i in range(4)])  10.1 us
    ppermute x2, waiting for transfers between devices, shards(): total = total + lax.ppermute(out, CORNER, corner_pairs(k)).astype(F32)  9.91 us
    ppermute x2, waiting for transfers between devices, shards(): lax.ppermute(tokens, CORNER, corner_pairs(k))  9.01 us
  transfers between devices with their start and end apart: 19, of which 8 were waited for; matrix products, arithmetic and copies ran while one was open for 1% of the time, Pallas kernels for 6%

profile of v4, /device:TPU:14, one launch (start us, length us, event | category | flops | bytes accessed | tf_op | source)
XLA Modules:
  0.0 217.1 jit_solution(12088844667108130578)
XLA Ops:
  1.0 3.8 %collective-permute-start.2 = (bf16[256,768]{1,0:T(8,128)(2,1)S(1)}, bf16[256,768]{1,0:T(8,128)(2,1)S(1)}, u32[]{:S(2)}, u32[]{:S(2)}) collective-permute-start(bf16[256,768]{1,0:T(8,128)(2,1)S(1)} %slice.6), channel_id=1, source_target_pairs={{0,64},{64,0},{1,65},{65,1},{2,66},{66,2},{3,67},{67,3},{4,68},{68... | collective-permute-start | bytes 1179656 | tf_op jit(solution)/shard_map/ppermute | solution.py:120
  6.8 16.9 %collective-permute-start.1 = (bf16[40,768]{1,0:T(8,128)(2,1)}, bf16[40,768]{1,0:T(8,128)(2,1)S(1)}, u32[]{:S(2)}, u32[]{:S(2)}) collective-permute-start(bf16[40,768]{1,0:T(8,128)(2,1)} %param.5), channel_id=1, source_target_pairs={{0,1},{1,0},{2,33},{3,32},{8,65},{9,64},{10,97},{11,96},{32,3},{33... | collective-permute-start | bytes 184328 | tf_op jit(solution)/shard_map/ppermute | solution.py:119
  23.7 9.0 %collective-permute-done.1 = bf16[40,768]{1,0:T(8,128)(2,1)S(1)} collective-permute-done((bf16[40,768]{1,0:T(8,128)(2,1)}, bf16[40,768]{1,0:T(8,128)(2,1)S(1)}, u32[]{:S(2)}, u32[]{:S(2)}) %collective-permute-start.1) | collective-permute-done | bytes 61472 | tf_op jit(solution)/shard_map/ppermute | solution.py:119
  34.1 7.8 %all-to-all-start = ((bf16[16,80,768]{2,1,0:T(8,128)(2,1)}), bf16[16,80,768]{2,1,0:T(8,128)(2,1)S(1)}, u32[]{:S(2)}, u32[]{:S(2)}) async-start(bf16[16,80,768]{2,1,0:T(8,128)(2,1)} %broadcast_in_dim.2), calls=%async_computation | async-start | bytes 3932160 | tf_op jit(solution)/shard_map/all_to_all | solution.py:129
  45.2 5.2 %collective-permute-start.3 = (bf16[512,768]{1,0:T(8,128)(2,1)S(1)}, bf16[512,768]{1,0:T(8,128)(2,1)S(1)}, u32[]{:S(2)}, u32[]{:S(2)}) collective-permute-start(bf16[512,768]{1,0:T(8,128)(2,1)S(1)} %slice.7), channel_id=1, source_target_pairs={{0,64},{64,0},{1,65},{65,1},{2,66},{66,2},{3,67},{67,3},{4,68},{68... | collective-permute-start | bytes 2359304 | tf_op jit(solution)/shard_map/ppermute | solution.py:123
  54.1 14.1 %collective-permute-done.3.w10b = bf16[512,768]{1,0:T(8,128)(2,1)S(1)} collective-permute-done((bf16[512,768]{1,0:T(8,128)(2,1)S(1)}, bf16[512,768]{1,0:T(8,128)(2,1)S(1)}, u32[]{:S(2)}, u32[]{:S(2)}) %collective-permute-start.3) | collective-permute-done | bytes 786464 | tf_op jit(solution)/shard_map/ppermute | solution.py:123
  72.3 6.1 %collective-permute-start.11 = (bf16[768,768]{1,0:T(8,128)(2,1)S(1)}, bf16[768,768]{1,0:T(8,128)(2,1)S(1)}, u32[]{:S(2)}, u32[]{:S(2)}) collective-permute-start(bf16[768,768]{1,0:T(8,128)(2,1)S(1)} %copy-done), channel_id=1, source_target_pairs={{0,64},{64,0},{1,65},{65,1},{2,66},{66,2},{3,67},{67,3},{4,68},{68... | collective-permute-start | bytes 3538952 | tf_op jit(solution)/shard_map/ppermute | solution.py:133
  78.3 4.8 %shard_map.55.total = f32[320,768]{1,0:T(8,128)} custom-call(bf16[16,80,768]{2,1,0:T(8,128)(2,1)} %copy-done.5, bf16[768,768]{1,0:T(8,128)(2,1)} %w00.3, bf16[768,768]{1,0:T(8,128)(2,1)} %collective-permute-done.5.w01, bf16[256,768]{1,0:T(8,128)(2,1)} %copy-done.7, bf16[512,768]{1,0:T(8,128)(2,1)} %copy-done.6), custom_call_target="tpu_custom_call" | custom-call | flops 1132462080 | bytes 8388608 | tf_op jit(solution)/shard_map/pallas_call | solution.py:139
  83.2 4.0 %shard_map.56 = bf16[4,80,768]{2,1,0:T(8,128)(2,1)} custom-call(bf16[16,80,768]{2,1,0:T(8,128)(2,1)} %copy-done.5, bf16[256,768]{1,0:T(8,128)(2,1)} %copy-done.8, bf16[512,768]{1,0:T(8,128)(2,1)} %collective-permute-done.6.w11b, f32[320,768]{1,0:T(8,128)} %shard_map.55.total), custom_call_target="tpu_custom_call" | custom-call | flops 377487360 | bytes 3145728 | tf_op jit(solution)/shard_map/pallas_call | solution.py:143
  87.2 4.1 %all-to-all-start.1 = ((bf16[4,80,768]{2,1,0:T(8,128)(2,1)}), bf16[4,80,768]{2,1,0:T(8,128)(2,1)}, u32[]{:S(2)}, u32[]{:S(2)}) async-start(bf16[4,80,768]{2,1,0:T(8,128)(2,1)} %shard_map.56), calls=%async_computation.1 | async-start | bytes 983040 | tf_op jit(solution)/shard_map/all_to_all | solution.py:146
  91.3 2.1 collective-permute-start.10
  93.5 19.4 %collective-permute-done.11.w10 = bf16[768,768]{1,0:T(8,128)(2,1)S(1)} collective-permute-done((bf16[768,768]{1,0:T(8,128)(2,1)S(1)}, bf16[768,768]{1,0:T(8,128)(2,1)S(1)}, u32[]{:S(2)}, u32[]{:S(2)}) %collective-permute-start.11) | collective-permute-done | bytes 1179680 | tf_op jit(solution)/shard_map/ppermute | solution.py:133
  116.6 27.1 %all-gather = bf16[160,768]{1,0:T(8,128)(2,1)S(1)} all-gather(bf16[40,768]{1,0:T(8,128)(2,1)S(1)} %get-tuple-element.33), channel_id=2, replica_groups=mesh['zq'=4,'zb'=2,'c'=2,'yp'=2,'y0'=2,'xp'=2,'x0'=2,'zh'=2] {'zq'}, dimensions={0}, use_global_device_ids=true | all-gather | bytes 307200 | tf_op jit(solution)/shard_map/all_gather | solution.py:152
  143.8 2.5 %shard_map.59 = bf16[16,40,768]{2,1,0:T(8,128)(2,1)S(1)} custom-call(bf16[4,40,768]{2,1,0:T(8,128)(2,1)S(1)} %bitcast.1, bf16[768,768]{1,0:T(8,128)(2,1)S(1)} %copy-done, bf16[768,768]{1,0:T(8,128)(2,1)S(1)} %collective-permute-done.10.w01, bf16[768,768]{1,0:T(8,128)(2,1)S(1)} %collective-permute-done.11.w10, bf16[768,768]{1,0:T(8,128)(2,1)} %collective-permute-done.12.w11), custom_call_target="tpu_custom_call" | custom-call | flops 754974720 | bytes 6291456 | tf_op jit(solution)/shard_map/pallas_call | solution.py:156
  147.2 9.0 %all-to-all-start.2 = ((bf16[16,40,768]{2,1,0:T(8,128)(2,1)}), bf16[16,40,768]{2,1,0:T(8,128)(2,1)}, u32[]{:S(2)}, u32[]{:S(2)}) async-start(bf16[16,40,768]{2,1,0:T(8,128)(2,1)} %copy-done.1), calls=%async_computation.2 | async-start | bytes 1966080 | tf_op jit(solution)/shard_map/all_to_all | solution.py:157
  156.2 5.0 %collective-permute-start.7 = (bf16[40,768]{1,0:T(8,128)(2,1)}, bf16[40,768]{1,0:T(8,128)(2,1)S(1)}, u32[]{:S(2)}, u32[]{:S(2)}) collective-permute-start(bf16[40,768]{1,0:T(8,128)(2,1)} %copy-done.3), channel_id=1, source_target_pairs={{0,128},{128,0},{256,384},{384,256},{1,129},{129,1},{257,385},{385... | collective-permute-start | bytes 184328 | tf_op jit(solution)/shard_map/ppermute | solution.py:154
  161.3 7.4 %collective-permute-start.8 = (bf16[40,768]{1,0:T(8,128)(2,1)}, bf16[40,768]{1,0:T(8,128)(2,1)S(1)}, u32[]{:S(2)}, u32[]{:S(2)}) collective-permute-start(bf16[40,768]{1,0:T(8,128)(2,1)} %copy-done.3), channel_id=1, source_target_pairs={{0,256},{128,384},{256,0},{384,128},{1,257},{129,385},{257,1},{385... | collective-permute-start | bytes 184328 | tf_op jit(solution)/shard_map/ppermute | solution.py:154
  170.6 3.0 %collective-permute-done.8.h2 = bf16[40,768]{1,0:T(8,128)(2,1)S(1)} collective-permute-done((bf16[40,768]{1,0:T(8,128)(2,1)}, bf16[40,768]{1,0:T(8,128)(2,1)S(1)}, u32[]{:S(2)}, u32[]{:S(2)}) %collective-permute-start.8) | collective-permute-done | bytes 61472 | tf_op jit(solution)/shard_map/ppermute | solution.py:154
  173.6 7.1 %collective-permute-done.9.h3 = bf16[40,768]{1,0:T(8,128)(2,1)S(1)} collective-permute-done((bf16[40,768]{1,0:T(8,128)(2,1)}, bf16[40,768]{1,0:T(8,128)(2,1)S(1)}, u32[]{:S(2)}, u32[]{:S(2)}) %collective-permute-start.9) | collective-permute-done | bytes 61472 | tf_op jit(solution)/shard_map/ppermute | solution.py:154
  181.5 2.5 %shard_map.58 = bf16[16,40,768]{2,1,0:T(8,128)(2,1)S(1)} custom-call(bf16[40,768]{1,0:T(8,128)(2,1)S(1)} %copy-done.4, bf16[40,768]{1,0:T(8,128)(2,1)S(1)} %collective-permute-done.7.h1, bf16[40,768]{1,0:T(8,128)(2,1)S(1)} %collective-permute-done.8.h2, bf16[40,768]{1,0:T(8,128)(2,1)S(1)} %collective-permute-done.9.h3, bf16[768,768]{1,0:T(8,128)(2,1)S(1)} %copy-done, ...), custom_call_target="tpu_custom_call" | custom-call | flops 754974720 | bytes 6291456 | tf_op jit(solution)/shard_map/pallas_call | solution.py:159
  185.0 7.2 %all-to-all-start.3 = ((bf16[16,40,768]{2,1,0:T(8,128)(2,1)}), bf16[16,40,768]{2,1,0:T(8,128)(2,1)S(1)}, u32[]{:S(2)}, u32[]{:S(2)}) async-start(bf16[16,40,768]{2,1,0:T(8,128)(2,1)} %copy-done.2), calls=%async_computation.3 | async-start | bytes 1966080 | tf_op jit(solution)/shard_map/all_to_all | solution.py:161
  195.5 6.5 %all-to-all-done.3 = bf16[16,40,768]{2,1,0:T(8,128)(2,1)S(1)} async-done(((bf16[16,40,768]{2,1,0:T(8,128)(2,1)}), bf16[16,40,768]{2,1,0:T(8,128)(2,1)S(1)}, u32[]{:S(2)}, u32[]{:S(2)}) %all-to-all-start.3) | async-done | bytes 983072 | tf_op jit(solution)/shard_map/all_to_all | solution.py:161
  202.1 4.4 %collective-permute-start.14 = (bf16[40,768]{1,0:T(8,128)(2,1)S(1)}, bf16[40,768]{1,0:T(8,128)(2,1)S(1)}, u32[]{:S(2)}, u32[]{:S(2)}) collective-permute-start(bf16[40,768]{1,0:T(8,128)(2,1)S(1)} %reduce_sum.25), channel_id=1, source_target_pairs={{0,0},{1,1},{2,32},{3,33},{8,64},{9,65},{10,96},{11,97},{32,2},{33... | collective-permute-start | bytes 184328 | tf_op jit(solution)/shard_map/ppermute | solution.py:166
  206.6 9.9 %collective-permute-done.13 = bf16[40,768]{1,0:T(8,128)(2,1)S(1)} collective-permute-done((bf16[40,768]{1,0:T(8,128)(2,1)S(1)}, bf16[40,768]{1,0:T(8,128)(2,1)S(1)}, u32[]{:S(2)}, u32[]{:S(2)}) %collective-permute-start.13) | collective-permute-done | bytes 61472 | tf_op jit(solution)/shard_map/ppermute | solution.py:166
  (51 shorter events, 27.8 us)
Async XLA Ops:
  1.0 31.7 %collective-permute-start.2 = (bf16[256,768]{1,0:T(8,128)(2,1)S(1)}, bf16[256,768]{1,0:T(8,128)(2,1)S(1)}, u32[]{:S(2)}, u32[]{:S(2)}) collective-permute-start(bf16[256,768]{1,0:T(8,128)(2,1)S(1)} %slice.6), channel_id=1, source_target_pairs={{0,64},{64,0},{1,65},{65,1},{2,66},{66,2},{3,67},{67,3},{4,68},{68... | collective-permute-start | bytes 1179656 | tf_op jit(solution)/shard_map/ppermute | solution.py:120
  4.9 18.8 %collective-permute-start = (bf16[40,768]{1,0:T(8,128)(2,1)}, bf16[40,768]{1,0:T(8,128)(2,1)S(1)}, u32[]{:S(2)}, u32[]{:S(2)}) collective-permute-start(bf16[40,768]{1,0:T(8,128)(2,1)} %param.5), channel_id=1, source_target_pairs={{0,0},{1,1},{2,32},{3,33},{8,64},{9,65},{10,96},{11,97},{32,2},{33... | collective-permute-start | bytes 184328 | tf_op jit(solution)/shard_map/ppermute | solution.py:119
  6.8 25.9 %collective-permute-start.1 = (bf16[40,768]{1,0:T(8,128)(2,1)}, bf16[40,768]{1,0:T(8,128)(2,1)S(1)}, u32[]{:S(2)}, u32[]{:S(2)}) collective-permute-start(bf16[40,768]{1,0:T(8,128)(2,1)} %param.5), channel_id=1, source_target_pairs={{0,1},{1,0},{2,33},{3,32},{8,65},{9,64},{10,97},{11,96},{32,3},{33... | collective-permute-start | bytes 184328 | tf_op jit(solution)/shard_map/ppermute | solution.py:119
  32.7 17.7 %copy-start.7 = (bf16[256,768]{1,0:T(8,128)(2,1)}, bf16[256,768]{1,0:T(8,128)(2,1)S(1)}, u32[]{:S(2)}) copy-start(bf16[256,768]{1,0:T(8,128)(2,1)S(1)} %collective-permute-done.2.w10a) | copy-start | bytes 1179652
  34.1 34.9 %all-to-all-start = ((bf16[16,80,768]{2,1,0:T(8,128)(2,1)}), bf16[16,80,768]{2,1,0:T(8,128)(2,1)S(1)}, u32[]{:S(2)}, u32[]{:S(2)}) async-start(bf16[16,80,768]{2,1,0:T(8,128)(2,1)} %broadcast_in_dim.2), calls=%async_computation | async-start | bytes 3932160 | tf_op jit(solution)/shard_map/all_to_all | solution.py:129
  42.0 30.3 %copy-start = (bf16[768,768]{1,0:T(8,128)(2,1)S(1)}, bf16[768,768]{1,0:T(8,128)(2,1)}, u32[]{:S(2)}) copy-start(bf16[768,768]{1,0:T(8,128)(2,1)} %w00.5) | copy-start | bytes 3538948
  42.0 27.1 %collective-permute-start.5 = (bf16[768,768]{1,0:T(8,128)(2,1)}, bf16[768,768]{1,0:T(8,128)(2,1)}, u32[]{:S(2)}, u32[]{:S(2)}) collective-permute-start(bf16[768,768]{1,0:T(8,128)(2,1)} %w00.3), channel_id=1, source_target_pairs={{0,32},{32,0},{1,33},{33,1},{2,34},{34,2},{3,35},{35,3},{4,36},{36... | collective-permute-start | bytes 3538952 | tf_op jit(solution)/shard_map/ppermute | solution.py:124
  45.2 22.9 %collective-permute-start.3 = (bf16[512,768]{1,0:T(8,128)(2,1)S(1)}, bf16[512,768]{1,0:T(8,128)(2,1)S(1)}, u32[]{:S(2)}, u32[]{:S(2)}) collective-permute-start(bf16[512,768]{1,0:T(8,128)(2,1)S(1)} %slice.7), channel_id=1, source_target_pairs={{0,64},{64,0},{1,65},{65,1},{2,66},{66,2},{3,67},{67,3},{4,68},{68... | collective-permute-start | bytes 2359304 | tf_op jit(solution)/shard_map/ppermute | solution.py:123
  50.4 3.6 %collective-permute-start.4 = (bf16[256,768]{1,0:T(8,128)(2,1)S(1)}, bf16[256,768]{1,0:T(8,128)(2,1)S(1)}, u32[]{:S(2)}, u32[]{:S(2)}) collective-permute-start(bf16[256,768]{1,0:T(8,128)(2,1)S(1)} %collective-permute-done.2.w10a), channel_id=1, source_target_pairs={{0,32},{32,0},{1,33},{33,1},{2,34},{34,2},{3,35},{35,3},{4,36},{36... | collective-permute-start | bytes 1179656 | tf_op jit(solution)/shard_map/ppermute | solution.py:125
  54.1 14.1 %copy-start.8 = (bf16[256,768]{1,0:T(8,128)(2,1)}, bf16[256,768]{1,0:T(8,128)(2,1)S(1)}, u32[]{:S(2)}) copy-start(bf16[256,768]{1,0:T(8,128)(2,1)S(1)} %collective-permute-done.4.w11a) | copy-start | bytes 1179652
  70.3 12.9 %collective-permute-start.6 = (bf16[512,768]{1,0:T(8,128)(2,1)}, bf16[512,768]{1,0:T(8,128)(2,1)}, u32[]{:S(2)}, u32[]{:S(2)}) collective-permute-start(bf16[512,768]{1,0:T(8,128)(2,1)} %copy-done.6), channel_id=1, source_target_pairs={{0,32},{32,0},{1,33},{33,1},{2,34},{34,2},{3,35},{35,3},{4,36},{36... | collective-permute-start | bytes 2359304 | tf_op jit(solution)/shard_map/ppermute | solution.py:132
  72.3 40.6 %collective-permute-start.11 = (bf16[768,768]{1,0:T(8,128)(2,1)S(1)}, bf16[768,768]{1,0:T(8,128)(2,1)S(1)}, u32[]{:S(2)}, u32[]{:S(2)}) collective-permute-start(bf16[768,768]{1,0:T(8,128)(2,1)S(1)} %copy-done), channel_id=1, source_target_pairs={{0,64},{64,0},{1,65},{65,1},{2,66},{66,2},{3,67},{67,3},{4,68},{68... | collective-permute-start | bytes 3538952 | tf_op jit(solution)/shard_map/ppermute | solution.py:133
  83.2 31.6 %copy-start.10 = (bf16[768]{0:T(1024)(128)(2,1)S(1)}, bf16[768]{0:T(1024)(128)(2,1)}, u32[]{:S(2)}) copy-start(bf16[768]{0:T(1024)(128)(2,1)} %param.7) | copy-start | bytes 4612
  87.2 27.6 %all-to-all-start.1 = ((bf16[4,80,768]{2,1,0:T(8,128)(2,1)}), bf16[4,80,768]{2,1,0:T(8,128)(2,1)}, u32[]{:S(2)}, u32[]{:S(2)}) async-start(bf16[4,80,768]{2,1,0:T(8,128)(2,1)} %shard_map.56), calls=%async_computation.1 | async-start | bytes 983040 | tf_op jit(solution)/shard_map/all_to_all | solution.py:146
  91.3 52.4 %collective-permute-start.10 = (bf16[768,768]{1,0:T(8,128)(2,1)S(1)}, bf16[768,768]{1,0:T(8,128)(2,1)S(1)}, u32[]{:S(2)}, u32[]{:S(2)}) collective-permute-start(bf16[768,768]{1,0:T(8,128)(2,1)S(1)} %copy-done), channel_id=1, source_target_pairs={{0,32},{32,0},{1,33},{33,1},{2,34},{34,2},{3,35},{35,3},{4,36},{36... | collective-permute-start | bytes 3538952 | tf_op jit(solution)/shard_map/ppermute | solution.py:144
  112.9 30.9 %collective-permute-start.12 = (bf16[768,768]{1,0:T(8,128)(2,1)S(1)}, bf16[768,768]{1,0:T(8,128)(2,1)}, u32[]{:S(2)}, u32[]{:S(2)}) collective-permute-start(bf16[768,768]{1,0:T(8,128)(2,1)S(1)} %collective-permute-done.11.w10), channel_id=1, source_target_pairs={{0,32},{32,0},{1,33},{33,1},{2,34},{34,2},{3,35},{35,3},{4,36},{36... | collective-permute-start | bytes 3538952 | tf_op jit(solution)/shard_map/ppermute | solution.py:144
  147.2 37.7 %all-to-all-start.2 = ((bf16[16,40,768]{2,1,0:T(8,128)(2,1)}), bf16[16,40,768]{2,1,0:T(8,128)(2,1)}, u32[]{:S(2)}, u32[]{:S(2)}) async-start(bf16[16,40,768]{2,1,0:T(8,128)(2,1)} %copy-done.1), calls=%async_computation.2 | async-start | bytes 1966080 | tf_op jit(solution)/shard_map/all_to_all | solution.py:157
  156.2 14.3 %collective-permute-start.7 = (bf16[40,768]{1,0:T(8,128)(2,1)}, bf16[40,768]{1,0:T(8,128)(2,1)S(1)}, u32[]{:S(2)}, u32[]{:S(2)}) collective-permute-start(bf16[40,768]{1,0:T(8,128)(2,1)} %copy-done.3), channel_id=1, source_target_pairs={{0,128},{128,0},{256,384},{384,256},{1,129},{129,1},{257,385},{385... | collective-permute-start | bytes 184328 | tf_op jit(solution)/shard_map/ppermute | solution.py:154
  161.3 12.3 %collective-permute-start.8 = (bf16[40,768]{1,0:T(8,128)(2,1)}, bf16[40,768]{1,0:T(8,128)(2,1)S(1)}, u32[]{:S(2)}, u32[]{:S(2)}) collective-permute-start(bf16[40,768]{1,0:T(8,128)(2,1)} %copy-done.3), channel_id=1, source_target_pairs={{0,256},{128,384},{256,0},{384,128},{1,257},{129,385},{257,1},{385... | collective-permute-start | bytes 184328 | tf_op jit(solution)/shard_map/ppermute | solution.py:154
  168.6 12.0 %collective-permute-start.9 = (bf16[40,768]{1,0:T(8,128)(2,1)}, bf16[40,768]{1,0:T(8,128)(2,1)S(1)}, u32[]{:S(2)}, u32[]{:S(2)}) collective-permute-start(bf16[40,768]{1,0:T(8,128)(2,1)} %copy-done.3), channel_id=1, source_target_pairs={{0,384},{128,256},{256,128},{384,0},{1,385},{129,257},{257,129},{3... | collective-permute-start | bytes 184328 | tf_op jit(solution)/shard_map/ppermute | solution.py:154
  185.0 17.0 %all-to-all-start.3 = ((bf16[16,40,768]{2,1,0:T(8,128)(2,1)}), bf16[16,40,768]{2,1,0:T(8,128)(2,1)S(1)}, u32[]{:S(2)}, u32[]{:S(2)}) async-start(bf16[16,40,768]{2,1,0:T(8,128)(2,1)} %copy-done.2), calls=%async_computation.3 | async-start | bytes 1966080 | tf_op jit(solution)/shard_map/all_to_all | solution.py:161
  192.2 14.3 %copy-start.9 = (bf16[768]{0:T(1024)(128)(2,1)S(1)}, bf16[768]{0:T(1024)(128)(2,1)}, u32[]{:S(2)}) copy-start(bf16[768]{0:T(1024)(128)(2,1)} %param.9) | copy-start | bytes 4612
  193.6 22.9 %collective-permute-start.13 = (bf16[40,768]{1,0:T(8,128)(2,1)S(1)}, bf16[40,768]{1,0:T(8,128)(2,1)S(1)}, u32[]{:S(2)}, u32[]{:S(2)}) collective-permute-start(bf16[40,768]{1,0:T(8,128)(2,1)S(1)} %reduce_sum.24), channel_id=1, source_target_pairs={{0,1},{1,0},{2,33},{3,32},{8,65},{9,64},{10,97},{11,96},{32,3},{33... | collective-permute-start | bytes 184328 | tf_op jit(solution)/shard_map/ppermute | solution.py:166
  202.1 14.4 %collective-permute-start.14 = (bf16[40,768]{1,0:T(8,128)(2,1)S(1)}, bf16[40,768]{1,0:T(8,128)(2,1)S(1)}, u32[]{:S(2)}, u32[]{:S(2)}) collective-permute-start(bf16[40,768]{1,0:T(8,128)(2,1)S(1)} %reduce_sum.25), channel_id=1, source_target_pairs={{0,0},{1,1},{2,32},{3,33},{8,64},{9,65},{10,96},{11,97},{32,2},{33... | collective-permute-start | bytes 184328 | tf_op jit(solution)/shard_map/ppermute | solution.py:166
  (6 other events, 5.6 us)

commit v5 on v3

v5 whole, which is shorter than its diff:
```python
import jax
import jax.numpy as jnp
from jax import lax
from jax.experimental import pallas as pl
from jax.experimental.pallas import tpu as pltpu
from jax.sharding import Mesh
from jax.sharding import PartitionSpec as P

ROW = ("zq", "zb", "c")
COL = ("yp", "y0", "xp", "x0", "zh")
SIZES = (4, 2, 2, 2, 2, 2, 2, 2)
PLANE = ("yp", "y0", "xp", "x0")
CORNER = ("zb", "c", "y0", "x0", "zh")
SWAP = [(0, 1), (1, 0)]
VMEM = pl.BlockSpec(memory_space=pltpu.VMEM)
ANY = pl.BlockSpec(memory_space=pl.ANY)

F32 = jnp.float32
BF16 = jnp.bfloat16
barrier = lax.optimization_barrier


def corner_pairs(other_zh):
    return [(i, ((i >> 1) & 3) << 3 | (i >> 3) << 1 | ((i & 1) ^ other_zh)) for i in range(32)]


def slot(block, dz, dc):
    y0 = jnp.bitwise_xor(lax.axis_index("zb"), dz)
    x0 = jnp.bitwise_xor(lax.axis_index("c"), dc)
    return (block & 2) * 4 + y0 * 4 + (block & 1) * 2 + x0


def kernel_call(kernel, shape, specs, out_spec, cost, scratch=(), limit=16):
    flops, nbytes = cost
    return pl.pallas_call(
        kernel,
        out_shape=jax.ShapeDtypeStruct(shape, BF16),
        in_specs=specs,
        out_specs=out_spec,
        scratch_shapes=scratch,
        compiler_params=pltpu.CompilerParams(vmem_limit_bytes=limit << 20),
        cost_estimate=pl.CostEstimate(flops=flops, bytes_accessed=nbytes, transcendentals=0),
    )


def start_all(pairs, sems):
    copies = [pltpu.make_async_copy(src, dst, sems.at[i]) for i, (src, dst) in enumerate(pairs)]
    for copy in copies:
        copy.start()
    return copies


def spread_kernel(here, other, out, block, sems):
    block[:40] = here[...]
    block[40:] = other[...]
    for copy in start_all([(block, out.at[i]) for i in range(16)], sems):
        copy.wait()


def first_kernel(got, w00, w01, w10, w11, part, total, held, sems):
    copies = start_all([(w00, held.at[0]), (w01, held.at[1])], sems)
    for i, k in enumerate((2, 3, 0, 1)):
        left = jnp.concatenate([got[slot(b, k // 2, k % 2)] for b in range(4)], axis=0)
        if k < 2:
            copies[k].wait()
        right = (w10[...], w11[...])[i] if k > 1 else held[k]
        product = jnp.dot(left, right, preferred_element_type=F32)
        if i < 3:
            total[...] = product if i == 0 else total[...] + product
        else:
            part[...] = (total[...] + product).astype(BF16).reshape(4, 80, 768)


def middle_kernel(parts, bias, h):
    preact = bias[...].astype(F32)
    for k in range(4):
        preact = preact + parts[k].astype(F32)
    h[...] = jax.nn.gelu(preact, approximate=True).astype(BF16)


def second_kernel(h0, h1, h2, h3, w00, w01, w10, w11, out, held, sems):
    copies = start_all([(w00, held.at[0]), (w01, held.at[1])], sems)
    zq = lax.axis_index("zq")
    left = jnp.concatenate([h[...] for h in (h0, h1, h2, h3)], axis=0)
    for i, k in enumerate((2, 3, 0, 1)):
        if k < 2:
            copies[k].wait()
        right = (w10[...], w11[...])[i] if k > 1 else held[k]
        product = jnp.dot(left, right, preferred_element_type=F32)
        for j in range(4):
            rows = product[j * 80 : (j + 1) * 80]
            out[slot(jnp.bitwise_xor(zq, j), k // 2, k % 2)] = rows.astype(BF16)


def shards(tokens, w1, b1, w2, b2):
    here, other = (lax.ppermute(tokens, CORNER, corner_pairs(k)) for k in range(2))
    w1_in, here = barrier((w1, here))
    w2_in, here = barrier((w2, here))

    def weights(w):
        w_z = lax.ppermute(w, "zb", SWAP)
        return [w, lax.ppermute(w, "c", SWAP), w_z, lax.ppermute(w_z, "c", SWAP)]

    w1_all = weights(w1_in)
    w2_all = weights(w2_in)

    scratch = [pltpu.VMEM((80, 768), BF16), pltpu.SemaphoreType.DMA((16,))]
    spread = kernel_call(spread_kernel, (16, 80, 768), [VMEM] * 2, ANY, (5 * 10**9, 4 << 20), scratch)(here, other)
    got = lax.all_to_all(spread, PLANE, 0, 0, tiled=True)

    held = [pltpu.VMEM((2, 768, 768), BF16), pltpu.SemaphoreType.DMA((2,))]
    weight_specs = [ANY, ANY, VMEM, VMEM]
    cost = (2 * 320 * 3072 * 768, 8 << 20)
    scratch = [pltpu.VMEM((320, 768), F32)] + held
    first = kernel_call(first_kernel, (4, 80, 768), [VMEM] + weight_specs, VMEM, cost, scratch, 54)
    part = lax.all_to_all(first(got, *w1_all), "zq", 0, 0, tiled=True)
    middle = kernel_call(middle_kernel, (80, 768), [VMEM] * 2, VMEM, (20 * 80 * 768, 1 << 20))
    h = middle(part, b1.reshape(1, 768))
    rows = [h] + [lax.ppermute(h, "zq", [(i, i ^ k) for i in range(4)]) for k in range(1, 4)]
    second = kernel_call(second_kernel, (16, 80, 768), [VMEM] * 4 + weight_specs, VMEM, cost, held, 50)
    out = lax.all_to_all(second(*rows, *w2_all), PLANE, 0, 0, tiled=True)
    out = out.astype(F32).sum(axis=0).astype(BF16)

    back = [lax.ppermute(out[k * 40 : (k + 1) * 40], CORNER, corner_pairs(k)) for k in range(2)]
    return (back[0].astype(F32) + back[1].astype(F32) + b2.astype(F32)).astype(BF16)


def solution(mesh):
    fine = Mesh(mesh.devices.reshape(SIZES), ROW + COL)
    in_specs = (P(COL, ROW), P(ROW, COL), P(COL), P(COL, ROW), P(ROW))
    return jax.shard_map(shards, mesh=fine, in_specs=in_specs, out_specs=P(COL, ROW), check_vma=False)
```

time: 190 us -> 192 us (1.011)
  the two profiles are of different devices: /device:TPU:32 before, /device:TPU:88 now
where the time goes in v5:
time: 192 us; the launch traced here: 191 us
  waiting for transfers between devices  73.5 us (38%)
  starting transfers between devices  72.3 us (38%)
  blocking collectives  31.6 us (16%)
  Pallas kernels  12.7 us (7%)
    ppermute x2, waiting for transfers between devices, weights(): w_z = lax.ppermute(w, 'zb', SWAP)  33.9 us
    all_to_all x1, blocking collectives, shards(): out = lax.all_to_all(second(*rows, *w2_all), PLANE, 0, 0, tiled=True)  31.6 us
    ppermute x3, waiting for transfers between devices, shards(): lax.ppermute(h, 'zq', [(i, i ^ k) for i in range(4)])  19.3 us
    ppermute x2, starting transfers between devices, shards(): lax.ppermute(tokens, CORNER, corner_pairs(k))  17.3 us
    all_to_all x1, starting transfers between devices, shards(): part = lax.all_to_all(first(got, *w1_all), 'zq', 0, 0, tiled=True)  13.5 us
    ppermute x3, starting transfers between devices, shards(): lax.ppermute(h, 'zq', [(i, i ^ k) for i in range(4)])  12.7 us
    ppermute x2, starting transfers between devices, shards(): lax.ppermute(out[k * 40:(k + 1) * 40], CORNER, corner_pairs(k))  10.2 us
    ppermute x2, waiting for transfers between devices, shards(): lax.ppermute(out[k * 40:(k + 1) * 40], CORNER, corner_pairs(k))  9.44 us
  transfers between devices with their start and end apart: 15, of which 8 were waited for; matrix products, arithmetic and copies ran while one was open for 0% of the time, Pallas kernels for 4%

profile of v5, /device:TPU:88, one launch (start us, length us, event | category | flops | bytes accessed | tf_op | source)
XLA Modules:
  0.0 191.3 jit_solution(1208436434655107266)
XLA Ops:
  0.0 4.0 %collective-permute-start = (bf16[40,768]{1,0:T(8,128)(2,1)}, bf16[40,768]{1,0:T(8,128)(2,1)S(1)}, u32[]{:S(2)}, u32[]{:S(2)}) collective-permute-start(bf16[40,768]{1,0:T(8,128)(2,1)} %param.5), channel_id=1, source_target_pairs={{0,0},{1,1},{2,32},{3,33},{8,64},{9,65},{10,96},{11,97},{32,2},{33... | collective-permute-start | bytes 184328 | tf_op jit(solution)/shard_map/ppermute | solution.py:96
  4.0 13.3 %collective-permute-start.1 = (bf16[40,768]{1,0:T(8,128)(2,1)}, bf16[40,768]{1,0:T(8,128)(2,1)S(1)}, u32[]{:S(2)}, u32[]{:S(2)}) collective-permute-start(bf16[40,768]{1,0:T(8,128)(2,1)} %param.5), channel_id=1, source_target_pairs={{0,1},{1,0},{2,33},{3,32},{8,65},{9,64},{10,97},{11,96},{32,3},{33... | collective-permute-start | bytes 184328 | tf_op jit(solution)/shard_map/ppermute | solution.py:96
  17.3 1.9 %collective-permute-start.3 = (bf16[768,768]{1,0:T(8,128)(2,1)}, bf16[768,768]{1,0:T(8,128)(2,1)}, u32[]{:S(2)}, u32[]{:S(2)}) collective-permute-start(bf16[768,768]{1,0:T(8,128)(2,1)} %w00), channel_id=1, source_target_pairs={{0,64},{64,0},{1,65},{65,1},{2,66},{66,2},{3,67},{67,3},{4,68},{68... | collective-permute-start | bytes 3538952 | tf_op jit(solution)/shard_map/ppermute | solution.py:101
  19.2 7.9 %collective-permute-done.1.other = bf16[40,768]{1,0:T(8,128)(2,1)S(1)} collective-permute-done((bf16[40,768]{1,0:T(8,128)(2,1)}, bf16[40,768]{1,0:T(8,128)(2,1)S(1)}, u32[]{:S(2)}, u32[]{:S(2)}) %collective-permute-start.1) | collective-permute-done | bytes 61472 | tf_op jit(solution)/shard_map/ppermute | solution.py:96
  28.6 7.1 %all-to-all-start = ((bf16[16,80,768]{2,1,0:T(8,128)(2,1)}), bf16[16,80,768]{2,1,0:T(8,128)(2,1)}, u32[]{:S(2)}, u32[]{:S(2)}) async-start(bf16[16,80,768]{2,1,0:T(8,128)(2,1)} %shard_map.55), calls=%async_computation | async-start | bytes 3932160 | tf_op jit(solution)/shard_map/all_to_all | solution.py:109
  35.7 1.9 %collective-permute-start.2 = (bf16[768,768]{1,0:T(8,128)(2,1)S(1)}, bf16[768,768]{1,0:T(8,128)(2,1)}, u32[]{:S(2)}, u32[]{:S(2)}) collective-permute-start(bf16[768,768]{1,0:T(8,128)(2,1)S(1)} %copy-done.1), channel_id=1, source_target_pairs={{0,32},{32,0},{1,33},{33,1},{2,34},{34,2},{3,35},{35,3},{4,36},{36... | collective-permute-start | bytes 3538952 | tf_op jit(solution)/shard_map/ppermute | solution.py:102
  37.6 15.2 %collective-permute-done.3.w10 = bf16[768,768]{1,0:T(8,128)(2,1)} collective-permute-done((bf16[768,768]{1,0:T(8,128)(2,1)}, bf16[768,768]{1,0:T(8,128)(2,1)}, u32[]{:S(2)}, u32[]{:S(2)}) %collective-permute-start.3) | collective-permute-done | bytes 1179680 | tf_op jit(solution)/shard_map/ppermute | solution.py:101
  52.8 2.0 %collective-permute-start.4 = (bf16[768,768]{1,0:T(8,128)(2,1)}, bf16[768,768]{1,0:T(8,128)(2,1)}, u32[]{:S(2)}, u32[]{:S(2)}) collective-permute-start(bf16[768,768]{1,0:T(8,128)(2,1)} %collective-permute-done.3.w10), channel_id=1, source_target_pairs={{0,32},{32,0},{1,33},{33,1},{2,34},{34,2},{3,35},{35,3},{4,36},{36... | collective-permute-start | bytes 3538952 | tf_op jit(solution)/shard_map/ppermute | solution.py:102
  54.8 1.9 %collective-permute-start.9 = (bf16[768,768]{1,0:T(8,128)(2,1)S(1)}, bf16[768,768]{1,0:T(8,128)(2,1)S(1)}, u32[]{:S(2)}, u32[]{:S(2)}) collective-permute-start(bf16[768,768]{1,0:T(8,128)(2,1)S(1)} %copy-done), channel_id=1, source_target_pairs={{0,64},{64,0},{1,65},{65,1},{2,66},{66,2},{3,67},{67,3},{4,68},{68... | collective-permute-start | bytes 3538952 | tf_op jit(solution)/shard_map/ppermute | solution.py:101
  56.8 2.2 %all-to-all-done.got = bf16[16,80,768]{2,1,0:T(8,128)(2,1)} async-done(((bf16[16,80,768]{2,1,0:T(8,128)(2,1)}), bf16[16,80,768]{2,1,0:T(8,128)(2,1)}, u32[]{:S(2)}, u32[]{:S(2)}) %all-to-all-start) | async-done | bytes 1966112 | tf_op jit(solution)/shard_map/all_to_all | solution.py:109
  59.0 5.6 %shard_map.56 = bf16[4,80,768]{2,1,0:T(8,128)(2,1)} custom-call(bf16[16,80,768]{2,1,0:T(8,128)(2,1)} %all-to-all-done.got, bf16[768,768]{1,0:T(8,128)(2,1)} %w00, bf16[768,768]{1,0:T(8,128)(2,1)} %collective-permute-done.2.w01, bf16[768,768]{1,0:T(8,128)(2,1)} %collective-permute-done.3.w10, bf16[768,768]{1,0:T(8,128)(2,1)} %collective-permute-done.4.w11), custom_call_target="tpu_custom_call" | custom-call | flops 1509949440 | bytes 8388608 | tf_op jit(solution)/shard_map/pallas_call | solution.py:116
  64.6 13.5 %all-to-all-start.1 = ((bf16[4,80,768]{2,1,0:T(8,128)(2,1)}), bf16[4,80,768]{2,1,0:T(8,128)(2,1)S(1)}, u32[]{:S(2)}, u32[]{:S(2)}) async-start(bf16[4,80,768]{2,1,0:T(8,128)(2,1)} %shard_map.56), calls=%async_computation.1 | async-start | bytes 983040 | tf_op jit(solution)/shard_map/all_to_all | solution.py:116
  80.0 18.6 %collective-permute-done.9.w10 = bf16[768,768]{1,0:T(8,128)(2,1)S(1)} collective-permute-done((bf16[768,768]{1,0:T(8,128)(2,1)S(1)}, bf16[768,768]{1,0:T(8,128)(2,1)S(1)}, u32[]{:S(2)}, u32[]{:S(2)}) %collective-permute-start.9) | collective-permute-done | bytes 1179680 | tf_op jit(solution)/shard_map/ppermute | solution.py:101
  98.7 1.9 collective-permute-start.10
  101.5 1.9 %collective-permute-start.5 = (bf16[80,768]{1,0:T(8,128)(2,1)S(1)}, bf16[80,768]{1,0:T(8,128)(2,1)S(1)}, u32[]{:S(2)}, u32[]{:S(2)}) collective-permute-start(bf16[80,768]{1,0:T(8,128)(2,1)S(1)} %shard_map.57.h0), channel_id=1, source_target_pairs={{0,128},{128,0},{256,384},{384,256},{1,129},{129,1},{257,385},{385... | collective-permute-start | bytes 368648 | tf_op jit(solution)/shard_map/ppermute | solution.py:119
  103.5 8.3 %collective-permute-start.6 = (bf16[80,768]{1,0:T(8,128)(2,1)S(1)}, bf16[80,768]{1,0:T(8,128)(2,1)S(1)}, u32[]{:S(2)}, u32[]{:S(2)}) collective-permute-start(bf16[80,768]{1,0:T(8,128)(2,1)S(1)} %shard_map.57.h0), channel_id=1, source_target_pairs={{0,256},{128,384},{256,0},{384,128},{1,257},{129,385},{257,1},{385... | collective-permute-start | bytes 368648 | tf_op jit(solution)/shard_map/ppermute | solution.py:119
  111.8 2.5 %collective-permute-start.7 = (bf16[80,768]{1,0:T(8,128)(2,1)S(1)}, bf16[80,768]{1,0:T(8,128)(2,1)S(1)}, u32[]{:S(2)}, u32[]{:S(2)}) collective-permute-start(bf16[80,768]{1,0:T(8,128)(2,1)S(1)} %shard_map.57.h0), channel_id=1, source_target_pairs={{0,384},{128,256},{256,128},{384,0},{1,385},{129,257},{257,129},{3... | collective-permute-start | bytes 368648 | tf_op jit(solution)/shard_map/ppermute | solution.py:119
  114.3 10.1 %collective-permute-done.6.h2 = bf16[80,768]{1,0:T(8,128)(2,1)S(1)} collective-permute-done((bf16[80,768]{1,0:T(8,128)(2,1)S(1)}, bf16[80,768]{1,0:T(8,128)(2,1)S(1)}, u32[]{:S(2)}, u32[]{:S(2)}) %collective-permute-start.6) | collective-permute-done | bytes 122912 | tf_op jit(solution)/shard_map/ppermute | solution.py:119
  124.4 9.2 %collective-permute-done.7.h3 = bf16[80,768]{1,0:T(8,128)(2,1)S(1)} collective-permute-done((bf16[80,768]{1,0:T(8,128)(2,1)S(1)}, bf16[80,768]{1,0:T(8,128)(2,1)S(1)}, u32[]{:S(2)}, u32[]{:S(2)}) %collective-permute-start.7) | collective-permute-done | bytes 122912 | tf_op jit(solution)/shard_map/ppermute | solution.py:119
  133.6 5.5 %shard_map.58 = bf16[16,80,768]{2,1,0:T(8,128)(2,1)} custom-call(bf16[80,768]{1,0:T(8,128)(2,1)S(1)} %shard_map.57.h0, bf16[80,768]{1,0:T(8,128)(2,1)S(1)} %collective-permute-done.5.h1, bf16[80,768]{1,0:T(8,128)(2,1)S(1)} %collective-permute-done.6.h2, bf16[80,768]{1,0:T(8,128)(2,1)S(1)} %collective-permute-done.7.h3, bf16[768,768]{1,0:T(8,128)(2,1)S(1)} %copy-done, ...), custom_call_target="tpu_custom_call" | custom-call | flops 1509949440 | bytes 8388608 | tf_op jit(solution)/shard_map/pallas_call | solution.py:121
  139.1 31.6 %all_to_all.15 = bf16[16,80,768]{2,1,0:T(8,128)(2,1)S(1)} all-to-all(bf16[16,80,768]{2,1,0:T(8,128)(2,1)} %shard_map.58), channel_id=1, replica_groups=mesh['zq'=4,'zb'=2,'c'=2,'yp'=2,'y0'=2,'xp'=2,'x0'=2,'zh'=2] {'yp','y0',..., dimensions={0} | all-to-all | bytes 3932160 | tf_op jit(solution)/shard_map/all_to_all | solution.py:121
  171.0 2.5 %collective-permute-start.12 = (bf16[40,768]{1,0:T(8,128)(2,1)S(1)}, bf16[40,768]{1,0:T(8,128)(2,1)S(1)}, u32[]{:S(2)}, u32[]{:S(2)}) collective-permute-start(bf16[40,768]{1,0:T(8,128)(2,1)S(1)} %get-tuple-element.14), channel_id=1, source_target_pairs={{0,1},{1,0},{2,33},{3,32},{8,65},{9,64},{10,97},{11,96},{32,3},{33... | collective-permute-start | bytes 184328 | tf_op jit(solution)/shard_map/ppermute | solution.py:124
  173.5 7.7 %collective-permute-start.11 = (bf16[40,768]{1,0:T(8,128)(2,1)S(1)}, bf16[40,768]{1,0:T(8,128)(2,1)S(1)}, u32[]{:S(2)}, u32[]{:S(2)}) collective-permute-start(bf16[40,768]{1,0:T(8,128)(2,1)S(1)} %get-tuple-element.13), channel_id=1, source_target_pairs={{0,0},{1,1},{2,32},{3,33},{8,64},{9,65},{10,96},{11,97},{32,2},{33... | collective-permute-start | bytes 184328 | tf_op jit(solution)/shard_map/ppermute | solution.py:124
  181.2 9.4 %collective-permute-done.12 = bf16[40,768]{1,0:T(8,128)(2,1)S(1)} collective-permute-done((bf16[40,768]{1,0:T(8,128)(2,1)S(1)}, bf16[40,768]{1,0:T(8,128)(2,1)S(1)}, u32[]{:S(2)}, u32[]{:S(2)}) %collective-permute-start.12) | collective-permute-done | bytes 61472 | tf_op jit(solution)/shard_map/ppermute | solution.py:124
  (24 shorter events, 5.3 us)
Async XLA Ops:
  0.0 17.3 %collective-permute-start = (bf16[40,768]{1,0:T(8,128)(2,1)}, bf16[40,768]{1,0:T(8,128)(2,1)S(1)}, u32[]{:S(2)}, u32[]{:S(2)}) collective-permute-start(bf16[40,768]{1,0:T(8,128)(2,1)} %param.5), channel_id=1, source_target_pairs={{0,0},{1,1},{2,32},{3,33},{8,64},{9,65},{10,96},{11,97},{32,2},{33... | collective-permute-start | bytes 184328 | tf_op jit(solution)/shard_map/ppermute | solution.py:96
  4.0 23.1 %collective-permute-start.1 = (bf16[40,768]{1,0:T(8,128)(2,1)}, bf16[40,768]{1,0:T(8,128)(2,1)S(1)}, u32[]{:S(2)}, u32[]{:S(2)}) collective-permute-start(bf16[40,768]{1,0:T(8,128)(2,1)} %param.5), channel_id=1, source_target_pairs={{0,1},{1,0},{2,33},{3,32},{8,65},{9,64},{10,97},{11,96},{32,3},{33... | collective-permute-start | bytes 184328 | tf_op jit(solution)/shard_map/ppermute | solution.py:96
  17.3 35.5 %collective-permute-start.3 = (bf16[768,768]{1,0:T(8,128)(2,1)}, bf16[768,768]{1,0:T(8,128)(2,1)}, u32[]{:S(2)}, u32[]{:S(2)}) collective-permute-start(bf16[768,768]{1,0:T(8,128)(2,1)} %w00), channel_id=1, source_target_pairs={{0,64},{64,0},{1,65},{65,1},{2,66},{66,2},{3,67},{67,3},{4,68},{68... | collective-permute-start | bytes 3538952 | tf_op jit(solution)/shard_map/ppermute | solution.py:101
  28.6 7.1 %copy-start.1 = (bf16[768,768]{1,0:T(8,128)(2,1)S(1)}, bf16[768,768]{1,0:T(8,128)(2,1)}, u32[]{:S(2)}) copy-start(bf16[768,768]{1,0:T(8,128)(2,1)} %w00) | copy-start | bytes 3538948
  28.6 26.3 %copy-start = (bf16[768,768]{1,0:T(8,128)(2,1)S(1)}, bf16[768,768]{1,0:T(8,128)(2,1)}, u32[]{:S(2)}) copy-start(bf16[768,768]{1,0:T(8,128)(2,1)} %w00.1) | copy-start | bytes 3538948
  28.6 30.4 %all-to-all-start = ((bf16[16,80,768]{2,1,0:T(8,128)(2,1)}), bf16[16,80,768]{2,1,0:T(8,128)(2,1)}, u32[]{:S(2)}, u32[]{:S(2)}) async-start(bf16[16,80,768]{2,1,0:T(8,128)(2,1)} %shard_map.55), calls=%async_computation | async-start | bytes 3932160 | tf_op jit(solution)/shard_map/all_to_all | solution.py:109
  35.7 64.9 %copy-start.3 = (bf16[768]{0:T(1024)(128)(2,1)S(1)}, bf16[768]{0:T(1024)(128)(2,1)}, u32[]{:S(2)}) copy-start(bf16[768]{0:T(1024)(128)(2,1)} %param.7) | copy-start | bytes 4612
  35.7 21.1 %collective-permute-start.2 = (bf16[768,768]{1,0:T(8,128)(2,1)S(1)}, bf16[768,768]{1,0:T(8,128)(2,1)}, u32[]{:S(2)}, u32[]{:S(2)}) collective-permute-start(bf16[768,768]{1,0:T(8,128)(2,1)S(1)} %copy-done.1), channel_id=1, source_target_pairs={{0,32},{32,0},{1,33},{33,1},{2,34},{34,2},{3,35},{35,3},{4,36},{36... | collective-permute-start | bytes 3538952 | tf_op jit(solution)/shard_map/ppermute | solution.py:102
  52.8 6.1 %collective-permute-start.4 = (bf16[768,768]{1,0:T(8,128)(2,1)}, bf16[768,768]{1,0:T(8,128)(2,1)}, u32[]{:S(2)}, u32[]{:S(2)}) collective-permute-start(bf16[768,768]{1,0:T(8,128)(2,1)} %collective-permute-done.3.w10), channel_id=1, source_target_pairs={{0,32},{32,0},{1,33},{33,1},{2,34},{34,2},{3,35},{35,3},{4,36},{36... | collective-permute-start | bytes 3538952 | tf_op jit(solution)/shard_map/ppermute | solution.py:102
  54.8 43.8 %collective-permute-start.9 = (bf16[768,768]{1,0:T(8,128)(2,1)S(1)}, bf16[768,768]{1,0:T(8,128)(2,1)S(1)}, u32[]{:S(2)}, u32[]{:S(2)}) collective-permute-start(bf16[768,768]{1,0:T(8,128)(2,1)S(1)} %copy-done), channel_id=1, source_target_pairs={{0,64},{64,0},{1,65},{65,1},{2,66},{66,2},{3,67},{67,3},{4,68},{68... | collective-permute-start | bytes 3538952 | tf_op jit(solution)/shard_map/ppermute | solution.py:101
  64.6 36.8 %all-to-all-start.1 = ((bf16[4,80,768]{2,1,0:T(8,128)(2,1)}), bf16[4,80,768]{2,1,0:T(8,128)(2,1)S(1)}, u32[]{:S(2)}, u32[]{:S(2)}) async-start(bf16[4,80,768]{2,1,0:T(8,128)(2,1)} %shard_map.56), calls=%async_computation.1 | async-start | bytes 983040 | tf_op jit(solution)/shard_map/all_to_all | solution.py:116
  78.1 36.1 %collective-permute-start.8 = (bf16[768,768]{1,0:T(8,128)(2,1)S(1)}, bf16[768,768]{1,0:T(8,128)(2,1)}, u32[]{:S(2)}, u32[]{:S(2)}) collective-permute-start(bf16[768,768]{1,0:T(8,128)(2,1)S(1)} %copy-done), channel_id=1, source_target_pairs={{0,32},{32,0},{1,33},{33,1},{2,34},{34,2},{3,35},{35,3},{4,36},{36... | collective-permute-start | bytes 3538952 | tf_op jit(solution)/shard_map/ppermute | solution.py:102
  98.7 15.6 %collective-permute-start.10 = (bf16[768,768]{1,0:T(8,128)(2,1)S(1)}, bf16[768,768]{1,0:T(8,128)(2,1)}, u32[]{:S(2)}, u32[]{:S(2)}) collective-permute-start(bf16[768,768]{1,0:T(8,128)(2,1)S(1)} %collective-permute-done.9.w10), channel_id=1, source_target_pairs={{0,32},{32,0},{1,33},{33,1},{2,34},{34,2},{3,35},{35,3},{4,36},{36... | collective-permute-start | bytes 3538952 | tf_op jit(solution)/shard_map/ppermute | solution.py:102
  101.5 12.7 %collective-permute-start.5 = (bf16[80,768]{1,0:T(8,128)(2,1)S(1)}, bf16[80,768]{1,0:T(8,128)(2,1)S(1)}, u32[]{:S(2)}, u32[]{:S(2)}) collective-permute-start(bf16[80,768]{1,0:T(8,128)(2,1)S(1)} %shard_map.57.h0), channel_id=1, source_target_pairs={{0,128},{128,0},{256,384},{384,256},{1,129},{129,1},{257,385},{385... | collective-permute-start | bytes 368648 | tf_op jit(solution)/shard_map/ppermute | solution.py:119
  103.5 20.9 %collective-permute-start.6 = (bf16[80,768]{1,0:T(8,128)(2,1)S(1)}, bf16[80,768]{1,0:T(8,128)(2,1)S(1)}, u32[]{:S(2)}, u32[]{:S(2)}) collective-permute-start(bf16[80,768]{1,0:T(8,128)(2,1)S(1)} %shard_map.57.h0), channel_id=1, source_target_pairs={{0,256},{128,384},{256,0},{384,128},{1,257},{129,385},{257,1},{385... | collective-permute-start | bytes 368648 | tf_op jit(solution)/shard_map/ppermute | solution.py:119
  111.8 21.8 %collective-permute-start.7 = (bf16[80,768]{1,0:T(8,128)(2,1)S(1)}, bf16[80,768]{1,0:T(8,128)(2,1)S(1)}, u32[]{:S(2)}, u32[]{:S(2)}) collective-permute-start(bf16[80,768]{1,0:T(8,128)(2,1)S(1)} %shard_map.57.h0), channel_id=1, source_target_pairs={{0,384},{128,256},{256,128},{384,0},{1,385},{129,257},{257,129},{3... | collective-permute-start | bytes 368648 | tf_op jit(solution)/shard_map/ppermute | solution.py:119
  170.7 10.5 %copy-start.2 = (bf16[768]{0:T(1024)(128)(2,1)S(1)}, bf16[768]{0:T(1024)(128)(2,1)}, u32[]{:S(2)}) copy-start(bf16[768]{0:T(1024)(128)(2,1)} %param.9) | copy-start | bytes 4612
  171.0 19.6 %collective-permute-start.12 = (bf16[40,768]{1,0:T(8,128)(2,1)S(1)}, bf16[40,768]{1,0:T(8,128)(2,1)S(1)}, u32[]{:S(2)}, u32[]{:S(2)}) collective-permute-start(bf16[40,768]{1,0:T(8,128)(2,1)S(1)} %get-tuple-element.14), channel_id=1, source_target_pairs={{0,1},{1,0},{2,33},{3,32},{8,65},{9,64},{10,97},{11,96},{32,3},{33... | collective-permute-start | bytes 184328 | tf_op jit(solution)/shard_map/ppermute | solution.py:124
  173.5 17.1 %collective-permute-start.11 = (bf16[40,768]{1,0:T(8,128)(2,1)S(1)}, bf16[40,768]{1,0:T(8,128)(2,1)S(1)}, u32[]{:S(2)}, u32[]{:S(2)}) collective-permute-start(bf16[40,768]{1,0:T(8,128)(2,1)S(1)} %get-tuple-element.13), channel_id=1, source_target_pairs={{0,0},{1,1},{2,32},{3,33},{8,64},{9,65},{10,96},{11,97},{32,2},{33... | collective-permute-start | bytes 184328 | tf_op jit(solution)/shard_map/ppermute | solution.py:124

commit v6 on v3

--- a/solution.py
+++ b/solution.py
@@ -29,14 +29,14 @@
     return (block & 2) * 4 + y0 * 4 + (block & 1) * 2 + x0
 
 
-def kernel_call(kernel, shape, n_in, flops, nbytes, scratch=()):
+def kernel_call(kernel, shapes, n_in, flops, nbytes, scratch=(), limit=12):
     return pl.pallas_call(
         kernel,
-        out_shape=jax.ShapeDtypeStruct(shape, BF16),
+        out_shape=[jax.ShapeDtypeStruct(shape, BF16) for shape in shapes],
         in_specs=[VMEM] * n_in,
-        out_specs=VMEM,
+        out_specs=[VMEM] * len(shapes),
         scratch_shapes=scratch,
-        compiler_params=pltpu.CompilerParams(vmem_limit_bytes=12 << 20),
+        compiler_params=pltpu.CompilerParams(vmem_limit_bytes=limit << 20),
         cost_estimate=pl.CostEstimate(flops=flops, bytes_accessed=nbytes, transcendentals=0),
     )
 
@@ -56,12 +56,13 @@
     h[...] = jax.nn.gelu(preact, approximate=True).astype(BF16)
 
 
-def second_kernel(hidden, w00, w01, w10, w11, out):
-    left = hidden[...].reshape(320, 768)
-    for k, w in enumerate((w00, w01, w10, w11)):
-        product = jnp.dot(left, w[...], preferred_element_type=F32).astype(BF16)
-        for b in range(4):
-            out[slot(b, k // 2, k % 2)] = product[b * 80 : (b + 1) * 80]
+def second_kernel(hidden, w00, w01, w10, w11, here, other):
+    for half, out in ((1, other), (0, here)):
+        left = jnp.concatenate([hidden[b, half * 40 : (half + 1) * 40] for b in range(4)], axis=0)
+        for k, w in enumerate((w00, w01, w10, w11)):
+            product = jnp.dot(left, w[...], preferred_element_type=F32).astype(BF16)
+            for b in range(4):
+                out[slot(b, k // 2, k % 2)] = product[b * 40 : (b + 1) * 40]
 
 
 def shards(tokens, w1, b1, w2, b2):
@@ -79,15 +80,21 @@
     got = lax.all_to_all(spread, PLANE, 0, 0, tiled=True)
     flops = 2 * 320 * 3072 * 768
     scratch = [pltpu.VMEM((320, 768), F32)]
-    part = kernel_call(first_kernel, (4, 80, 768), 5, flops, 8 << 20, scratch)(got, *w1_all)
+    (part,) = kernel_call(first_kernel, [(4, 80, 768)], 5, flops, 8 << 20, scratch, 54)(got, *w1_all)
     part = lax.all_to_all(part, "zq", 0, 0, tiled=True)
-    h = kernel_call(middle_kernel, (80, 768), 2, 20 * 80 * 768, 1 << 20)(part, b1.reshape(1, 768))
+    (h,) = kernel_call(middle_kernel, [(80, 768)], 2, 20 * 80 * 768, 1 << 20)(part, b1.reshape(1, 768))
     hidden = lax.all_gather(h, "zq", axis=0, tiled=False)
-    out = kernel_call(second_kernel, (16, 80, 768), 5, flops, 8 << 20)(hidden, *w2_all)
-    out = lax.all_to_all(out, PLANE, 0, 0, tiled=True).astype(F32).sum(axis=0).astype(BF16)
+    shapes = [(16, 40, 768)] * 2
+    here, other = kernel_call(second_kernel, shapes, 5, flops, 8 << 20, (), 12)(hidden, *w2_all)
 
-    back = [lax.ppermute(out[k * 40 : (k + 1) * 40], CORNER, corner_pairs(k)) for k in range(2)]
-    return (back[0].astype(F32) + back[1].astype(F32) + b2.astype(F32)).astype(BF16)
+    other = lax.all_to_all(other, PLANE, 0, 0, tiled=True)
+    here, _ = barrier((here, other))
+    here = lax.all_to_all(here, PLANE, 0, 0, tiled=True)
+    total = b2.astype(F32)
+    for k, out in ((1, other), (0, here)):
+        out = out.astype(F32).sum(axis=0).astype(BF16)
+        total = total + lax.ppermute(out, CORNER, corner_pairs(k)).astype(F32)
+    return total.astype(BF16)
 
 
 def solution(mesh):

time: 190 us -> 186 us (0.979)
  blocking collectives: 55.2 us -> 44.5 us
  starting transfers between devices: 60.5 us -> 64.3 us
  waiting for transfers between devices: 61.2 us -> 64.2 us
  local copies, waits for them, and re-layouts: 3.75 us -> 1.41 us
  Pallas kernels: 7.59 us -> 9.89 us
    all_to_all x1, blocking collectives: 31.6 us -> 20.9 us  [shards(): other = lax.all_to_all(other, PLANE, 0, 0, tiled=True)]
    all_to_all x0 -> x1, starting transfers between devices: none -> 3.64 us  [shards(): here = lax.all_to_all(here, PLANE, 0, 0, tiled=True)]
    pallas_call x3, Pallas kernels: 7.59 us -> 9.89 us  [the longest x1 5.43 us: shards(): kernel_call(first_kernel, [(4, 80, 768)], 5, flops, 8 << 20, scratch, 54)]
    unnamed x12 -> x8, local copies, waits for them, and re-layouts: 2.31 us -> 0.02 us
    ppermute x2, waiting for transfers between devices: 4.66 us -> 6.67 us  [shards(): total = total + lax.ppermute(out, CORNER, corner_pairs(k)).astype(F32)]
  transfers between devices with their start and end apart: 12 -> 13, of which waited for: 6 -> 6; matrix products, arithmetic and copies ran while one was open for 1% -> 1% of each run, Pallas kernels for 2% -> 3%
where the time goes in v6:
time: 186 us; the launch traced here: 185 us
  starting transfers between devices  64.3 us (35%)
  waiting for transfers between devices  64.2 us (35%)
  blocking collectives  44.5 us (24%)
  Pallas kernels  9.89 us (5%)
    ppermute x2, waiting for transfers between devices, weights(): w_z = lax.ppermute(w, 'zb', SWAP)  30.4 us
    all_gather x1, blocking collectives, shards(): hidden = lax.all_gather(h, 'zq', axis=0, tiled=False)  23.6 us
    all_to_all x1, blocking collectives, shards(): other = lax.all_to_all(other, PLANE, 0, 0, tiled=True)  20.9 us
    ppermute x2, starting transfers between devices, shards(): lax.ppermute(tokens, CORNER, corner_pairs(k))  18.2 us
    ppermute x2, starting transfers between devices, shards(): total = total + lax.ppermute(out, CORNER, corner_pairs(k)).astype(F32)  18.1 us
    all_to_all x1, waiting for transfers between devices, shards(): part = lax.all_to_all(part, 'zq', 0, 0, tiled=True)  10.7 us
    ppermute x2, waiting for transfers between devices, shards(): lax.ppermute(tokens, CORNER, corner_pairs(k))  8.69 us
    ppermute x4, starting transfers between devices, weights(): return [w, lax.ppermute(w, 'c', SWAP), w_z, lax.ppermute(w_z, 'c', SWAP)]  7.83 us
  transfers between devices with their start and end apart: 13, of which 6 were waited for; matrix products, arithmetic and copies ran while one was open for 1% of the time, Pallas kernels for 3%

profile of v6, /device:TPU:32, one launch (start us, length us, event | category | flops | bytes accessed | tf_op | source)
XLA Modules:
  0.0 185.3 jit_solution(15859843286661072238)
XLA Ops:
  0.0 15.4 %collective-permute-start.1 = (bf16[40,768]{1,0:T(8,128)(2,1)}, bf16[40,768]{1,0:T(8,128)(2,1)S(1)}, u32[]{:S(2)}, u32[]{:S(2)}) collective-permute-start(bf16[40,768]{1,0:T(8,128)(2,1)} %param.5), channel_id=1, source_target_pairs={{0,1},{1,0},{2,33},{3,32},{8,65},{9,64},{10,97},{11,96},{32,3},{33... | collective-permute-start | bytes 184328 | tf_op jit(solution)/shard_map/ppermute | solution.py:69
  15.4 2.8 %collective-permute-start = (bf16[40,768]{1,0:T(8,128)(2,1)}, bf16[40,768]{1,0:T(8,128)(2,1)S(1)}, u32[]{:S(2)}, u32[]{:S(2)}) collective-permute-start(bf16[40,768]{1,0:T(8,128)(2,1)} %param.5), channel_id=1, source_target_pairs={{0,0},{1,1},{2,32},{3,33},{8,64},{9,65},{10,96},{11,97},{32,2},{33... | collective-permute-start | bytes 184328 | tf_op jit(solution)/shard_map/ppermute | solution.py:69
  18.2 8.7 %collective-permute-done.1 = bf16[40,768]{1,0:T(8,128)(2,1)S(1)} collective-permute-done((bf16[40,768]{1,0:T(8,128)(2,1)}, bf16[40,768]{1,0:T(8,128)(2,1)S(1)}, u32[]{:S(2)}, u32[]{:S(2)}) %collective-permute-start.1) | collective-permute-done | bytes 61472 | tf_op jit(solution)/shard_map/ppermute | solution.py:69
  26.9 1.9 %collective-permute-start.3 = (bf16[768,768]{1,0:T(8,128)(2,1)}, bf16[768,768]{1,0:T(8,128)(2,1)}, u32[]{:S(2)}, u32[]{:S(2)}) collective-permute-start(bf16[768,768]{1,0:T(8,128)(2,1)} %w00), channel_id=1, source_target_pairs={{0,64},{64,0},{1,65},{65,1},{2,66},{66,2},{3,67},{67,3},{4,68},{68... | collective-permute-start | bytes 3538952 | tf_op jit(solution)/shard_map/ppermute | solution.py:73
  28.8 1.4 broadcast_in_dim.2
  30.2 7.0 %all-to-all-start = ((bf16[16,80,768]{2,1,0:T(8,128)(2,1)}), bf16[16,80,768]{2,1,0:T(8,128)(2,1)}, u32[]{:S(2)}, u32[]{:S(2)}) async-start(bf16[16,80,768]{2,1,0:T(8,128)(2,1)} %broadcast_in_dim.2), calls=%async_computation | async-start | bytes 3932160 | tf_op jit(solution)/shard_map/all_to_all | solution.py:80
  37.2 2.1 %collective-permute-start.2 = (bf16[768,768]{1,0:T(8,128)(2,1)S(1)}, bf16[768,768]{1,0:T(8,128)(2,1)}, u32[]{:S(2)}, u32[]{:S(2)}) collective-permute-start(bf16[768,768]{1,0:T(8,128)(2,1)S(1)} %copy-done.1), channel_id=1, source_target_pairs={{0,32},{32,0},{1,33},{33,1},{2,34},{34,2},{3,35},{35,3},{4,36},{36... | collective-permute-start | bytes 3538952 | tf_op jit(solution)/shard_map/ppermute | solution.py:74
  39.4 18.3 %collective-permute-done.3.w10 = bf16[768,768]{1,0:T(8,128)(2,1)} collective-permute-done((bf16[768,768]{1,0:T(8,128)(2,1)}, bf16[768,768]{1,0:T(8,128)(2,1)}, u32[]{:S(2)}, u32[]{:S(2)}) %collective-permute-start.3) | collective-permute-done | bytes 1179680 | tf_op jit(solution)/shard_map/ppermute | solution.py:73
  57.7 1.9 %collective-permute-start.4 = (bf16[768,768]{1,0:T(8,128)(2,1)}, bf16[768,768]{1,0:T(8,128)(2,1)}, u32[]{:S(2)}, u32[]{:S(2)}) collective-permute-start(bf16[768,768]{1,0:T(8,128)(2,1)} %collective-permute-done.3.w10), channel_id=1, source_target_pairs={{0,32},{32,0},{1,33},{33,1},{2,34},{34,2},{3,35},{35,3},{4,36},{36... | collective-permute-start | bytes 3538952 | tf_op jit(solution)/shard_map/ppermute | solution.py:74
  59.6 2.3 %collective-permute-start.6 = (bf16[768,768]{1,0:T(8,128)(2,1)S(1)}, bf16[768,768]{1,0:T(8,128)(2,1)S(1)}, u32[]{:S(2)}, u32[]{:S(2)}) collective-permute-start(bf16[768,768]{1,0:T(8,128)(2,1)S(1)} %copy-done), channel_id=1, source_target_pairs={{0,64},{64,0},{1,65},{65,1},{2,66},{66,2},{3,67},{67,3},{4,68},{68... | collective-permute-start | bytes 3538952 | tf_op jit(solution)/shard_map/ppermute | solution.py:73
  61.9 7.6 %all-to-all-done.got = bf16[16,80,768]{2,1,0:T(8,128)(2,1)} async-done(((bf16[16,80,768]{2,1,0:T(8,128)(2,1)}), bf16[16,80,768]{2,1,0:T(8,128)(2,1)}, u32[]{:S(2)}, u32[]{:S(2)}) %all-to-all-start) | async-done | bytes 1966112 | tf_op jit(solution)/shard_map/all_to_all | solution.py:80
  69.6 5.4 %shard_map.55 = bf16[4,80,768]{2,1,0:T(8,128)(2,1)} custom-call(bf16[16,80,768]{2,1,0:T(8,128)(2,1)} %all-to-all-done.got, bf16[768,768]{1,0:T(8,128)(2,1)} %w00, bf16[768,768]{1,0:T(8,128)(2,1)} %collective-permute-done.2.w01, bf16[768,768]{1,0:T(8,128)(2,1)} %collective-permute-done.3.w10, bf16[768,768]{1,0:T(8,128)(2,1)} %collective-permute-done.4.w11), custom_call_target="tpu_custom_call" | custom-call | flops 1509949440 | bytes 8388608 | tf_op jit(solution)/shard_map/pallas_call | solution.py:83
  75.0 5.3 %all-to-all-start.1 = ((bf16[4,80,768]{2,1,0:T(8,128)(2,1)}), bf16[4,80,768]{2,1,0:T(8,128)(2,1)S(1)}, u32[]{:S(2)}, u32[]{:S(2)}) async-start(bf16[4,80,768]{2,1,0:T(8,128)(2,1)} %shard_map.55), calls=%async_computation.1 | async-start | bytes 983040 | tf_op jit(solution)/shard_map/all_to_all | solution.py:84
  80.3 1.9 %collective-permute-start.5 = (bf16[768,768]{1,0:T(8,128)(2,1)S(1)}, bf16[768,768]{1,0:T(8,128)(2,1)}, u32[]{:S(2)}, u32[]{:S(2)}) collective-permute-start(bf16[768,768]{1,0:T(8,128)(2,1)S(1)} %copy-done), channel_id=1, source_target_pairs={{0,32},{32,0},{1,33},{33,1},{2,34},{34,2},{3,35},{35,3},{4,36},{36... | collective-permute-start | bytes 3538952 | tf_op jit(solution)/shard_map/ppermute | solution.py:74
  82.2 12.1 %collective-permute-done.6.w10 = bf16[768,768]{1,0:T(8,128)(2,1)S(1)} collective-permute-done((bf16[768,768]{1,0:T(8,128)(2,1)S(1)}, bf16[768,768]{1,0:T(8,128)(2,1)S(1)}, u32[]{:S(2)}, u32[]{:S(2)}) %collective-permute-start.6) | collective-permute-done | bytes 1179680 | tf_op jit(solution)/shard_map/ppermute | solution.py:73
  94.3 1.9 %collective-permute-start.7 = (bf16[768,768]{1,0:T(8,128)(2,1)S(1)}, bf16[768,768]{1,0:T(8,128)(2,1)}, u32[]{:S(2)}, u32[]{:S(2)}) collective-permute-start(bf16[768,768]{1,0:T(8,128)(2,1)S(1)} %collective-permute-done.6.w10), channel_id=1, source_target_pairs={{0,32},{32,0},{1,33},{33,1},{2,34},{34,2},{3,35},{35,3},{4,36},{36... | collective-permute-start | bytes 3538952 | tf_op jit(solution)/shard_map/ppermute | solution.py:74
  96.2 10.7 %all-to-all-done.1.parts = bf16[4,80,768]{2,1,0:T(8,128)(2,1)S(1)} async-done(((bf16[4,80,768]{2,1,0:T(8,128)(2,1)}), bf16[4,80,768]{2,1,0:T(8,128)(2,1)S(1)}, u32[]{:S(2)}, u32[]{:S(2)}) %all-to-all-start.1) | async-done | bytes 491552 | tf_op jit(solution)/shard_map/all_to_all | solution.py:84
  107.1 23.6 %all-gather = bf16[320,768]{1,0:T(8,128)(2,1)S(1)} all-gather(bf16[80,768]{1,0:T(8,128)(2,1)S(1)} %shard_map.56), channel_id=2, replica_groups=mesh['zq'=4,'zb'=2,'c'=2,'yp'=2,'y0'=2,'xp'=2,'x0'=2,'zh'=2] {'zq'}, dimensions={0}, use_global_device_ids=true | all-gather | bytes 614400 | tf_op jit(solution)/shard_map/all_gather | solution.py:86
  130.7 4.3 %shard_map.57 = (bf16[16,40,768]{2,1,0:T(8,128)(2,1)}, bf16[16,40,768]{2,1,0:T(8,128)(2,1)S(1)}) custom-call(bf16[4,80,768]{2,1,0:T(8,128)(2,1)S(1)} %bitcast.1, bf16[768,768]{1,0:T(8,128)(2,1)S(1)} %copy-done, bf16[768,768]{1,0:T(8,128)(2,1)} %collective-permute-done.5.w01, bf16[768,768]{1,0:T(8,128)(2,1)S(1)} %collective-permute-done.6.w10, ...), custom_call_target="tpu_custom_call" | custom-call | flops 1509949440 | bytes 8388608 | tf_op jit(solution)/shard_map/pallas_call | solution.py:88
  135.0 20.9 %all_to_all.20 = bf16[16,40,768]{2,1,0:T(8,128)(2,1)S(1)} all-to-all(bf16[16,40,768]{2,1,0:T(8,128)(2,1)S(1)} %get-tuple-element.14), channel_id=1, replica_groups=mesh['zq'=4,'zb'=2,'c'=2,'yp'=2,'y0'=2,'xp'=2,'x0'=2,'zh'=2] {'yp','y0',..., dimensions={0} | all-to-all | bytes 1966080 | tf_op jit(solution)/shard_map/all_to_all | solution.py:90
  155.9 3.6 %all-to-all-start.3 = ((bf16[16,40,768]{2,1,0:T(8,128)(2,1)}), bf16[16,40,768]{2,1,0:T(8,128)(2,1)S(1)}, u32[]{:S(2)}, u32[]{:S(2)}) async-start(bf16[16,40,768]{2,1,0:T(8,128)(2,1)} %get-tuple-element.16), calls=%async_computation.3 | async-start | bytes 1966080 | tf_op jit(solution)/shard_map/all_to_all | solution.py:92
  159.7 14.3 %collective-permute-start.8 = (bf16[40,768]{1,0:T(8,128)(2,1)S(1)}, bf16[40,768]{1,0:T(8,128)(2,1)S(1)}, u32[]{:S(2)}, u32[]{:S(2)}) collective-permute-start(bf16[40,768]{1,0:T(8,128)(2,1)S(1)} %reduce_sum.24), channel_id=1, source_target_pairs={{0,1},{1,0},{2,33},{3,32},{8,65},{9,64},{10,97},{11,96},{32,3},{33... | collective-permute-start | bytes 184328 | tf_op jit(solution)/shard_map/ppermute | solution.py:96
  174.2 3.8 %collective-permute-start.9 = (bf16[40,768]{1,0:T(8,128)(2,1)S(1)}, bf16[40,768]{1,0:T(8,128)(2,1)S(1)}, u32[]{:S(2)}, u32[]{:S(2)}) collective-permute-start(bf16[40,768]{1,0:T(8,128)(2,1)S(1)} %reduce_sum.25), channel_id=1, source_target_pairs={{0,0},{1,1},{2,32},{3,33},{8,64},{9,65},{10,96},{11,97},{32,2},{33... | collective-permute-start | bytes 184328 | tf_op jit(solution)/shard_map/ppermute | solution.py:96
  178.0 6.7 %collective-permute-done.8 = bf16[40,768]{1,0:T(8,128)(2,1)S(1)} collective-permute-done((bf16[40,768]{1,0:T(8,128)(2,1)S(1)}, bf16[40,768]{1,0:T(8,128)(2,1)S(1)}, u32[]{:S(2)}, u32[]{:S(2)}) %collective-permute-start.8) | collective-permute-done | bytes 61472 | tf_op jit(solution)/shard_map/ppermute | solution.py:96
  (22 shorter events, 1.2 us)
Async XLA Ops:
  0.0 26.9 %collective-permute-start.1 = (bf16[40,768]{1,0:T(8,128)(2,1)}, bf16[40,768]{1,0:T(8,128)(2,1)S(1)}, u32[]{:S(2)}, u32[]{:S(2)}) collective-permute-start(bf16[40,768]{1,0:T(8,128)(2,1)} %param.5), channel_id=1, source_target_pairs={{0,1},{1,0},{2,33},{3,32},{8,65},{9,64},{10,97},{11,96},{32,3},{33... | collective-permute-start | bytes 184328 | tf_op jit(solution)/shard_map/ppermute | solution.py:69
  15.4 11.5 %collective-permute-start = (bf16[40,768]{1,0:T(8,128)(2,1)}, bf16[40,768]{1,0:T(8,128)(2,1)S(1)}, u32[]{:S(2)}, u32[]{:S(2)}) collective-permute-start(bf16[40,768]{1,0:T(8,128)(2,1)} %param.5), channel_id=1, source_target_pairs={{0,0},{1,1},{2,32},{3,33},{8,64},{9,65},{10,96},{11,97},{32,2},{33... | collective-permute-start | bytes 184328 | tf_op jit(solution)/shard_map/ppermute | solution.py:69
  26.9 30.8 %collective-permute-start.3 = (bf16[768,768]{1,0:T(8,128)(2,1)}, bf16[768,768]{1,0:T(8,128)(2,1)}, u32[]{:S(2)}, u32[]{:S(2)}) collective-permute-start(bf16[768,768]{1,0:T(8,128)(2,1)} %w00), channel_id=1, source_target_pairs={{0,64},{64,0},{1,65},{65,1},{2,66},{66,2},{3,67},{67,3},{4,68},{68... | collective-permute-start | bytes 3538952 | tf_op jit(solution)/shard_map/ppermute | solution.py:73
  30.2 7.0 %copy-start.1 = (bf16[768,768]{1,0:T(8,128)(2,1)S(1)}, bf16[768,768]{1,0:T(8,128)(2,1)}, u32[]{:S(2)}) copy-start(bf16[768,768]{1,0:T(8,128)(2,1)} %w00) | copy-start | bytes 3538948
  30.2 29.4 %copy-start = (bf16[768,768]{1,0:T(8,128)(2,1)S(1)}, bf16[768,768]{1,0:T(8,128)(2,1)}, u32[]{:S(2)}) copy-start(bf16[768,768]{1,0:T(8,128)(2,1)} %w00.1) | copy-start | bytes 3538948
  30.2 39.3 %all-to-all-start = ((bf16[16,80,768]{2,1,0:T(8,128)(2,1)}), bf16[16,80,768]{2,1,0:T(8,128)(2,1)}, u32[]{:S(2)}, u32[]{:S(2)}) async-start(bf16[16,80,768]{2,1,0:T(8,128)(2,1)} %broadcast_in_dim.2), calls=%async_computation | async-start | bytes 3932160 | tf_op jit(solution)/shard_map/all_to_all | solution.py:80
  37.2 59.0 %copy-start.3 = (bf16[768]{0:T(1024)(128)(2,1)S(1)}, bf16[768]{0:T(1024)(128)(2,1)}, u32[]{:S(2)}) copy-start(bf16[768]{0:T(1024)(128)(2,1)} %param.7) | copy-start | bytes 4612
  37.2 24.7 %collective-permute-start.2 = (bf16[768,768]{1,0:T(8,128)(2,1)S(1)}, bf16[768,768]{1,0:T(8,128)(2,1)}, u32[]{:S(2)}, u32[]{:S(2)}) collective-permute-start(bf16[768,768]{1,0:T(8,128)(2,1)S(1)} %copy-done.1), channel_id=1, source_target_pairs={{0,32},{32,0},{1,33},{33,1},{2,34},{34,2},{3,35},{35,3},{4,36},{36... | collective-permute-start | bytes 3538952 | tf_op jit(solution)/shard_map/ppermute | solution.py:74
  57.7 11.9 %collective-permute-start.4 = (bf16[768,768]{1,0:T(8,128)(2,1)}, bf16[768,768]{1,0:T(8,128)(2,1)}, u32[]{:S(2)}, u32[]{:S(2)}) collective-permute-start(bf16[768,768]{1,0:T(8,128)(2,1)} %collective-permute-done.3.w10), channel_id=1, source_target_pairs={{0,32},{32,0},{1,33},{33,1},{2,34},{34,2},{3,35},{35,3},{4,36},{36... | collective-permute-start | bytes 3538952 | tf_op jit(solution)/shard_map/ppermute | solution.py:74
  59.6 34.7 %collective-permute-start.6 = (bf16[768,768]{1,0:T(8,128)(2,1)S(1)}, bf16[768,768]{1,0:T(8,128)(2,1)S(1)}, u32[]{:S(2)}, u32[]{:S(2)}) collective-permute-start(bf16[768,768]{1,0:T(8,128)(2,1)S(1)} %copy-done), channel_id=1, source_target_pairs={{0,64},{64,0},{1,65},{65,1},{2,66},{66,2},{3,67},{67,3},{4,68},{68... | collective-permute-start | bytes 3538952 | tf_op jit(solution)/shard_map/ppermute | solution.py:73
  75.0 32.0 %all-to-all-start.1 = ((bf16[4,80,768]{2,1,0:T(8,128)(2,1)}), bf16[4,80,768]{2,1,0:T(8,128)(2,1)S(1)}, u32[]{:S(2)}, u32[]{:S(2)}) async-start(bf16[4,80,768]{2,1,0:T(8,128)(2,1)} %shard_map.55), calls=%async_computation.1 | async-start | bytes 983040 | tf_op jit(solution)/shard_map/all_to_all | solution.py:84
  80.3 50.4 %collective-permute-start.5 = (bf16[768,768]{1,0:T(8,128)(2,1)S(1)}, bf16[768,768]{1,0:T(8,128)(2,1)}, u32[]{:S(2)}, u32[]{:S(2)}) collective-permute-start(bf16[768,768]{1,0:T(8,128)(2,1)S(1)} %copy-done), channel_id=1, source_target_pairs={{0,32},{32,0},{1,33},{33,1},{2,34},{34,2},{3,35},{35,3},{4,36},{36... | collective-permute-start | bytes 3538952 | tf_op jit(solution)/shard_map/ppermute | solution.py:74
  94.3 36.4 %collective-permute-start.7 = (bf16[768,768]{1,0:T(8,128)(2,1)S(1)}, bf16[768,768]{1,0:T(8,128)(2,1)}, u32[]{:S(2)}, u32[]{:S(2)}) collective-permute-start(bf16[768,768]{1,0:T(8,128)(2,1)S(1)} %collective-permute-done.6.w10), channel_id=1, source_target_pairs={{0,32},{32,0},{1,33},{33,1},{2,34},{34,2},{3,35},{35,3},{4,36},{36... | collective-permute-start | bytes 3538952 | tf_op jit(solution)/shard_map/ppermute | solution.py:74
  155.9 18.1 %all-to-all-start.3 = ((bf16[16,40,768]{2,1,0:T(8,128)(2,1)}), bf16[16,40,768]{2,1,0:T(8,128)(2,1)S(1)}, u32[]{:S(2)}, u32[]{:S(2)}) async-start(bf16[16,40,768]{2,1,0:T(8,128)(2,1)} %get-tuple-element.16), calls=%async_computation.3 | async-start | bytes 1966080 | tf_op jit(solution)/shard_map/all_to_all | solution.py:92
  159.6 18.4 %copy-start.2 = (bf16[768]{0:T(1024)(128)(2,1)S(1)}, bf16[768]{0:T(1024)(128)(2,1)}, u32[]{:S(2)}) copy-start(bf16[768]{0:T(1024)(128)(2,1)} %param.9) | copy-start | bytes 4612
  159.7 25.0 %collective-permute-start.8 = (bf16[40,768]{1,0:T(8,128)(2,1)S(1)}, bf16[40,768]{1,0:T(8,128)(2,1)S(1)}, u32[]{:S(2)}, u32[]{:S(2)}) collective-permute-start(bf16[40,768]{1,0:T(8,128)(2,1)S(1)} %reduce_sum.24), channel_id=1, source_target_pairs={{0,1},{1,0},{2,33},{3,32},{8,65},{9,64},{10,97},{11,96},{32,3},{33... | collective-permute-start | bytes 184328 | tf_op jit(solution)/shard_map/ppermute | solution.py:96
  174.2 10.5 %collective-permute-start.9 = (bf16[40,768]{1,0:T(8,128)(2,1)S(1)}, bf16[40,768]{1,0:T(8,128)(2,1)S(1)}, u32[]{:S(2)}, u32[]{:S(2)}) collective-permute-start(bf16[40,768]{1,0:T(8,128)(2,1)S(1)} %reduce_sum.25), channel_id=1, source_target_pairs={{0,0},{1,1},{2,32},{3,33},{8,64},{9,65},{10,96},{11,97},{32,2},{33... | collective-permute-start | bytes 184328 | tf_op jit(solution)/shard_map/ppermute | solution.py:96

commit v7 on v6

--- a/solution.py
+++ b/solution.py
@@ -41,10 +41,17 @@
     )
 
 
-def first_kernel(got, w00, w01, w10, w11, part, total):
-    for k, w in enumerate((w00, w01, w10, w11)):
-        left = jnp.concatenate([got[slot(b, k // 2, k % 2)] for b in range(4)], axis=0)
-        product = jnp.dot(left, w[...], preferred_element_type=F32)
+def spread_kernel(block, out):
+    for i in range(16):
+        out[i] = block[...]
+
+
+def first_kernel(here, other, w00, w01, w10, w11a, w11b, part, total):
+    for k, ws in enumerate(((w00,), (w01,), (w10,), (w11a, w11b))):
+        rows = [got[slot(b, k // 2, k % 2)] for b in range(4) for got in (here, other)]
+        left = jnp.concatenate(rows, axis=0)
+        right = ws[0][...] if k < 3 else jnp.concatenate([w[...] for w in ws], axis=0)
+        product = jnp.dot(left, right, preferred_element_type=F32)
         total[...] = product if k == 0 else total[...] + product
     part[...] = total[...].astype(BF16).reshape(4, 80, 768)
 
@@ -66,21 +73,25 @@
 
 
 def shards(tokens, w1, b1, w2, b2):
-    tok = jnp.concatenate([lax.ppermute(tokens, CORNER, corner_pairs(k)) for k in range(2)], axis=0)
-    w1_in, w2_in, tok = barrier((w1, w2, tok))
+    here, other = (lax.ppermute(tokens, CORNER, corner_pairs(k)) for k in range(2))
+    w1_in, w2_in, here = barrier((w1, w2, here))
 
-    def weights(w):
-        w_z = lax.ppermute(w, "zb", SWAP)
-        return [w, lax.ppermute(w, "c", SWAP), w_z, lax.ppermute(w_z, "c", SWAP)]
+    shape = [(16, 40, 768)]
+    (here,) = kernel_call(spread_kernel, shape, 1, 10**9, 1 << 20)(here)
+    (other,) = kernel_call(spread_kernel, shape, 1, 40 * 10**9, 1 << 20)(other)
+    here = lax.all_to_all(here, PLANE, 0, 0, tiled=True)
+    other, _ = barrier((other, here))
+    other = lax.all_to_all(other, PLANE, 0, 0, tiled=True)
 
-    w1_all = weights(w1_in)
-    w2_all = weights(w2_in)
+    w1_z = lax.ppermute(w1_in, "zb", SWAP)
+    w1_all = [w1, lax.ppermute(w1_in, "c", SWAP), w1_z]
+    w1_all += [lax.ppermute(w1_z[at : at + 384], "c", SWAP) for at in (0, 384)]
+    w2_z = lax.ppermute(w2_in, "zb", SWAP)
+    w2_all = [w2, lax.ppermute(w2_in, "c", SWAP), w2_z, lax.ppermute(w2_z, "c", SWAP)]
 
-    spread = jnp.broadcast_to(tok[None], (16, 80, 768))
-    got = lax.all_to_all(spread, PLANE, 0, 0, tiled=True)
     flops = 2 * 320 * 3072 * 768
     scratch = [pltpu.VMEM((320, 768), F32)]
-    (part,) = kernel_call(first_kernel, [(4, 80, 768)], 5, flops, 8 << 20, scratch, 54)(got, *w1_all)
+    (part,) = kernel_call(first_kernel, [(4, 80, 768)], 7, flops, 8 << 20, scratch, 54)(here, other, *w1_all)
     part = lax.all_to_all(part, "zq", 0, 0, tiled=True)
     (h,) = kernel_call(middle_kernel, [(80, 768)], 2, 20 * 80 * 768, 1 << 20)(part, b1.reshape(1, 768))
     hidden = lax.all_gather(h, "zq", axis=0, tiled=False)

time: 186 us -> 185 us (level)
  the two profiles are of different devices: /device:TPU:32 before, /device:TPU:38 now
where the time goes in v7:
time: 185 us; the launch traced here: 184 us
  waiting for transfers between devices  64 us (35%)
  starting transfers between devices  63.9 us (35%)
  blocking collectives  41.2 us (22%)
  Pallas kernels  11.9 us (6%)
  local copies, waits for them, and re-layouts  1.95 us (1%)
    all_gather x1, blocking collectives, shards(): hidden = lax.all_gather(h, 'zq', axis=0, tiled=False)  23.7 us
    all_to_all x2, waiting for transfers between devices, shards(): here = lax.all_to_all(here, PLANE, 0, 0, tiled=True)  21.8 us
    ppermute x2, starting transfers between devices, shards(): lax.ppermute(tokens, CORNER, corner_pairs(k))  18.8 us
    all_to_all x1, blocking collectives, shards(): other = lax.all_to_all(other, PLANE, 0, 0, tiled=True)  17.4 us
    ppermute x1, waiting for transfers between devices, shards(): w2_z = lax.ppermute(w2_in, 'zb', SWAP)  16.6 us
    all_to_all x2, starting transfers between devices, shards(): here = lax.all_to_all(here, PLANE, 0, 0, tiled=True)  14.2 us
    all_to_all x1, waiting for transfers between devices, shards(): part = lax.all_to_all(part, 'zq', 0, 0, tiled=True)  11.4 us
    ppermute x2, waiting for transfers between devices, shards(): total = total + lax.ppermute(out, CORNER, corner_pairs(k)).astype(F32)  9.41 us
  transfers between devices with their start and end apart: 15, of which 6 were waited for; matrix products, arithmetic and copies ran while one was open for 0% of the time, Pallas kernels for 4%

profile of v7, /device:TPU:38, one launch (start us, length us, event | category | flops | bytes accessed | tf_op | source)
XLA Modules:
  0.0 184.1 jit_solution(2735777319380152985)
XLA Ops:
  0.0 2.7 %collective-permute-start = (bf16[40,768]{1,0:T(8,128)(2,1)}, bf16[40,768]{1,0:T(8,128)(2,1)S(1)}, u32[]{:S(2)}, u32[]{:S(2)}) collective-permute-start(bf16[40,768]{1,0:T(8,128)(2,1)} %param.5), channel_id=1, source_target_pairs={{0,0},{1,1},{2,32},{3,33},{8,64},{9,65},{10,96},{11,97},{32,2},{33... | collective-permute-start | bytes 184328 | tf_op jit(solution)/shard_map/ppermute | solution.py:76
  2.7 16.1 %collective-permute-start.1 = (bf16[40,768]{1,0:T(8,128)(2,1)}, bf16[40,768]{1,0:T(8,128)(2,1)S(1)}, u32[]{:S(2)}, u32[]{:S(2)}) collective-permute-start(bf16[40,768]{1,0:T(8,128)(2,1)} %param.5), channel_id=1, source_target_pairs={{0,1},{1,0},{2,33},{3,32},{8,65},{9,64},{10,97},{11,96},{32,3},{33... | collective-permute-start | bytes 184328 | tf_op jit(solution)/shard_map/ppermute | solution.py:76
  18.8 2.0 %collective-permute-start.3 = (bf16[768,768]{1,0:T(8,128)(2,1)}, bf16[768,768]{1,0:T(8,128)(2,1)S(1)}, u32[]{:S(2)}, u32[]{:S(2)}) collective-permute-start(bf16[768,768]{1,0:T(8,128)(2,1)} %w00.2), channel_id=1, source_target_pairs={{0,64},{64,0},{1,65},{65,1},{2,66},{66,2},{3,67},{67,3},{4,68},{68... | collective-permute-start | bytes 3538952 | tf_op jit(solution)/shard_map/ppermute | solution.py:86
  20.9 1.9 %collective-permute-start.2 = (bf16[768,768]{1,0:T(8,128)(2,1)}, bf16[768,768]{1,0:T(8,128)(2,1)S(1)}, u32[]{:S(2)}, u32[]{:S(2)}) collective-permute-start(bf16[768,768]{1,0:T(8,128)(2,1)} %w00.2), channel_id=1, source_target_pairs={{0,32},{32,0},{1,33},{33,1},{2,34},{34,2},{3,35},{35,3},{4,36},{36... | collective-permute-start | bytes 3538952 | tf_op jit(solution)/shard_map/ppermute | solution.py:87
  23.8 7.9 %all-to-all-start = ((bf16[16,40,768]{2,1,0:T(8,128)(2,1)}), bf16[16,40,768]{2,1,0:T(8,128)(2,1)S(1)}, u32[]{:S(2)}, u32[]{:S(2)}) async-start(bf16[16,40,768]{2,1,0:T(8,128)(2,1)} %shard_map.55), calls=%async_computation | async-start | bytes 1966080 | tf_op jit(solution)/shard_map/all_to_all | solution.py:82
  32.8 13.4 %all-to-all-done.here = bf16[16,40,768]{2,1,0:T(8,128)(2,1)S(1)} async-done(((bf16[16,40,768]{2,1,0:T(8,128)(2,1)}), bf16[16,40,768]{2,1,0:T(8,128)(2,1)S(1)}, u32[]{:S(2)}, u32[]{:S(2)}) %all-to-all-start) | async-done | bytes 983072 | tf_op jit(solution)/shard_map/all_to_all | solution.py:82
  47.1 7.3 %all-to-all-start.1 = ((bf16[16,40,768]{2,1,0:T(8,128)(2,1)}), bf16[16,40,768]{2,1,0:T(8,128)(2,1)}, u32[]{:S(2)}, u32[]{:S(2)}) async-start(bf16[16,40,768]{2,1,0:T(8,128)(2,1)} %shard_map.56), calls=%async_computation.1 | async-start | bytes 1966080 | tf_op jit(solution)/shard_map/all_to_all | solution.py:84
  55.5 1.9 %collective-permute-start.4 = (bf16[384,768]{1,0:T(8,128)(2,1)S(1)}, bf16[384,768]{1,0:T(8,128)(2,1)}, u32[]{:S(2)}, u32[]{:S(2)}) collective-permute-start(bf16[384,768]{1,0:T(8,128)(2,1)S(1)} %get-tuple-element.20), channel_id=1, source_target_pairs={{0,32},{32,0},{1,33},{33,1},{2,34},{34,2},{3,35},{35,3},{4,36},{36... | collective-permute-start | bytes 1769480 | tf_op jit(solution)/shard_map/ppermute | solution.py:88
  57.4 2.4 %collective-permute-start.5 = (bf16[384,768]{1,0:T(8,128)(2,1)S(1)}, bf16[384,768]{1,0:T(8,128)(2,1)}, u32[]{:S(2)}, u32[]{:S(2)}) collective-permute-start(bf16[384,768]{1,0:T(8,128)(2,1)S(1)} %get-tuple-element.19), channel_id=1, source_target_pairs={{0,32},{32,0},{1,33},{33,1},{2,34},{34,2},{3,35},{35,3},{4,36},{36... | collective-permute-start | bytes 1769480 | tf_op jit(solution)/shard_map/ppermute | solution.py:88
  59.8 3.1 %collective-permute-start.7 = (bf16[768,768]{1,0:T(8,128)(2,1)S(1)}, bf16[768,768]{1,0:T(8,128)(2,1)S(1)}, u32[]{:S(2)}, u32[]{:S(2)}) collective-permute-start(bf16[768,768]{1,0:T(8,128)(2,1)S(1)} %copy-done), channel_id=1, source_target_pairs={{0,64},{64,0},{1,65},{65,1},{2,66},{66,2},{3,67},{67,3},{4,68},{68... | collective-permute-start | bytes 3538952 | tf_op jit(solution)/shard_map/ppermute | solution.py:89
  63.0 4.8 %all-to-all-done.1.other = bf16[16,40,768]{2,1,0:T(8,128)(2,1)} async-done(((bf16[16,40,768]{2,1,0:T(8,128)(2,1)}), bf16[16,40,768]{2,1,0:T(8,128)(2,1)}, u32[]{:S(2)}, u32[]{:S(2)}) %all-to-all-start.1) | async-done | bytes 983072 | tf_op jit(solution)/shard_map/all_to_all | solution.py:84
  67.8 5.4 %shard_map.57 = bf16[4,80,768]{2,1,0:T(8,128)(2,1)} custom-call(bf16[16,40,768]{2,1,0:T(8,128)(2,1)} %copy-done.2, bf16[16,40,768]{2,1,0:T(8,128)(2,1)} %all-to-all-done.1.other, bf16[768,768]{1,0:T(8,128)(2,1)} %w00.2, bf16[768,768]{1,0:T(8,128)(2,1)} %copy-done.3, bf16[768,768]{1,0:T(8,128)(2,1)} %copy-done.1, ...), custom_call_target="tpu_custom_call" | custom-call | flops 1509949440 | bytes 8388608 | tf_op jit(solution)/shard_map/pallas_call | solution.py:94
  73.2 4.6 %all-to-all-start.2 = ((bf16[4,80,768]{2,1,0:T(8,128)(2,1)}), bf16[4,80,768]{2,1,0:T(8,128)(2,1)S(1)}, u32[]{:S(2)}, u32[]{:S(2)}) async-start(bf16[4,80,768]{2,1,0:T(8,128)(2,1)} %shard_map.57), calls=%async_computation.2 | async-start | bytes 983040 | tf_op jit(solution)/shard_map/all_to_all | solution.py:95
  77.7 1.9 %collective-permute-start.6 = (bf16[768,768]{1,0:T(8,128)(2,1)S(1)}, bf16[768,768]{1,0:T(8,128)(2,1)}, u32[]{:S(2)}, u32[]{:S(2)}) collective-permute-start(bf16[768,768]{1,0:T(8,128)(2,1)S(1)} %copy-done), channel_id=1, source_target_pairs={{0,32},{32,0},{1,33},{33,1},{2,34},{34,2},{3,35},{35,3},{4,36},{36... | collective-permute-start | bytes 3538952 | tf_op jit(solution)/shard_map/ppermute | solution.py:90
  79.7 16.6 %collective-permute-done.7.w10 = bf16[768,768]{1,0:T(8,128)(2,1)S(1)} collective-permute-done((bf16[768,768]{1,0:T(8,128)(2,1)S(1)}, bf16[768,768]{1,0:T(8,128)(2,1)S(1)}, u32[]{:S(2)}, u32[]{:S(2)}) %collective-permute-start.7) | collective-permute-done | bytes 1179680 | tf_op jit(solution)/shard_map/ppermute | solution.py:89
  98.2 11.4 %all-to-all-done.2.parts = bf16[4,80,768]{2,1,0:T(8,128)(2,1)S(1)} async-done(((bf16[4,80,768]{2,1,0:T(8,128)(2,1)}), bf16[4,80,768]{2,1,0:T(8,128)(2,1)S(1)}, u32[]{:S(2)}, u32[]{:S(2)}) %all-to-all-start.2) | async-done | bytes 491552 | tf_op jit(solution)/shard_map/all_to_all | solution.py:95
  109.7 23.7 %all-gather = bf16[320,768]{1,0:T(8,128)(2,1)S(1)} all-gather(bf16[80,768]{1,0:T(8,128)(2,1)S(1)} %shard_map.58), channel_id=2, replica_groups=mesh['zq'=4,'zb'=2,'c'=2,'yp'=2,'y0'=2,'xp'=2,'x0'=2,'zh'=2] {'zq'}, dimensions={0}, use_global_device_ids=true | all-gather | bytes 614400 | tf_op jit(solution)/shard_map/all_gather | solution.py:97
  133.5 4.3 %shard_map.59 = (bf16[16,40,768]{2,1,0:T(8,128)(2,1)}, bf16[16,40,768]{2,1,0:T(8,128)(2,1)S(1)}) custom-call(bf16[4,80,768]{2,1,0:T(8,128)(2,1)S(1)} %bitcast.1, bf16[768,768]{1,0:T(8,128)(2,1)S(1)} %copy-done, bf16[768,768]{1,0:T(8,128)(2,1)} %collective-permute-done.6.w01, bf16[768,768]{1,0:T(8,128)(2,1)S(1)} %collective-permute-done.7.w10, ...), custom_call_target="tpu_custom_call" | custom-call | flops 1509949440 | bytes 8388608 | tf_op jit(solution)/shard_map/pallas_call | solution.py:99
  137.8 17.4 %all_to_all.25 = bf16[16,40,768]{2,1,0:T(8,128)(2,1)S(1)} all-to-all(bf16[16,40,768]{2,1,0:T(8,128)(2,1)S(1)} %get-tuple-element.16), channel_id=1, replica_groups=mesh['zq'=4,'zb'=2,'c'=2,'yp'=2,'y0'=2,'xp'=2,'x0'=2,'zh'=2] {'yp','y0',..., dimensions={0} | all-to-all | bytes 1966080 | tf_op jit(solution)/shard_map/all_to_all | solution.py:101
  155.2 6.3 %all-to-all-start.4 = ((bf16[16,40,768]{2,1,0:T(8,128)(2,1)}), bf16[16,40,768]{2,1,0:T(8,128)(2,1)S(1)}, u32[]{:S(2)}, u32[]{:S(2)}) async-start(bf16[16,40,768]{2,1,0:T(8,128)(2,1)} %get-tuple-element.18), calls=%async_computation.4 | async-start | bytes 1966080 | tf_op jit(solution)/shard_map/all_to_all | solution.py:103
  161.7 1.9 %collective-permute-start.9 = (bf16[40,768]{1,0:T(8,128)(2,1)S(1)}, bf16[40,768]{1,0:T(8,128)(2,1)S(1)}, u32[]{:S(2)}, u32[]{:S(2)}) collective-permute-start(bf16[40,768]{1,0:T(8,128)(2,1)S(1)} %reduce_sum.24), channel_id=1, source_target_pairs={{0,1},{1,0},{2,33},{3,32},{8,65},{9,64},{10,97},{11,96},{32,3},{33... | collective-permute-start | bytes 184328 | tf_op jit(solution)/shard_map/ppermute | solution.py:107
  163.6 8.4 %all-to-all-done.4 = bf16[16,40,768]{2,1,0:T(8,128)(2,1)S(1)} async-done(((bf16[16,40,768]{2,1,0:T(8,128)(2,1)}), bf16[16,40,768]{2,1,0:T(8,128)(2,1)S(1)}, u32[]{:S(2)}, u32[]{:S(2)}) %all-to-all-start.4) | async-done | bytes 983072 | tf_op jit(solution)/shard_map/all_to_all | solution.py:103
  172.1 1.9 %collective-permute-start.10 = (bf16[40,768]{1,0:T(8,128)(2,1)S(1)}, bf16[40,768]{1,0:T(8,128)(2,1)S(1)}, u32[]{:S(2)}, u32[]{:S(2)}) collective-permute-start(bf16[40,768]{1,0:T(8,128)(2,1)S(1)} %reduce_sum.25), channel_id=1, source_target_pairs={{0,0},{1,1},{2,32},{3,33},{8,64},{9,65},{10,96},{11,97},{32,2},{33... | collective-permute-start | bytes 184328 | tf_op jit(solution)/shard_map/ppermute | solution.py:107
  174.1 9.4 %collective-permute-done.9 = bf16[40,768]{1,0:T(8,128)(2,1)S(1)} collective-permute-done((bf16[40,768]{1,0:T(8,128)(2,1)S(1)}, bf16[40,768]{1,0:T(8,128)(2,1)S(1)}, u32[]{:S(2)}, u32[]{:S(2)}) %collective-permute-start.9) | collective-permute-done | bytes 61472 | tf_op jit(solution)/shard_map/ppermute | solution.py:107
  (31 shorter events, 7.1 us)
Async XLA Ops:
  0.0 18.8 %collective-permute-start = (bf16[40,768]{1,0:T(8,128)(2,1)}, bf16[40,768]{1,0:T(8,128)(2,1)S(1)}, u32[]{:S(2)}, u32[]{:S(2)}) collective-permute-start(bf16[40,768]{1,0:T(8,128)(2,1)} %param.5), channel_id=1, source_target_pairs={{0,0},{1,1},{2,32},{3,33},{8,64},{9,65},{10,96},{11,97},{32,2},{33... | collective-permute-start | bytes 184328 | tf_op jit(solution)/shard_map/ppermute | solution.py:76
  2.7 29.0 %collective-permute-start.1 = (bf16[40,768]{1,0:T(8,128)(2,1)}, bf16[40,768]{1,0:T(8,128)(2,1)S(1)}, u32[]{:S(2)}, u32[]{:S(2)}) collective-permute-start(bf16[40,768]{1,0:T(8,128)(2,1)} %param.5), channel_id=1, source_target_pairs={{0,1},{1,0},{2,33},{3,32},{8,65},{9,64},{10,97},{11,96},{32,3},{33... | collective-permute-start | bytes 184328 | tf_op jit(solution)/shard_map/ppermute | solution.py:76
  18.8 35.6 %collective-permute-start.3 = (bf16[768,768]{1,0:T(8,128)(2,1)}, bf16[768,768]{1,0:T(8,128)(2,1)S(1)}, u32[]{:S(2)}, u32[]{:S(2)}) collective-permute-start(bf16[768,768]{1,0:T(8,128)(2,1)} %w00.2), channel_id=1, source_target_pairs={{0,64},{64,0},{1,65},{65,1},{2,66},{66,2},{3,67},{67,3},{4,68},{68... | collective-permute-start | bytes 3538952 | tf_op jit(solution)/shard_map/ppermute | solution.py:86
  20.9 42.1 %collective-permute-start.2 = (bf16[768,768]{1,0:T(8,128)(2,1)}, bf16[768,768]{1,0:T(8,128)(2,1)S(1)}, u32[]{:S(2)}, u32[]{:S(2)}) collective-permute-start(bf16[768,768]{1,0:T(8,128)(2,1)} %w00.2), channel_id=1, source_target_pairs={{0,32},{32,0},{1,33},{33,1},{2,34},{34,2},{3,35},{35,3},{4,36},{36... | collective-permute-start | bytes 3538952 | tf_op jit(solution)/shard_map/ppermute | solution.py:87
  23.8 22.4 %all-to-all-start = ((bf16[16,40,768]{2,1,0:T(8,128)(2,1)}), bf16[16,40,768]{2,1,0:T(8,128)(2,1)S(1)}, u32[]{:S(2)}, u32[]{:S(2)}) async-start(bf16[16,40,768]{2,1,0:T(8,128)(2,1)} %shard_map.55), calls=%async_computation | async-start | bytes 1966080 | tf_op jit(solution)/shard_map/all_to_all | solution.py:82
  46.2 0.9 copy-start.2
  47.1 20.7 %all-to-all-start.1 = ((bf16[16,40,768]{2,1,0:T(8,128)(2,1)}), bf16[16,40,768]{2,1,0:T(8,128)(2,1)}, u32[]{:S(2)}, u32[]{:S(2)}) async-start(bf16[16,40,768]{2,1,0:T(8,128)(2,1)} %shard_map.56), calls=%async_computation.1 | async-start | bytes 1966080 | tf_op jit(solution)/shard_map/all_to_all | solution.py:84
  54.4 5.4 %copy-start = (bf16[768,768]{1,0:T(8,128)(2,1)S(1)}, bf16[768,768]{1,0:T(8,128)(2,1)}, u32[]{:S(2)}) copy-start(bf16[768,768]{1,0:T(8,128)(2,1)} %w00.3) | copy-start | bytes 3538948
  54.5 1.0 copy-start.1
  55.5 7.5 %collective-permute-start.4 = (bf16[384,768]{1,0:T(8,128)(2,1)S(1)}, bf16[384,768]{1,0:T(8,128)(2,1)}, u32[]{:S(2)}, u32[]{:S(2)}) collective-permute-start(bf16[384,768]{1,0:T(8,128)(2,1)S(1)} %get-tuple-element.20), channel_id=1, source_target_pairs={{0,32},{32,0},{1,33},{33,1},{2,34},{34,2},{3,35},{35,3},{4,36},{36... | collective-permute-start | bytes 1769480 | tf_op jit(solution)/shard_map/ppermute | solution.py:88
  57.4 40.8 %copy-start.5 = (bf16[768]{0:T(1024)(128)(2,1)S(1)}, bf16[768]{0:T(1024)(128)(2,1)}, u32[]{:S(2)}) copy-start(bf16[768]{0:T(1024)(128)(2,1)} %param.7) | copy-start | bytes 4612
  57.4 5.6 %collective-permute-start.5 = (bf16[384,768]{1,0:T(8,128)(2,1)S(1)}, bf16[384,768]{1,0:T(8,128)(2,1)}, u32[]{:S(2)}, u32[]{:S(2)}) collective-permute-start(bf16[384,768]{1,0:T(8,128)(2,1)S(1)} %get-tuple-element.19), channel_id=1, source_target_pairs={{0,32},{32,0},{1,33},{33,1},{2,34},{34,2},{3,35},{35,3},{4,36},{36... | collective-permute-start | bytes 1769480 | tf_op jit(solution)/shard_map/ppermute | solution.py:88
  59.8 36.4 %collective-permute-start.7 = (bf16[768,768]{1,0:T(8,128)(2,1)S(1)}, bf16[768,768]{1,0:T(8,128)(2,1)S(1)}, u32[]{:S(2)}, u32[]{:S(2)}) collective-permute-start(bf16[768,768]{1,0:T(8,128)(2,1)S(1)} %copy-done), channel_id=1, source_target_pairs={{0,64},{64,0},{1,65},{65,1},{2,66},{66,2},{3,67},{67,3},{4,68},{68... | collective-permute-start | bytes 3538952 | tf_op jit(solution)/shard_map/ppermute | solution.py:89
  62.9 4.9 %copy-start.3 = (bf16[768,768]{1,0:T(8,128)(2,1)}, bf16[768,768]{1,0:T(8,128)(2,1)S(1)}, u32[]{:S(2)}) copy-start(bf16[768,768]{1,0:T(8,128)(2,1)S(1)} %collective-permute-done.2.w01) | copy-start | bytes 3538948
  73.2 36.4 %all-to-all-start.2 = ((bf16[4,80,768]{2,1,0:T(8,128)(2,1)}), bf16[4,80,768]{2,1,0:T(8,128)(2,1)S(1)}, u32[]{:S(2)}, u32[]{:S(2)}) async-start(bf16[4,80,768]{2,1,0:T(8,128)(2,1)} %shard_map.57), calls=%async_computation.2 | async-start | bytes 983040 | tf_op jit(solution)/shard_map/all_to_all | solution.py:95
  77.7 55.8 %collective-permute-start.6 = (bf16[768,768]{1,0:T(8,128)(2,1)S(1)}, bf16[768,768]{1,0:T(8,128)(2,1)}, u32[]{:S(2)}, u32[]{:S(2)}) collective-permute-start(bf16[768,768]{1,0:T(8,128)(2,1)S(1)} %copy-done), channel_id=1, source_target_pairs={{0,32},{32,0},{1,33},{33,1},{2,34},{34,2},{3,35},{35,3},{4,36},{36... | collective-permute-start | bytes 3538952 | tf_op jit(solution)/shard_map/ppermute | solution.py:90
  96.2 37.3 %collective-permute-start.8 = (bf16[768,768]{1,0:T(8,128)(2,1)S(1)}, bf16[768,768]{1,0:T(8,128)(2,1)}, u32[]{:S(2)}, u32[]{:S(2)}) collective-permute-start(bf16[768,768]{1,0:T(8,128)(2,1)S(1)} %collective-permute-done.7.w10), channel_id=1, source_target_pairs={{0,32},{32,0},{1,33},{33,1},{2,34},{34,2},{3,35},{35,3},{4,36},{36... | collective-permute-start | bytes 3538952 | tf_op jit(solution)/shard_map/ppermute | solution.py:90
  155.2 16.7 %all-to-all-start.4 = ((bf16[16,40,768]{2,1,0:T(8,128)(2,1)}), bf16[16,40,768]{2,1,0:T(8,128)(2,1)S(1)}, u32[]{:S(2)}, u32[]{:S(2)}) async-start(bf16[16,40,768]{2,1,0:T(8,128)(2,1)} %get-tuple-element.18), calls=%async_computation.4 | async-start | bytes 1966080 | tf_op jit(solution)/shard_map/all_to_all | solution.py:103
  161.5 12.5 %copy-start.4 = (bf16[768]{0:T(1024)(128)(2,1)S(1)}, bf16[768]{0:T(1024)(128)(2,1)}, u32[]{:S(2)}) copy-start(bf16[768]{0:T(1024)(128)(2,1)} %param.9) | copy-start | bytes 4612
  161.7 21.8 %collective-permute-start.9 = (bf16[40,768]{1,0:T(8,128)(2,1)S(1)}, bf16[40,768]{1,0:T(8,128)(2,1)S(1)}, u32[]{:S(2)}, u32[]{:S(2)}) collective-permute-start(bf16[40,768]{1,0:T(8,128)(2,1)S(1)} %reduce_sum.24), channel_id=1, source_target_pairs={{0,1},{1,0},{2,33},{3,32},{8,65},{9,64},{10,97},{11,96},{32,3},{33... | collective-permute-start | bytes 184328 | tf_op jit(solution)/shard_map/ppermute | solution.py:107
  172.1 11.4 %collective-permute-start.10 = (bf16[40,768]{1,0:T(8,128)(2,1)S(1)}, bf16[40,768]{1,0:T(8,128)(2,1)S(1)}, u32[]{:S(2)}, u32[]{:S(2)}) collective-permute-start(bf16[40,768]{1,0:T(8,128)(2,1)S(1)} %reduce_sum.25), channel_id=1, source_target_pairs={{0,0},{1,1},{2,32},{3,33},{8,64},{9,65},{10,96},{11,97},{32,2},{33... | collective-permute-start | bytes 184328 | tf_op jit(solution)/shard_map/ppermute | solution.py:107

commit v8 on v7

--- a/solution.py
+++ b/solution.py
@@ -92,6 +92,7 @@
     flops = 2 * 320 * 3072 * 768
     scratch = [pltpu.VMEM((320, 768), F32)]
     (part,) = kernel_call(first_kernel, [(4, 80, 768)], 7, flops, 8 << 20, scratch, 54)(here, other, *w1_all)
+    part, _ = barrier((part, w2_z))
     part = lax.all_to_all(part, "zq", 0, 0, tiled=True)
     (h,) = kernel_call(middle_kernel, [(80, 768)], 2, 20 * 80 * 768, 1 << 20)(part, b1.reshape(1, 768))
     hidden = lax.all_gather(h, "zq", axis=0, tiled=False)

time: 185 us -> 190 us (1.027)
  the two profiles are of different devices: /device:TPU:38 before, /device:TPU:14 now
where the time goes in v8:
time: 190 us; the launch traced here: 189 us
  starting transfers between devices  66.3 us (35%)
  waiting for transfers between devices  65.6 us (35%)
  blocking collectives  42.5 us (22%)
  Pallas kernels  11.9 us (6%)
    all_gather x1, blocking collectives, shards(): hidden = lax.all_gather(h, 'zq', axis=0, tiled=False)  24.2 us
    all_to_all x1, waiting for transfers between devices, shards(): part = lax.all_to_all(part, 'zq', 0, 0, tiled=True)  21.5 us
    ppermute x2, starting transfers between devices, shards(): lax.ppermute(tokens, CORNER, corner_pairs(k))  19.7 us
    all_to_all x1, blocking collectives, shards(): other = lax.all_to_all(other, PLANE, 0, 0, tiled=True)  18.3 us
    all_to_all x2, waiting for transfers between devices, shards(): here = lax.all_to_all(here, PLANE, 0, 0, tiled=True)  17.7 us
    all_to_all x2, starting transfers between devices, shards(): here = lax.all_to_all(here, PLANE, 0, 0, tiled=True)  15 us
    ppermute x2, waiting for transfers between devices, shards(): total = total + lax.ppermute(out, CORNER, corner_pairs(k)).astype(F32)  12.5 us
    all_to_all x1, starting transfers between devices, shards(): other = lax.all_to_all(other, PLANE, 0, 0, tiled=True)  7.48 us
  transfers between devices with their start and end apart: 15, of which 8 were waited for; matrix products, arithmetic and copies ran while one was open for 1% of the time, Pallas kernels for 4%

profile of v8, /device:TPU:14, one launch (start us, length us, event | category | flops | bytes accessed | tf_op | source)
XLA Modules:
  0.0 188.8 jit_solution(18068593836263540876)
XLA Ops:
  0.0 3.4 %collective-permute-start = (bf16[40,768]{1,0:T(8,128)(2,1)}, bf16[40,768]{1,0:T(8,128)(2,1)S(1)}, u32[]{:S(2)}, u32[]{:S(2)}) collective-permute-start(bf16[40,768]{1,0:T(8,128)(2,1)} %param.5), channel_id=1, source_target_pairs={{0,0},{1,1},{2,32},{3,33},{8,64},{9,65},{10,96},{11,97},{32,2},{33... | collective-permute-start | bytes 184328 | tf_op jit(solution)/shard_map/ppermute | solution.py:76
  3.4 16.3 %collective-permute-start.1 = (bf16[40,768]{1,0:T(8,128)(2,1)}, bf16[40,768]{1,0:T(8,128)(2,1)S(1)}, u32[]{:S(2)}, u32[]{:S(2)}) collective-permute-start(bf16[40,768]{1,0:T(8,128)(2,1)} %param.5), channel_id=1, source_target_pairs={{0,1},{1,0},{2,33},{3,32},{8,65},{9,64},{10,97},{11,96},{32,3},{33... | collective-permute-start | bytes 184328 | tf_op jit(solution)/shard_map/ppermute | solution.py:76
  19.7 2.0 %collective-permute-start.3 = (bf16[768,768]{1,0:T(8,128)(2,1)}, bf16[768,768]{1,0:T(8,128)(2,1)}, u32[]{:S(2)}, u32[]{:S(2)}) collective-permute-start(bf16[768,768]{1,0:T(8,128)(2,1)} %w00.2), channel_id=1, source_target_pairs={{0,64},{64,0},{1,65},{65,1},{2,66},{66,2},{3,67},{67,3},{4,68},{68... | collective-permute-start | bytes 3538952 | tf_op jit(solution)/shard_map/ppermute | solution.py:86
  21.8 1.9 %collective-permute-start.2 = (bf16[768,768]{1,0:T(8,128)(2,1)}, bf16[768,768]{1,0:T(8,128)(2,1)}, u32[]{:S(2)}, u32[]{:S(2)}) collective-permute-start(bf16[768,768]{1,0:T(8,128)(2,1)} %w00.2), channel_id=1, source_target_pairs={{0,32},{32,0},{1,33},{33,1},{2,34},{34,2},{3,35},{35,3},{4,36},{36... | collective-permute-start | bytes 3538952 | tf_op jit(solution)/shard_map/ppermute | solution.py:87
  24.7 8.1 %all-to-all-start = ((bf16[16,40,768]{2,1,0:T(8,128)(2,1)}), bf16[16,40,768]{2,1,0:T(8,128)(2,1)}, u32[]{:S(2)}, u32[]{:S(2)}) async-start(bf16[16,40,768]{2,1,0:T(8,128)(2,1)} %shard_map.55), calls=%async_computation | async-start | bytes 1966080 | tf_op jit(solution)/shard_map/all_to_all | solution.py:82
  32.8 2.7 %collective-permute-start.6 = (bf16[768,768]{1,0:T(8,128)(2,1)S(1)}, bf16[768,768]{1,0:T(8,128)(2,1)S(1)}, u32[]{:S(2)}, u32[]{:S(2)}) collective-permute-start(bf16[768,768]{1,0:T(8,128)(2,1)S(1)} %copy-done), channel_id=1, source_target_pairs={{0,64},{64,0},{1,65},{65,1},{2,66},{66,2},{3,67},{67,3},{4,68},{68... | collective-permute-start | bytes 3538952 | tf_op jit(solution)/shard_map/ppermute | solution.py:89
  36.6 10.7 %all-to-all-done.here = bf16[16,40,768]{2,1,0:T(8,128)(2,1)} async-done(((bf16[16,40,768]{2,1,0:T(8,128)(2,1)}), bf16[16,40,768]{2,1,0:T(8,128)(2,1)}, u32[]{:S(2)}, u32[]{:S(2)}) %all-to-all-start) | async-done | bytes 983072 | tf_op jit(solution)/shard_map/all_to_all | solution.py:82
  47.2 7.5 %all-to-all-start.1 = ((bf16[16,40,768]{2,1,0:T(8,128)(2,1)}), bf16[16,40,768]{2,1,0:T(8,128)(2,1)}, u32[]{:S(2)}, u32[]{:S(2)}) async-start(bf16[16,40,768]{2,1,0:T(8,128)(2,1)} %shard_map.56), calls=%async_computation.1 | async-start | bytes 1966080 | tf_op jit(solution)/shard_map/all_to_all | solution.py:84
  58.8 2.4 %collective-permute-start.5 = (bf16[384,768]{1,0:T(8,128)(2,1)S(1)}, bf16[384,768]{1,0:T(8,128)(2,1)S(1)}, u32[]{:S(2)}, u32[]{:S(2)}) collective-permute-start(bf16[384,768]{1,0:T(8,128)(2,1)S(1)} %get-tuple-element.21), channel_id=1, source_target_pairs={{0,32},{32,0},{1,33},{33,1},{2,34},{34,2},{3,35},{35,3},{4,36},{36... | collective-permute-start | bytes 1769480 | tf_op jit(solution)/shard_map/ppermute | solution.py:88
  62.9 4.8 %all-to-all-done.1.other = bf16[16,40,768]{2,1,0:T(8,128)(2,1)} async-done(((bf16[16,40,768]{2,1,0:T(8,128)(2,1)}), bf16[16,40,768]{2,1,0:T(8,128)(2,1)}, u32[]{:S(2)}, u32[]{:S(2)}) %all-to-all-start.1) | async-done | bytes 983072 | tf_op jit(solution)/shard_map/all_to_all | solution.py:84
  67.6 5.4 %shard_map.57 = bf16[4,80,768]{2,1,0:T(8,128)(2,1)} custom-call(bf16[16,40,768]{2,1,0:T(8,128)(2,1)} %all-to-all-done.here, bf16[16,40,768]{2,1,0:T(8,128)(2,1)} %all-to-all-done.1.other, bf16[768,768]{1,0:T(8,128)(2,1)} %w00.2, bf16[768,768]{1,0:T(8,128)(2,1)} %collective-permute-done.2.w01, bf16[768,768]{1,0:T(8,128)(2,1)} %collective-permute-done.3.w10, ...), custom_call_target="tpu_custom_call" | custom-call | flops 1509949440 | bytes 8388608 | tf_op jit(solution)/shard_map/pallas_call | solution.py:94
  73.0 6.7 %collective-permute-done.6.w10 = bf16[768,768]{1,0:T(8,128)(2,1)S(1)} collective-permute-done((bf16[768,768]{1,0:T(8,128)(2,1)S(1)}, bf16[768,768]{1,0:T(8,128)(2,1)S(1)}, u32[]{:S(2)}, u32[]{:S(2)}) %collective-permute-start.6) | collective-permute-done | bytes 1179680 | tf_op jit(solution)/shard_map/ppermute | solution.py:89
  79.7 3.5 %all-to-all-start.2 = ((bf16[4,80,768]{2,1,0:T(8,128)(2,1)}), bf16[4,80,768]{2,1,0:T(8,128)(2,1)S(1)}, u32[]{:S(2)}, u32[]{:S(2)}) async-start(bf16[4,80,768]{2,1,0:T(8,128)(2,1)} %shard_map.57), calls=%async_computation.2 | async-start | bytes 983040 | tf_op jit(solution)/shard_map/all_to_all | solution.py:96
  83.2 1.9 %collective-permute-start.7 = (bf16[768,768]{1,0:T(8,128)(2,1)S(1)}, bf16[768,768]{1,0:T(8,128)(2,1)}, u32[]{:S(2)}, u32[]{:S(2)}) collective-permute-start(bf16[768,768]{1,0:T(8,128)(2,1)S(1)} %copy-done), channel_id=1, source_target_pairs={{0,32},{32,0},{1,33},{33,1},{2,34},{34,2},{3,35},{35,3},{4,36},{36... | collective-permute-start | bytes 3538952 | tf_op jit(solution)/shard_map/ppermute | solution.py:90
  85.1 2.4 %collective-permute-start.8 = (bf16[768,768]{1,0:T(8,128)(2,1)S(1)}, bf16[768,768]{1,0:T(8,128)(2,1)}, u32[]{:S(2)}, u32[]{:S(2)}) collective-permute-start(bf16[768,768]{1,0:T(8,128)(2,1)S(1)} %collective-permute-done.6.w10), channel_id=1, source_target_pairs={{0,32},{32,0},{1,33},{33,1},{2,34},{34,2},{3,35},{35,3},{4,36},{36... | collective-permute-start | bytes 3538952 | tf_op jit(solution)/shard_map/ppermute | solution.py:90
  87.5 21.5 %all-to-all-done.2.parts = bf16[4,80,768]{2,1,0:T(8,128)(2,1)S(1)} async-done(((bf16[4,80,768]{2,1,0:T(8,128)(2,1)}), bf16[4,80,768]{2,1,0:T(8,128)(2,1)S(1)}, u32[]{:S(2)}, u32[]{:S(2)}) %all-to-all-start.2) | async-done | bytes 491552 | tf_op jit(solution)/shard_map/all_to_all | solution.py:96
  109.2 24.2 %all-gather = bf16[320,768]{1,0:T(8,128)(2,1)S(1)} all-gather(bf16[80,768]{1,0:T(8,128)(2,1)S(1)} %shard_map.58), channel_id=2, replica_groups=mesh['zq'=4,'zb'=2,'c'=2,'yp'=2,'y0'=2,'xp'=2,'x0'=2,'zh'=2] {'zq'}, dimensions={0}, use_global_device_ids=true | all-gather | bytes 614400 | tf_op jit(solution)/shard_map/all_gather | solution.py:98
  133.4 4.3 %shard_map.59 = (bf16[16,40,768]{2,1,0:T(8,128)(2,1)}, bf16[16,40,768]{2,1,0:T(8,128)(2,1)S(1)}) custom-call(bf16[4,80,768]{2,1,0:T(8,128)(2,1)S(1)} %bitcast.1, bf16[768,768]{1,0:T(8,128)(2,1)S(1)} %copy-done, bf16[768,768]{1,0:T(8,128)(2,1)} %collective-permute-done.7.w01, bf16[768,768]{1,0:T(8,128)(2,1)S(1)} %collective-permute-done.6.w10, ...), custom_call_target="tpu_custom_call" | custom-call | flops 1509949440 | bytes 8388608 | tf_op jit(solution)/shard_map/pallas_call | solution.py:100
  137.7 18.3 %all_to_all.25 = bf16[16,40,768]{2,1,0:T(8,128)(2,1)S(1)} all-to-all(bf16[16,40,768]{2,1,0:T(8,128)(2,1)S(1)} %get-tuple-element.18), channel_id=1, replica_groups=mesh['zq'=4,'zb'=2,'c'=2,'yp'=2,'y0'=2,'xp'=2,'x0'=2,'zh'=2] {'yp','y0',..., dimensions={0} | all-to-all | bytes 1966080 | tf_op jit(solution)/shard_map/all_to_all | solution.py:102
  156.0 7.0 %all-to-all-start.4 = ((bf16[16,40,768]{2,1,0:T(8,128)(2,1)}), bf16[16,40,768]{2,1,0:T(8,128)(2,1)S(1)}, u32[]{:S(2)}, u32[]{:S(2)}) async-start(bf16[16,40,768]{2,1,0:T(8,128)(2,1)} %get-tuple-element.20), calls=%async_computation.4 | async-start | bytes 1966080 | tf_op jit(solution)/shard_map/all_to_all | solution.py:104
  163.2 2.9 %collective-permute-start.9 = (bf16[40,768]{1,0:T(8,128)(2,1)S(1)}, bf16[40,768]{1,0:T(8,128)(2,1)S(1)}, u32[]{:S(2)}, u32[]{:S(2)}) collective-permute-start(bf16[40,768]{1,0:T(8,128)(2,1)S(1)} %reduce_sum.24), channel_id=1, source_target_pairs={{0,1},{1,0},{2,33},{3,32},{8,65},{9,64},{10,97},{11,96},{32,3},{33... | collective-permute-start | bytes 184328 | tf_op jit(solution)/shard_map/ppermute | solution.py:108
  166.1 7.0 %all-to-all-done.4 = bf16[16,40,768]{2,1,0:T(8,128)(2,1)S(1)} async-done(((bf16[16,40,768]{2,1,0:T(8,128)(2,1)}), bf16[16,40,768]{2,1,0:T(8,128)(2,1)S(1)}, u32[]{:S(2)}, u32[]{:S(2)}) %all-to-all-start.4) | async-done | bytes 983072 | tf_op jit(solution)/shard_map/all_to_all | solution.py:104
  173.3 2.3 %collective-permute-start.10 = (bf16[40,768]{1,0:T(8,128)(2,1)S(1)}, bf16[40,768]{1,0:T(8,128)(2,1)S(1)}, u32[]{:S(2)}, u32[]{:S(2)}) collective-permute-start(bf16[40,768]{1,0:T(8,128)(2,1)S(1)} %reduce_sum.25), channel_id=1, source_target_pairs={{0,0},{1,1},{2,32},{3,33},{8,64},{9,65},{10,96},{11,97},{32,2},{33... | collective-permute-start | bytes 184328 | tf_op jit(solution)/shard_map/ppermute | solution.py:108
  175.6 12.5 %collective-permute-done.9 = bf16[40,768]{1,0:T(8,128)(2,1)S(1)} collective-permute-done((bf16[40,768]{1,0:T(8,128)(2,1)S(1)}, bf16[40,768]{1,0:T(8,128)(2,1)S(1)}, u32[]{:S(2)}, u32[]{:S(2)}) %collective-permute-start.9) | collective-permute-done | bytes 61472 | tf_op jit(solution)/shard_map/ppermute | solution.py:108
  (29 shorter events, 8.9 us)
Async XLA Ops:
  0.0 19.7 %collective-permute-start = (bf16[40,768]{1,0:T(8,128)(2,1)}, bf16[40,768]{1,0:T(8,128)(2,1)S(1)}, u32[]{:S(2)}, u32[]{:S(2)}) collective-permute-start(bf16[40,768]{1,0:T(8,128)(2,1)} %param.5), channel_id=1, source_target_pairs={{0,0},{1,1},{2,32},{3,33},{8,64},{9,65},{10,96},{11,97},{32,2},{33... | collective-permute-start | bytes 184328 | tf_op jit(solution)/shard_map/ppermute | solution.py:76
  3.4 32.1 %collective-permute-start.1 = (bf16[40,768]{1,0:T(8,128)(2,1)}, bf16[40,768]{1,0:T(8,128)(2,1)S(1)}, u32[]{:S(2)}, u32[]{:S(2)}) collective-permute-start(bf16[40,768]{1,0:T(8,128)(2,1)} %param.5), channel_id=1, source_target_pairs={{0,1},{1,0},{2,33},{3,32},{8,65},{9,64},{10,97},{11,96},{32,3},{33... | collective-permute-start | bytes 184328 | tf_op jit(solution)/shard_map/ppermute | solution.py:76
  19.7 35.8 %collective-permute-start.3 = (bf16[768,768]{1,0:T(8,128)(2,1)}, bf16[768,768]{1,0:T(8,128)(2,1)}, u32[]{:S(2)}, u32[]{:S(2)}) collective-permute-start(bf16[768,768]{1,0:T(8,128)(2,1)} %w00.2), channel_id=1, source_target_pairs={{0,64},{64,0},{1,65},{65,1},{2,66},{66,2},{3,67},{67,3},{4,68},{68... | collective-permute-start | bytes 3538952 | tf_op jit(solution)/shard_map/ppermute | solution.py:86
  21.8 39.5 %collective-permute-start.2 = (bf16[768,768]{1,0:T(8,128)(2,1)}, bf16[768,768]{1,0:T(8,128)(2,1)}, u32[]{:S(2)}, u32[]{:S(2)}) collective-permute-start(bf16[768,768]{1,0:T(8,128)(2,1)} %w00.2), channel_id=1, source_target_pairs={{0,32},{32,0},{1,33},{33,1},{2,34},{34,2},{3,35},{35,3},{4,36},{36... | collective-permute-start | bytes 3538952 | tf_op jit(solution)/shard_map/ppermute | solution.py:87
  24.7 8.1 %copy-start = (bf16[768,768]{1,0:T(8,128)(2,1)S(1)}, bf16[768,768]{1,0:T(8,128)(2,1)}, u32[]{:S(2)}) copy-start(bf16[768,768]{1,0:T(8,128)(2,1)} %w00.3) | copy-start | bytes 3538948
  24.7 22.5 %all-to-all-start = ((bf16[16,40,768]{2,1,0:T(8,128)(2,1)}), bf16[16,40,768]{2,1,0:T(8,128)(2,1)}, u32[]{:S(2)}, u32[]{:S(2)}) async-start(bf16[16,40,768]{2,1,0:T(8,128)(2,1)} %shard_map.55), calls=%async_computation | async-start | bytes 1966080 | tf_op jit(solution)/shard_map/all_to_all | solution.py:82
  32.8 46.9 %collective-permute-start.6 = (bf16[768,768]{1,0:T(8,128)(2,1)S(1)}, bf16[768,768]{1,0:T(8,128)(2,1)S(1)}, u32[]{:S(2)}, u32[]{:S(2)}) collective-permute-start(bf16[768,768]{1,0:T(8,128)(2,1)S(1)} %copy-done), channel_id=1, source_target_pairs={{0,64},{64,0},{1,65},{65,1},{2,66},{66,2},{3,67},{67,3},{4,68},{68... | collective-permute-start | bytes 3538952 | tf_op jit(solution)/shard_map/ppermute | solution.py:89
  47.2 20.4 %all-to-all-start.1 = ((bf16[16,40,768]{2,1,0:T(8,128)(2,1)}), bf16[16,40,768]{2,1,0:T(8,128)(2,1)}, u32[]{:S(2)}, u32[]{:S(2)}) async-start(bf16[16,40,768]{2,1,0:T(8,128)(2,1)} %shard_map.56), calls=%async_computation.1 | async-start | bytes 1966080 | tf_op jit(solution)/shard_map/all_to_all | solution.py:84
  56.9 4.4 %collective-permute-start.4 = (bf16[384,768]{1,0:T(8,128)(2,1)S(1)}, bf16[384,768]{1,0:T(8,128)(2,1)S(1)}, u32[]{:S(2)}, u32[]{:S(2)}) collective-permute-start(bf16[384,768]{1,0:T(8,128)(2,1)S(1)} %get-tuple-element.22), channel_id=1, source_target_pairs={{0,32},{32,0},{1,33},{33,1},{2,34},{34,2},{3,35},{35,3},{4,36},{36... | collective-permute-start | bytes 1769480 | tf_op jit(solution)/shard_map/ppermute | solution.py:88
  58.8 28.7 %copy-start.4 = (bf16[768]{0:T(1024)(128)(2,1)S(1)}, bf16[768]{0:T(1024)(128)(2,1)}, u32[]{:S(2)}) copy-start(bf16[768]{0:T(1024)(128)(2,1)} %param.7) | copy-start | bytes 4612
  58.8 4.0 %collective-permute-start.5 = (bf16[384,768]{1,0:T(8,128)(2,1)S(1)}, bf16[384,768]{1,0:T(8,128)(2,1)S(1)}, u32[]{:S(2)}, u32[]{:S(2)}) collective-permute-start(bf16[384,768]{1,0:T(8,128)(2,1)S(1)} %get-tuple-element.21), channel_id=1, source_target_pairs={{0,32},{32,0},{1,33},{33,1},{2,34},{34,2},{3,35},{35,3},{4,36},{36... | collective-permute-start | bytes 1769480 | tf_op jit(solution)/shard_map/ppermute | solution.py:88
  61.3 6.4 %copy-start.1 = (bf16[384,768]{1,0:T(8,128)(2,1)}, bf16[384,768]{1,0:T(8,128)(2,1)S(1)}, u32[]{:S(2)}) copy-start(bf16[384,768]{1,0:T(8,128)(2,1)S(1)} %collective-permute-done.4.w11a) | copy-start | bytes 1769476
  62.9 4.8 %copy-start.2 = (bf16[384,768]{1,0:T(8,128)(2,1)}, bf16[384,768]{1,0:T(8,128)(2,1)S(1)}, u32[]{:S(2)}) copy-start(bf16[384,768]{1,0:T(8,128)(2,1)S(1)} %collective-permute-done.5.w11b) | copy-start | bytes 1769476
  79.7 29.3 %all-to-all-start.2 = ((bf16[4,80,768]{2,1,0:T(8,128)(2,1)}), bf16[4,80,768]{2,1,0:T(8,128)(2,1)S(1)}, u32[]{:S(2)}, u32[]{:S(2)}) async-start(bf16[4,80,768]{2,1,0:T(8,128)(2,1)} %shard_map.57), calls=%async_computation.2 | async-start | bytes 983040 | tf_op jit(solution)/shard_map/all_to_all | solution.py:96
  83.2 50.3 %collective-permute-start.7 = (bf16[768,768]{1,0:T(8,128)(2,1)S(1)}, bf16[768,768]{1,0:T(8,128)(2,1)}, u32[]{:S(2)}, u32[]{:S(2)}) collective-permute-start(bf16[768,768]{1,0:T(8,128)(2,1)S(1)} %copy-done), channel_id=1, source_target_pairs={{0,32},{32,0},{1,33},{33,1},{2,34},{34,2},{3,35},{35,3},{4,36},{36... | collective-permute-start | bytes 3538952 | tf_op jit(solution)/shard_map/ppermute | solution.py:90
  85.1 48.3 %collective-permute-start.8 = (bf16[768,768]{1,0:T(8,128)(2,1)S(1)}, bf16[768,768]{1,0:T(8,128)(2,1)}, u32[]{:S(2)}, u32[]{:S(2)}) collective-permute-start(bf16[768,768]{1,0:T(8,128)(2,1)S(1)} %collective-permute-done.6.w10), channel_id=1, source_target_pairs={{0,32},{32,0},{1,33},{33,1},{2,34},{34,2},{3,35},{35,3},{4,36},{36... | collective-permute-start | bytes 3538952 | tf_op jit(solution)/shard_map/ppermute | solution.py:90
  156.0 17.1 %all-to-all-start.4 = ((bf16[16,40,768]{2,1,0:T(8,128)(2,1)}), bf16[16,40,768]{2,1,0:T(8,128)(2,1)S(1)}, u32[]{:S(2)}, u32[]{:S(2)}) async-start(bf16[16,40,768]{2,1,0:T(8,128)(2,1)} %get-tuple-element.20), calls=%async_computation.4 | async-start | bytes 1966080 | tf_op jit(solution)/shard_map/all_to_all | solution.py:104
  163.0 12.6 %copy-start.3 = (bf16[768]{0:T(1024)(128)(2,1)S(1)}, bf16[768]{0:T(1024)(128)(2,1)}, u32[]{:S(2)}) copy-start(bf16[768]{0:T(1024)(128)(2,1)} %param.9) | copy-start | bytes 4612
  163.2 25.0 %collective-permute-start.9 = (bf16[40,768]{1,0:T(8,128)(2,1)S(1)}, bf16[40,768]{1,0:T(8,128)(2,1)S(1)}, u32[]{:S(2)}, u32[]{:S(2)}) collective-permute-start(bf16[40,768]{1,0:T(8,128)(2,1)S(1)} %reduce_sum.24), channel_id=1, source_target_pairs={{0,1},{1,0},{2,33},{3,32},{8,65},{9,64},{10,97},{11,96},{32,3},{33... | collective-permute-start | bytes 184328 | tf_op jit(solution)/shard_map/ppermute | solution.py:108
  173.3 14.9 %collective-permute-start.10 = (bf16[40,768]{1,0:T(8,128)(2,1)S(1)}, bf16[40,768]{1,0:T(8,128)(2,1)S(1)}, u32[]{:S(2)}, u32[]{:S(2)}) collective-permute-start(bf16[40,768]{1,0:T(8,128)(2,1)S(1)} %reduce_sum.25), channel_id=1, source_target_pairs={{0,0},{1,1},{2,32},{3,33},{8,64},{9,65},{10,96},{11,97},{32,2},{33... | collective-permute-start | bytes 184328 | tf_op jit(solution)/shard_map/ppermute | solution.py:108

commit v9 on v7

--- a/solution.py
+++ b/solution.py
@@ -80,18 +80,19 @@
     (here,) = kernel_call(spread_kernel, shape, 1, 10**9, 1 << 20)(here)
     (other,) = kernel_call(spread_kernel, shape, 1, 40 * 10**9, 1 << 20)(other)
     here = lax.all_to_all(here, PLANE, 0, 0, tiled=True)
+    w1_late, _ = barrier((w1, other))
     other, _ = barrier((other, here))
     other = lax.all_to_all(other, PLANE, 0, 0, tiled=True)
 
     w1_z = lax.ppermute(w1_in, "zb", SWAP)
-    w1_all = [w1, lax.ppermute(w1_in, "c", SWAP), w1_z]
+    w1_all = [w1, lax.ppermute(w1_late, "c", SWAP), w1_z]
     w1_all += [lax.ppermute(w1_z[at : at + 384], "c", SWAP) for at in (0, 384)]
     w2_z = lax.ppermute(w2_in, "zb", SWAP)
     w2_all = [w2, lax.ppermute(w2_in, "c", SWAP), w2_z, lax.ppermute(w2_z, "c", SWAP)]
 
     flops = 2 * 320 * 3072 * 768
     scratch = [pltpu.VMEM((320, 768), F32)]
-    (part,) = kernel_call(first_kernel, [(4, 80, 768)], 7, flops, 8 << 20, scratch, 54)(here, other, *w1_all)
+    (part,) = kernel_call(first_kernel, [(4, 80, 768)], 7, flops, 8 << 20, scratch, 50)(here, other, *w1_all)
     part = lax.all_to_all(part, "zq", 0, 0, tiled=True)
     (h,) = kernel_call(middle_kernel, [(80, 768)], 2, 20 * 80 * 768, 1 << 20)(part, b1.reshape(1, 768))
     hidden = lax.all_gather(h, "zq", axis=0, tiled=False)

time: 185 us -> 187 us (1.011)
  waiting for transfers between devices: 64 us -> 69.3 us
    all_to_all x2, waiting for transfers between devices: 21.8 us -> 18.6 us  [shards(): here = lax.all_to_all(here, PLANE, 0, 0, tiled=True)]
    ppermute x2, waiting for transfers between devices: 9.41 us -> 12.3 us  [shards(): total = total + lax.ppermute(out, CORNER, corner_pairs(k)).astype(F32)]
    ppermute x1, waiting for transfers between devices: 16.6 us -> 19.1 us  [shards(): w2_z = lax.ppermute(w2_in, 'zb', SWAP)]
  transfers between devices with their start and end apart: 15 -> 15, of which waited for: 6 -> 8; matrix products, arithmetic and copies ran while one was open for 0% -> 0% of each run, Pallas kernels for 4% -> 4%
where the time goes in v9:
time: 187 us; the launch traced here: 186 us
  waiting for transfers between devices  69.3 us (37%)
  starting transfers between devices  62.1 us (33%)
  blocking collectives  41.8 us (22%)
  Pallas kernels  11 us (6%)
    all_gather x1, blocking collectives, shards(): hidden = lax.all_gather(h, 'zq', axis=0, tiled=False)  23.5 us
    ppermute x1, waiting for transfers between devices, shards(): w2_z = lax.ppermute(w2_in, 'zb', SWAP)  19.1 us
    ppermute x2, starting transfers between devices, shards(): lax.ppermute(tokens, CORNER, corner_pairs(k))  18.8 us
    all_to_all x2, waiting for transfers between devices, shards(): here = lax.all_to_all(here, PLANE, 0, 0, tiled=True)  18.6 us
    all_to_all x1, blocking collectives, shards(): other = lax.all_to_all(other, PLANE, 0, 0, tiled=True)  18.2 us
    all_to_all x2, starting transfers between devices, shards(): here = lax.all_to_all(here, PLANE, 0, 0, tiled=True)  14.2 us
    all_to_all x1, waiting for transfers between devices, shards(): part = lax.all_to_all(part, 'zq', 0, 0, tiled=True)  13.3 us
    ppermute x2, waiting for transfers between devices, shards(): total = total + lax.ppermute(out, CORNER, corner_pairs(k)).astype(F32)  12.3 us
  transfers between devices with their start and end apart: 15, of which 8 were waited for; matrix products, arithmetic and copies ran while one was open for 0% of the time, Pallas kernels for 4%

profile of v9, /device:TPU:38, one launch (start us, length us, event | category | flops | bytes accessed | tf_op | source)
XLA Modules:
  0.0 186.3 jit_solution(17505608049112240390)
XLA Ops:
  0.0 2.7 %collective-permute-start = (bf16[40,768]{1,0:T(8,128)(2,1)}, bf16[40,768]{1,0:T(8,128)(2,1)S(1)}, u32[]{:S(2)}, u32[]{:S(2)}) collective-permute-start(bf16[40,768]{1,0:T(8,128)(2,1)} %param.5), channel_id=1, source_target_pairs={{0,0},{1,1},{2,32},{3,33},{8,64},{9,65},{10,96},{11,97},{32,2},{33... | collective-permute-start | bytes 184328 | tf_op jit(solution)/shard_map/ppermute | solution.py:76
  2.7 16.1 %collective-permute-start.1 = (bf16[40,768]{1,0:T(8,128)(2,1)}, bf16[40,768]{1,0:T(8,128)(2,1)S(1)}, u32[]{:S(2)}, u32[]{:S(2)}) collective-permute-start(bf16[40,768]{1,0:T(8,128)(2,1)} %param.5), channel_id=1, source_target_pairs={{0,1},{1,0},{2,33},{3,32},{8,65},{9,64},{10,97},{11,96},{32,3},{33... | collective-permute-start | bytes 184328 | tf_op jit(solution)/shard_map/ppermute | solution.py:76
  18.8 2.0 %collective-permute-start.3 = (bf16[768,768]{1,0:T(8,128)(2,1)}, bf16[768,768]{1,0:T(8,128)(2,1)S(1)}, u32[]{:S(2)}, u32[]{:S(2)}) collective-permute-start(bf16[768,768]{1,0:T(8,128)(2,1)} %w00.2), channel_id=1, source_target_pairs={{0,64},{64,0},{1,65},{65,1},{2,66},{66,2},{3,67},{67,3},{4,68},{68... | collective-permute-start | bytes 3538952 | tf_op jit(solution)/shard_map/ppermute | solution.py:87
  21.9 7.9 %all-to-all-start = ((bf16[16,40,768]{2,1,0:T(8,128)(2,1)}), bf16[16,40,768]{2,1,0:T(8,128)(2,1)S(1)}, u32[]{:S(2)}, u32[]{:S(2)}) async-start(bf16[16,40,768]{2,1,0:T(8,128)(2,1)} %shard_map.55), calls=%async_computation | async-start | bytes 1966080 | tf_op jit(solution)/shard_map/all_to_all | solution.py:82
  31.3 1.9 %collective-permute-start.2 = (bf16[768,768]{1,0:T(8,128)(2,1)}, bf16[768,768]{1,0:T(8,128)(2,1)}, u32[]{:S(2)}, u32[]{:S(2)}) collective-permute-start(bf16[768,768]{1,0:T(8,128)(2,1)} %w00.2), channel_id=1, source_target_pairs={{0,32},{32,0},{1,33},{33,1},{2,34},{34,2},{3,35},{35,3},{4,36},{36... | collective-permute-start | bytes 3538952 | tf_op jit(solution)/shard_map/ppermute | solution.py:88
  33.2 10.3 %all-to-all-done.here = bf16[16,40,768]{2,1,0:T(8,128)(2,1)S(1)} async-done(((bf16[16,40,768]{2,1,0:T(8,128)(2,1)}), bf16[16,40,768]{2,1,0:T(8,128)(2,1)S(1)}, u32[]{:S(2)}, u32[]{:S(2)}) %all-to-all-start) | async-done | bytes 983072 | tf_op jit(solution)/shard_map/all_to_all | solution.py:82
  43.6 6.6 %all-to-all-start.1 = ((bf16[16,40,768]{2,1,0:T(8,128)(2,1)}), bf16[16,40,768]{2,1,0:T(8,128)(2,1)S(1)}, u32[]{:S(2)}, u32[]{:S(2)}) async-start(bf16[16,40,768]{2,1,0:T(8,128)(2,1)} %shard_map.56), calls=%async_computation.1 | async-start | bytes 1966080 | tf_op jit(solution)/shard_map/all_to_all | solution.py:85
  52.9 1.9 %collective-permute-start.4 = (bf16[384,768]{1,0:T(8,128)(2,1)S(1)}, bf16[384,768]{1,0:T(8,128)(2,1)S(1)}, u32[]{:S(2)}, u32[]{:S(2)}) collective-permute-start(bf16[384,768]{1,0:T(8,128)(2,1)S(1)} %get-tuple-element.22), channel_id=1, source_target_pairs={{0,32},{32,0},{1,33},{33,1},{2,34},{34,2},{3,35},{35,3},{4,36},{36... | collective-permute-start | bytes 1769480 | tf_op jit(solution)/shard_map/ppermute | solution.py:89
  54.9 2.4 %collective-permute-start.5 = (bf16[384,768]{1,0:T(8,128)(2,1)S(1)}, bf16[384,768]{1,0:T(8,128)(2,1)S(1)}, u32[]{:S(2)}, u32[]{:S(2)}) collective-permute-start(bf16[384,768]{1,0:T(8,128)(2,1)S(1)} %get-tuple-element.21), channel_id=1, source_target_pairs={{0,32},{32,0},{1,33},{33,1},{2,34},{34,2},{3,35},{35,3},{4,36},{36... | collective-permute-start | bytes 1769480 | tf_op jit(solution)/shard_map/ppermute | solution.py:89
  57.3 1.9 %collective-permute-start.7 = (bf16[768,768]{1,0:T(8,128)(2,1)}, bf16[768,768]{1,0:T(8,128)(2,1)}, u32[]{:S(2)}, u32[]{:S(2)}) collective-permute-start(bf16[768,768]{1,0:T(8,128)(2,1)} %w00.3), channel_id=1, source_target_pairs={{0,64},{64,0},{1,65},{65,1},{2,66},{66,2},{3,67},{67,3},{4,68},{68... | collective-permute-start | bytes 3538952 | tf_op jit(solution)/shard_map/ppermute | solution.py:90
  59.2 3.7 %all-to-all-done.1.other = bf16[16,40,768]{2,1,0:T(8,128)(2,1)S(1)} async-done(((bf16[16,40,768]{2,1,0:T(8,128)(2,1)}), bf16[16,40,768]{2,1,0:T(8,128)(2,1)S(1)}, u32[]{:S(2)}, u32[]{:S(2)}) %all-to-all-start.1) | async-done | bytes 983072 | tf_op jit(solution)/shard_map/all_to_all | solution.py:85
  62.9 4.5 %shard_map.57 = bf16[4,80,768]{2,1,0:T(8,128)(2,1)} custom-call(bf16[16,40,768]{2,1,0:T(8,128)(2,1)S(1)} %all-to-all-done.here, bf16[16,40,768]{2,1,0:T(8,128)(2,1)S(1)} %all-to-all-done.1.other, bf16[768,768]{1,0:T(8,128)(2,1)} %w00.2, bf16[768,768]{1,0:T(8,128)(2,1)} %collective-permute-done.2.w01, bf16[768,768]{1,0:T(8,128)(2,1)} %copy-done, ...), custom_call_target="tpu_custom_call" | custom-call | flops 1509949440 | bytes 8388608 | tf_op jit(solution)/shard_map/pallas_call | solution.py:95
  67.4 4.7 %all-to-all-start.2 = ((bf16[4,80,768]{2,1,0:T(8,128)(2,1)}), bf16[4,80,768]{2,1,0:T(8,128)(2,1)S(1)}, u32[]{:S(2)}, u32[]{:S(2)}) async-start(bf16[4,80,768]{2,1,0:T(8,128)(2,1)} %shard_map.57), calls=%async_computation.2 | async-start | bytes 983040 | tf_op jit(solution)/shard_map/all_to_all | solution.py:96
  72.1 1.9 %collective-permute-start.6 = (bf16[768,768]{1,0:T(8,128)(2,1)}, bf16[768,768]{1,0:T(8,128)(2,1)S(1)}, u32[]{:S(2)}, u32[]{:S(2)}) collective-permute-start(bf16[768,768]{1,0:T(8,128)(2,1)} %w00.3), channel_id=1, source_target_pairs={{0,32},{32,0},{1,33},{33,1},{2,34},{34,2},{3,35},{35,3},{4,36},{36... | collective-permute-start | bytes 3538952 | tf_op jit(solution)/shard_map/ppermute | solution.py:91
  74.0 19.1 %collective-permute-done.7.w10 = bf16[768,768]{1,0:T(8,128)(2,1)} collective-permute-done((bf16[768,768]{1,0:T(8,128)(2,1)}, bf16[768,768]{1,0:T(8,128)(2,1)}, u32[]{:S(2)}, u32[]{:S(2)}) %collective-permute-start.7) | collective-permute-done | bytes 1179680 | tf_op jit(solution)/shard_map/ppermute | solution.py:90
  95.0 13.3 %all-to-all-done.2.parts = bf16[4,80,768]{2,1,0:T(8,128)(2,1)S(1)} async-done(((bf16[4,80,768]{2,1,0:T(8,128)(2,1)}), bf16[4,80,768]{2,1,0:T(8,128)(2,1)S(1)}, u32[]{:S(2)}, u32[]{:S(2)}) %all-to-all-start.2) | async-done | bytes 491552 | tf_op jit(solution)/shard_map/all_to_all | solution.py:96
  108.5 23.5 %all-gather = bf16[320,768]{1,0:T(8,128)(2,1)S(1)} all-gather(bf16[80,768]{1,0:T(8,128)(2,1)S(1)} %shard_map.58), channel_id=2, replica_groups=mesh['zq'=4,'zb'=2,'c'=2,'yp'=2,'y0'=2,'xp'=2,'x0'=2,'zh'=2] {'zq'}, dimensions={0}, use_global_device_ids=true | all-gather | bytes 614400 | tf_op jit(solution)/shard_map/all_gather | solution.py:98
  132.0 4.3 %shard_map.59 = (bf16[16,40,768]{2,1,0:T(8,128)(2,1)}, bf16[16,40,768]{2,1,0:T(8,128)(2,1)S(1)}) custom-call(bf16[4,80,768]{2,1,0:T(8,128)(2,1)S(1)} %bitcast.1, bf16[768,768]{1,0:T(8,128)(2,1)} %w00.3, bf16[768,768]{1,0:T(8,128)(2,1)S(1)} %collective-permute-done.6.w01, bf16[768,768]{1,0:T(8,128)(2,1)} %collective-permute-done.7.w10, ...), custom_call_target="tpu_custom_call" | custom-call | flops 1509949440 | bytes 8388608 | tf_op jit(solution)/shard_map/pallas_call | solution.py:100
  136.3 18.2 %all_to_all.25 = bf16[16,40,768]{2,1,0:T(8,128)(2,1)S(1)} all-to-all(bf16[16,40,768]{2,1,0:T(8,128)(2,1)S(1)} %get-tuple-element.18), channel_id=1, replica_groups=mesh['zq'=4,'zb'=2,'c'=2,'yp'=2,'y0'=2,'xp'=2,'x0'=2,'zh'=2] {'yp','y0',..., dimensions={0} | all-to-all | bytes 1966080 | tf_op jit(solution)/shard_map/all_to_all | solution.py:102
  154.6 6.3 %all-to-all-start.4 = ((bf16[16,40,768]{2,1,0:T(8,128)(2,1)}), bf16[16,40,768]{2,1,0:T(8,128)(2,1)S(1)}, u32[]{:S(2)}, u32[]{:S(2)}) async-start(bf16[16,40,768]{2,1,0:T(8,128)(2,1)} %get-tuple-element.20), calls=%async_computation.4 | async-start | bytes 1966080 | tf_op jit(solution)/shard_map/all_to_all | solution.py:104
  161.0 1.9 %collective-permute-start.9 = (bf16[40,768]{1,0:T(8,128)(2,1)S(1)}, bf16[40,768]{1,0:T(8,128)(2,1)S(1)}, u32[]{:S(2)}, u32[]{:S(2)}) collective-permute-start(bf16[40,768]{1,0:T(8,128)(2,1)S(1)} %reduce_sum.24), channel_id=1, source_target_pairs={{0,1},{1,0},{2,33},{3,32},{8,65},{9,64},{10,97},{11,96},{32,3},{33... | collective-permute-start | bytes 184328 | tf_op jit(solution)/shard_map/ppermute | solution.py:108
  163.0 8.3 %all-to-all-done.4 = bf16[16,40,768]{2,1,0:T(8,128)(2,1)S(1)} async-done(((bf16[16,40,768]{2,1,0:T(8,128)(2,1)}), bf16[16,40,768]{2,1,0:T(8,128)(2,1)S(1)}, u32[]{:S(2)}, u32[]{:S(2)}) %all-to-all-start.4) | async-done | bytes 983072 | tf_op jit(solution)/shard_map/all_to_all | solution.py:104
  171.4 1.9 %collective-permute-start.10 = (bf16[40,768]{1,0:T(8,128)(2,1)S(1)}, bf16[40,768]{1,0:T(8,128)(2,1)S(1)}, u32[]{:S(2)}, u32[]{:S(2)}) collective-permute-start(bf16[40,768]{1,0:T(8,128)(2,1)S(1)} %reduce_sum.25), channel_id=1, source_target_pairs={{0,0},{1,1},{2,32},{3,33},{8,64},{9,65},{10,96},{11,97},{32,2},{33... | collective-permute-start | bytes 184328 | tf_op jit(solution)/shard_map/ppermute | solution.py:108
  173.3 12.3 %collective-permute-done.9 = bf16[40,768]{1,0:T(8,128)(2,1)S(1)} collective-permute-done((bf16[40,768]{1,0:T(8,128)(2,1)S(1)}, bf16[40,768]{1,0:T(8,128)(2,1)S(1)}, u32[]{:S(2)}, u32[]{:S(2)}) %collective-permute-start.9) | collective-permute-done | bytes 61472 | tf_op jit(solution)/shard_map/ppermute | solution.py:108
  (25 shorter events, 8.4 us)
Async XLA Ops:
  0.0 18.8 %collective-permute-start = (bf16[40,768]{1,0:T(8,128)(2,1)}, bf16[40,768]{1,0:T(8,128)(2,1)S(1)}, u32[]{:S(2)}, u32[]{:S(2)}) collective-permute-start(bf16[40,768]{1,0:T(8,128)(2,1)} %param.5), channel_id=1, source_target_pairs={{0,0},{1,1},{2,32},{3,33},{8,64},{9,65},{10,96},{11,97},{32,2},{33... | collective-permute-start | bytes 184328 | tf_op jit(solution)/shard_map/ppermute | solution.py:76
  2.7 27.6 %collective-permute-start.1 = (bf16[40,768]{1,0:T(8,128)(2,1)}, bf16[40,768]{1,0:T(8,128)(2,1)S(1)}, u32[]{:S(2)}, u32[]{:S(2)}) collective-permute-start(bf16[40,768]{1,0:T(8,128)(2,1)} %param.5), channel_id=1, source_target_pairs={{0,1},{1,0},{2,33},{3,32},{8,65},{9,64},{10,97},{11,96},{32,3},{33... | collective-permute-start | bytes 184328 | tf_op jit(solution)/shard_map/ppermute | solution.py:76
  18.8 33.1 %collective-permute-start.3 = (bf16[768,768]{1,0:T(8,128)(2,1)}, bf16[768,768]{1,0:T(8,128)(2,1)S(1)}, u32[]{:S(2)}, u32[]{:S(2)}) collective-permute-start(bf16[768,768]{1,0:T(8,128)(2,1)} %w00.2), channel_id=1, source_target_pairs={{0,64},{64,0},{1,65},{65,1},{2,66},{66,2},{3,67},{67,3},{4,68},{68... | collective-permute-start | bytes 3538952 | tf_op jit(solution)/shard_map/ppermute | solution.py:87
  21.9 21.7 %all-to-all-start = ((bf16[16,40,768]{2,1,0:T(8,128)(2,1)}), bf16[16,40,768]{2,1,0:T(8,128)(2,1)S(1)}, u32[]{:S(2)}, u32[]{:S(2)}) async-start(bf16[16,40,768]{2,1,0:T(8,128)(2,1)} %shard_map.55), calls=%async_computation | async-start | bytes 1966080 | tf_op jit(solution)/shard_map/all_to_all | solution.py:82
  31.3 27.9 %collective-permute-start.2 = (bf16[768,768]{1,0:T(8,128)(2,1)}, bf16[768,768]{1,0:T(8,128)(2,1)}, u32[]{:S(2)}, u32[]{:S(2)}) collective-permute-start(bf16[768,768]{1,0:T(8,128)(2,1)} %w00.2), channel_id=1, source_target_pairs={{0,32},{32,0},{1,33},{33,1},{2,34},{34,2},{3,35},{35,3},{4,36},{36... | collective-permute-start | bytes 3538952 | tf_op jit(solution)/shard_map/ppermute | solution.py:88
  43.6 19.4 %all-to-all-start.1 = ((bf16[16,40,768]{2,1,0:T(8,128)(2,1)}), bf16[16,40,768]{2,1,0:T(8,128)(2,1)S(1)}, u32[]{:S(2)}, u32[]{:S(2)}) async-start(bf16[16,40,768]{2,1,0:T(8,128)(2,1)} %shard_map.56), calls=%async_computation.1 | async-start | bytes 1966080 | tf_op jit(solution)/shard_map/all_to_all | solution.py:85
  51.9 1.1 copy-start
  52.9 6.3 %collective-permute-start.4 = (bf16[384,768]{1,0:T(8,128)(2,1)S(1)}, bf16[384,768]{1,0:T(8,128)(2,1)S(1)}, u32[]{:S(2)}, u32[]{:S(2)}) collective-permute-start(bf16[384,768]{1,0:T(8,128)(2,1)S(1)} %get-tuple-element.22), channel_id=1, source_target_pairs={{0,32},{32,0},{1,33},{33,1},{2,34},{34,2},{3,35},{35,3},{4,36},{36... | collective-permute-start | bytes 1769480 | tf_op jit(solution)/shard_map/ppermute | solution.py:89
  54.9 40.2 %copy-start.2 = (bf16[768]{0:T(1024)(128)(2,1)S(1)}, bf16[768]{0:T(1024)(128)(2,1)}, u32[]{:S(2)}) copy-start(bf16[768]{0:T(1024)(128)(2,1)} %param.7) | copy-start | bytes 4612
  54.9 4.4 %collective-permute-start.5 = (bf16[384,768]{1,0:T(8,128)(2,1)S(1)}, bf16[384,768]{1,0:T(8,128)(2,1)S(1)}, u32[]{:S(2)}, u32[]{:S(2)}) collective-permute-start(bf16[384,768]{1,0:T(8,128)(2,1)S(1)} %get-tuple-element.21), channel_id=1, source_target_pairs={{0,32},{32,0},{1,33},{33,1},{2,34},{34,2},{3,35},{35,3},{4,36},{36... | collective-permute-start | bytes 1769480 | tf_op jit(solution)/shard_map/ppermute | solution.py:89
  57.3 35.8 %collective-permute-start.7 = (bf16[768,768]{1,0:T(8,128)(2,1)}, bf16[768,768]{1,0:T(8,128)(2,1)}, u32[]{:S(2)}, u32[]{:S(2)}) collective-permute-start(bf16[768,768]{1,0:T(8,128)(2,1)} %w00.3), channel_id=1, source_target_pairs={{0,64},{64,0},{1,65},{65,1},{2,66},{66,2},{3,67},{67,3},{4,68},{68... | collective-permute-start | bytes 3538952 | tf_op jit(solution)/shard_map/ppermute | solution.py:90
  67.4 40.9 %all-to-all-start.2 = ((bf16[4,80,768]{2,1,0:T(8,128)(2,1)}), bf16[4,80,768]{2,1,0:T(8,128)(2,1)S(1)}, u32[]{:S(2)}, u32[]{:S(2)}) async-start(bf16[4,80,768]{2,1,0:T(8,128)(2,1)} %shard_map.57), calls=%async_computation.2 | async-start | bytes 983040 | tf_op jit(solution)/shard_map/all_to_all | solution.py:96
  72.1 59.9 %collective-permute-start.6 = (bf16[768,768]{1,0:T(8,128)(2,1)}, bf16[768,768]{1,0:T(8,128)(2,1)S(1)}, u32[]{:S(2)}, u32[]{:S(2)}) collective-permute-start(bf16[768,768]{1,0:T(8,128)(2,1)} %w00.3), channel_id=1, source_target_pairs={{0,32},{32,0},{1,33},{33,1},{2,34},{34,2},{3,35},{35,3},{4,36},{36... | collective-permute-start | bytes 3538952 | tf_op jit(solution)/shard_map/ppermute | solution.py:91
  93.1 38.9 %collective-permute-start.8 = (bf16[768,768]{1,0:T(8,128)(2,1)}, bf16[768,768]{1,0:T(8,128)(2,1)S(1)}, u32[]{:S(2)}, u32[]{:S(2)}) collective-permute-start(bf16[768,768]{1,0:T(8,128)(2,1)} %collective-permute-done.7.w10), channel_id=1, source_target_pairs={{0,32},{32,0},{1,33},{33,1},{2,34},{34,2},{3,35},{35,3},{4,36},{36... | collective-permute-start | bytes 3538952 | tf_op jit(solution)/shard_map/ppermute | solution.py:91
  154.6 16.6 %all-to-all-start.4 = ((bf16[16,40,768]{2,1,0:T(8,128)(2,1)}), bf16[16,40,768]{2,1,0:T(8,128)(2,1)S(1)}, u32[]{:S(2)}, u32[]{:S(2)}) async-start(bf16[16,40,768]{2,1,0:T(8,128)(2,1)} %get-tuple-element.20), calls=%async_computation.4 | async-start | bytes 1966080 | tf_op jit(solution)/shard_map/all_to_all | solution.py:104
  160.9 12.4 %copy-start.1 = (bf16[768]{0:T(1024)(128)(2,1)S(1)}, bf16[768]{0:T(1024)(128)(2,1)}, u32[]{:S(2)}) copy-start(bf16[768]{0:T(1024)(128)(2,1)} %param.9) | copy-start | bytes 4612
  161.0 24.6 %collective-permute-start.9 = (bf16[40,768]{1,0:T(8,128)(2,1)S(1)}, bf16[40,768]{1,0:T(8,128)(2,1)S(1)}, u32[]{:S(2)}, u32[]{:S(2)}) collective-permute-start(bf16[40,768]{1,0:T(8,128)(2,1)S(1)} %reduce_sum.24), channel_id=1, source_target_pairs={{0,1},{1,0},{2,33},{3,32},{8,65},{9,64},{10,97},{11,96},{32,3},{33... | collective-permute-start | bytes 184328 | tf_op jit(solution)/shard_map/ppermute | solution.py:108
  171.4 14.3 %collective-permute-start.10 = (bf16[40,768]{1,0:T(8,128)(2,1)S(1)}, bf16[40,768]{1,0:T(8,128)(2,1)S(1)}, u32[]{:S(2)}, u32[]{:S(2)}) collective-permute-start(bf16[40,768]{1,0:T(8,128)(2,1)S(1)} %reduce_sum.25), channel_id=1, source_target_pairs={{0,0},{1,1},{2,32},{3,33},{8,64},{9,65},{10,96},{11,97},{32,2},{33... | collective-permute-start | bytes 184328 | tf_op jit(solution)/shard_map/ppermute | solution.py:108

commit v10 on v9

--- a/solution.py
+++ b/solution.py
@@ -19,8 +19,14 @@
 barrier = lax.optimization_barrier
 
 
-def corner_pairs(other_zh):
-    return [(i, ((i >> 1) & 3) << 3 | (i >> 3) << 1 | ((i & 1) ^ other_zh)) for i in range(32)]
+def corner_pairs(other_zh, with_zb):
+    pairs = []
+    for i in range(32):
+        zb, c, y0, x0, zh = i >> 4, (i >> 3) & 1, (i >> 2) & 1, (i >> 1) & 1, i & 1
+        if with_zb:
+            zb, y0 = y0, zb
+        pairs.append((i, zb << 4 | x0 << 3 | y0 << 2 | c << 1 | (zh ^ other_zh)))
+    return pairs
 
 
 def slot(block, dz, dc):
@@ -46,14 +52,22 @@
         out[i] = block[...]
 
 
-def first_kernel(here, other, w00, w01, w10, w11a, w11b, part, total):
-    for k, ws in enumerate(((w00,), (w01,), (w10,), (w11a, w11b))):
-        rows = [got[slot(b, k // 2, k % 2)] for b in range(4) for got in (here, other)]
-        left = jnp.concatenate(rows, axis=0)
-        right = ws[0][...] if k < 3 else jnp.concatenate([w[...] for w in ws], axis=0)
-        product = jnp.dot(left, right, preferred_element_type=F32)
-        total[...] = product if k == 0 else total[...] + product
-    part[...] = total[...].astype(BF16).reshape(4, 80, 768)
+def first_kernel(got, w0, w1, keep, send):
+    zb, c = lax.axis_index("zb"), lax.axis_index("c")
+    for out, dy in ((keep, 0), (send, 1)):
+        y0 = jnp.bitwise_xor(zb, dy)
+        total = None
+        for dc, w in enumerate((w0, w1)):
+            x0 = jnp.bitwise_xor(c, dc)
+            rows = [got[(b & 2) * 4 + y0 * 4 + (b & 1) * 2 + x0] for b in range(4)]
+            product = jnp.dot(jnp.concatenate(rows, axis=0), w[...], preferred_element_type=F32)
+            total = product if total is None else total + product
+        out[...] = total.astype(BF16).reshape(4, 40, 768)
+
+
+def pair_kernel(here, here_z, other, other_z, part):
+    part[:, :40] = (here[...].astype(F32) + here_z[...].astype(F32)).astype(BF16)
+    part[:, 40:] = (other[...].astype(F32) + other_z[...].astype(F32)).astype(BF16)
 
 
 def middle_kernel(parts, bias, h):
@@ -73,26 +87,32 @@
 
 
 def shards(tokens, w1, b1, w2, b2):
-    here, other = (lax.ppermute(tokens, CORNER, corner_pairs(k)) for k in range(2))
-    w1_in, w2_in, here = barrier((w1, w2, here))
+    here, other = (lax.ppermute(tokens, CORNER, corner_pairs(k, False)) for k in range(2))
+    w2_in, here = barrier((w2, here))
 
     shape = [(16, 40, 768)]
     (here,) = kernel_call(spread_kernel, shape, 1, 10**9, 1 << 20)(here)
     (other,) = kernel_call(spread_kernel, shape, 1, 40 * 10**9, 1 << 20)(other)
     here = lax.all_to_all(here, PLANE, 0, 0, tiled=True)
     w1_late, _ = barrier((w1, other))
+    w1_c = lax.ppermute(w1_late, "c", SWAP)
     other, _ = barrier((other, here))
     other = lax.all_to_all(other, PLANE, 0, 0, tiled=True)
 
-    w1_z = lax.ppermute(w1_in, "zb", SWAP)
-    w1_all = [w1, lax.ppermute(w1_late, "c", SWAP), w1_z]
-    w1_all += [lax.ppermute(w1_z[at : at + 384], "c", SWAP) for at in (0, 384)]
     w2_z = lax.ppermute(w2_in, "zb", SWAP)
     w2_all = [w2, lax.ppermute(w2_in, "c", SWAP), w2_z, lax.ppermute(w2_z, "c", SWAP)]
 
     flops = 2 * 320 * 3072 * 768
-    scratch = [pltpu.VMEM((320, 768), F32)]
-    (part,) = kernel_call(first_kernel, [(4, 80, 768)], 7, flops, 8 << 20, scratch, 50)(here, other, *w1_all)
+    first = kernel_call(first_kernel, [(4, 40, 768)] * 2, 3, flops // 2, 4 << 20, (), 50)
+    here, _ = barrier((here, w2_z))
+    here, send = first(here, w1, w1_c)
+    send, _ = barrier((send, w2_z))
+    here_z = lax.ppermute(send, "zb", SWAP)
+    other, _ = barrier((other, here_z))
+    other, send = first(other, w1, w1_c)
+    other_z = lax.ppermute(send, "zb", SWAP)
+    pair = kernel_call(pair_kernel, [(4, 80, 768)], 4, 10**6, 1 << 20)
+    (part,) = pair(here, here_z, other, other_z)
     part = lax.all_to_all(part, "zq", 0, 0, tiled=True)
     (h,) = kernel_call(middle_kernel, [(80, 768)], 2, 20 * 80 * 768, 1 << 20)(part, b1.reshape(1, 768))
     hidden = lax.all_gather(h, "zq", axis=0, tiled=False)
@@ -105,7 +125,7 @@
     total = b2.astype(F32)
     for k, out in ((1, other), (0, here)):
         out = out.astype(F32).sum(axis=0).astype(BF16)
-        total = total + lax.ppermute(out, CORNER, corner_pairs(k)).astype(F32)
+        total = total + lax.ppermute(out, CORNER, corner_pairs(k, True)).astype(F32)
     return total.astype(BF16)
 
 

time: 187 us -> 183 us (0.979)
  the two profiles are of different devices: /device:TPU:38 before, /device:TPU:14 now
where the time goes in v10:
time: 183 us; the launch traced here: 182 us
  starting transfers between devices  64.3 us (35%)
  waiting for transfers between devices  61.3 us (33%)
  blocking collectives  43.7 us (24%)
  Pallas kernels  9.57 us (5%)
  local copies, waits for them, and re-layouts  2.22 us (1%)
    all_gather x1, blocking collectives, shards(): hidden = lax.all_gather(h, 'zq', axis=0, tiled=False)  23.8 us
    all_to_all x1, blocking collectives, shards(): other = lax.all_to_all(other, PLANE, 0, 0, tiled=True)  19.9 us
    all_to_all x1, waiting for transfers between devices, shards(): part = lax.all_to_all(part, 'zq', 0, 0, tiled=True)  19 us
    ppermute x2, starting transfers between devices, shards(): lax.ppermute(tokens, CORNER, corner_pairs(k, False))  18.8 us
    all_to_all x2, waiting for transfers between devices, shards(): here = lax.all_to_all(here, PLANE, 0, 0, tiled=True)  18 us
    all_to_all x2, starting transfers between devices, shards(): here = lax.all_to_all(here, PLANE, 0, 0, tiled=True)  14.2 us
    ppermute x2, waiting for transfers between devices, shards(): total = total + lax.ppermute(out, CORNER, corner_pairs(k, True)).astype(F32)  11.8 us
    all_to_all x1, starting transfers between devices, shards(): other = lax.all_to_all(other, PLANE, 0, 0, tiled=True)  7.82 us
  transfers between devices with their start and end apart: 14, of which 7 were waited for; matrix products, arithmetic and copies ran while one was open for 0% of the time, Pallas kernels for 1%

profile of v10, /device:TPU:14, one launch (start us, length us, event | category | flops | bytes accessed | tf_op | source)
XLA Modules:
  0.0 182.3 jit_solution(5923475069789909460)
XLA Ops:
  0.0 2.2 %collective-permute-start = (bf16[40,768]{1,0:T(8,128)(2,1)}, bf16[40,768]{1,0:T(8,128)(2,1)S(1)}, u32[]{:S(2)}, u32[]{:S(2)}) collective-permute-start(bf16[40,768]{1,0:T(8,128)(2,1)} %param.5), channel_id=1, source_target_pairs={{0,0},{1,1},{2,32},{3,33},{8,8},{9,9},{10,40},{11,41},{32,2},{33,3... | collective-permute-start | bytes 184328 | tf_op jit(solution)/shard_map/ppermute | solution.py:90
  2.2 16.6 %collective-permute-start.2 = (bf16[40,768]{1,0:T(8,128)(2,1)}, bf16[40,768]{1,0:T(8,128)(2,1)S(1)}, u32[]{:S(2)}, u32[]{:S(2)}) collective-permute-start(bf16[40,768]{1,0:T(8,128)(2,1)} %param.5), channel_id=1, source_target_pairs={{0,1},{1,0},{2,33},{3,32},{8,9},{9,8},{10,41},{11,40},{32,3},{33,2... | collective-permute-start | bytes 184328 | tf_op jit(solution)/shard_map/ppermute | solution.py:90
  18.8 2.9 %collective-permute-start.1 = (bf16[768,768]{1,0:T(8,128)(2,1)}, bf16[768,768]{1,0:T(8,128)(2,1)}, u32[]{:S(2)}, u32[]{:S(2)}) collective-permute-start(bf16[768,768]{1,0:T(8,128)(2,1)} %w00.1), channel_id=1, source_target_pairs={{0,64},{64,0},{1,65},{65,1},{2,66},{66,2},{3,67},{67,3},{4,68},{68... | collective-permute-start | bytes 3538952 | tf_op jit(solution)/shard_map/ppermute | solution.py:102
  22.8 7.0 %all-to-all-start = ((bf16[16,40,768]{2,1,0:T(8,128)(2,1)}), bf16[16,40,768]{2,1,0:T(8,128)(2,1)S(1)}, u32[]{:S(2)}, u32[]{:S(2)}) async-start(bf16[16,40,768]{2,1,0:T(8,128)(2,1)} %shard_map.55), calls=%async_computation | async-start | bytes 1966080 | tf_op jit(solution)/shard_map/all_to_all | solution.py:96
  31.5 1.9 %collective-permute-start.3 = (bf16[768,768]{1,0:T(8,128)(2,1)S(1)}, bf16[768,768]{1,0:T(8,128)(2,1)S(1)}, u32[]{:S(2)}, u32[]{:S(2)}) collective-permute-start(bf16[768,768]{1,0:T(8,128)(2,1)S(1)} %copy-done), channel_id=1, source_target_pairs={{0,32},{32,0},{1,33},{33,1},{2,34},{34,2},{3,35},{35,3},{4,36},{36... | collective-permute-start | bytes 3538952 | tf_op jit(solution)/shard_map/ppermute | solution.py:98
  33.4 9.7 %all-to-all-done.got = bf16[16,40,768]{2,1,0:T(8,128)(2,1)S(1)} async-done(((bf16[16,40,768]{2,1,0:T(8,128)(2,1)}), bf16[16,40,768]{2,1,0:T(8,128)(2,1)S(1)}, u32[]{:S(2)}, u32[]{:S(2)}) %all-to-all-start) | async-done | bytes 983072 | tf_op jit(solution)/shard_map/all_to_all | solution.py:96
  43.1 7.8 %all-to-all-start.1 = ((bf16[16,40,768]{2,1,0:T(8,128)(2,1)}), bf16[16,40,768]{2,1,0:T(8,128)(2,1)}, u32[]{:S(2)}, u32[]{:S(2)}) async-start(bf16[16,40,768]{2,1,0:T(8,128)(2,1)} %copy-done.1), calls=%async_computation.1 | async-start | bytes 1966080 | tf_op jit(solution)/shard_map/all_to_all | solution.py:100
  52.5 3.0 %collective-permute-start.4 = (bf16[4,40,768]{2,1,0:T(8,128)(2,1)S(1)}, bf16[4,40,768]{2,1,0:T(8,128)(2,1)S(1)}, u32[]{:S(2)}, u32[]{:S(2)}) collective-permute-start(bf16[4,40,768]{2,1,0:T(8,128)(2,1)S(1)} %get-tuple-element.25), channel_id=1, source_target_pairs={{0,64},{64,0},{1,65},{65,1},{2,66},{66,2},{3,67},{67,3},{4,68},{68... | collective-permute-start | bytes 737288 | tf_op jit(solution)/shard_map/ppermute | solution.py:110
  55.6 5.8 %collective-permute-done.4.here_z = bf16[4,40,768]{2,1,0:T(8,128)(2,1)S(1)} collective-permute-done((bf16[4,40,768]{2,1,0:T(8,128)(2,1)S(1)}, bf16[4,40,768]{2,1,0:T(8,128)(2,1)S(1)}, u32[]{:S(2)}, u32[]{:S(2)}) %collective-permute-start.4) | collective-permute-done | bytes 245792 | tf_op jit(solution)/shard_map/ppermute | solution.py:110
  62.9 2.1 %shard_map.58 = (bf16[4,40,768]{2,1,0:T(8,128)(2,1)S(1)}, bf16[4,40,768]{2,1,0:T(8,128)(2,1)S(1)}) custom-call(bf16[16,40,768]{2,1,0:T(8,128)(2,1)} %all-to-all-done.1.got, bf16[768,768]{1,0:T(8,128)(2,1)S(1)} %copy-done, bf16[768,768]{1,0:T(8,128)(2,1)S(1)} %collective-permute-done.3.w1), custom_call_target="tpu_custom_call" | custom-call | flops 754974720 | bytes 4194304 | tf_op jit(solution)/shard_map/pallas_call | solution.py:112
  65.1 2.9 %collective-permute-start.5 = (bf16[4,40,768]{2,1,0:T(8,128)(2,1)S(1)}, bf16[4,40,768]{2,1,0:T(8,128)(2,1)S(1)}, u32[]{:S(2)}, u32[]{:S(2)}) collective-permute-start(bf16[4,40,768]{2,1,0:T(8,128)(2,1)S(1)} %get-tuple-element.29), channel_id=1, source_target_pairs={{0,64},{64,0},{1,65},{65,1},{2,66},{66,2},{3,67},{67,3},{4,68},{68... | collective-permute-start | bytes 737288 | tf_op jit(solution)/shard_map/ppermute | solution.py:113
  68.0 5.2 %collective-permute-done.5.other_z = bf16[4,40,768]{2,1,0:T(8,128)(2,1)S(1)} collective-permute-done((bf16[4,40,768]{2,1,0:T(8,128)(2,1)S(1)}, bf16[4,40,768]{2,1,0:T(8,128)(2,1)S(1)}, u32[]{:S(2)}, u32[]{:S(2)}) %collective-permute-start.5) | collective-permute-done | bytes 245792 | tf_op jit(solution)/shard_map/ppermute | solution.py:113
  74.1 4.6 %all-to-all-start.2 = ((bf16[4,80,768]{2,1,0:T(8,128)(2,1)}), bf16[4,80,768]{2,1,0:T(8,128)(2,1)S(1)}, u32[]{:S(2)}, u32[]{:S(2)}) async-start(bf16[4,80,768]{2,1,0:T(8,128)(2,1)} %shard_map.59), calls=%async_computation.2 | async-start | bytes 983040 | tf_op jit(solution)/shard_map/all_to_all | solution.py:116
  78.7 1.9 %collective-permute-start.6 = (bf16[768,768]{1,0:T(8,128)(2,1)S(1)}, bf16[768,768]{1,0:T(8,128)(2,1)S(1)}, u32[]{:S(2)}, u32[]{:S(2)}) collective-permute-start(bf16[768,768]{1,0:T(8,128)(2,1)S(1)} %copy-done.4), channel_id=1, source_target_pairs={{0,32},{32,0},{1,33},{33,1},{2,34},{34,2},{3,35},{35,3},{4,36},{36... | collective-permute-start | bytes 3538952 | tf_op jit(solution)/shard_map/ppermute | solution.py:103
  80.6 2.4 %collective-permute-start.7 = (bf16[768,768]{1,0:T(8,128)(2,1)}, bf16[768,768]{1,0:T(8,128)(2,1)}, u32[]{:S(2)}, u32[]{:S(2)}) collective-permute-start(bf16[768,768]{1,0:T(8,128)(2,1)} %collective-permute-done.1.w10), channel_id=1, source_target_pairs={{0,32},{32,0},{1,33},{33,1},{2,34},{34,2},{3,35},{35,3},{4,36},{36... | collective-permute-start | bytes 3538952 | tf_op jit(solution)/shard_map/ppermute | solution.py:103
  83.0 19.0 %all-to-all-done.2.parts = bf16[4,80,768]{2,1,0:T(8,128)(2,1)S(1)} async-done(((bf16[4,80,768]{2,1,0:T(8,128)(2,1)}), bf16[4,80,768]{2,1,0:T(8,128)(2,1)S(1)}, u32[]{:S(2)}, u32[]{:S(2)}) %all-to-all-start.2) | async-done | bytes 491552 | tf_op jit(solution)/shard_map/all_to_all | solution.py:116
  102.1 23.8 %all-gather = bf16[320,768]{1,0:T(8,128)(2,1)S(1)} all-gather(bf16[80,768]{1,0:T(8,128)(2,1)S(1)} %shard_map.60), channel_id=2, replica_groups=mesh['zq'=4,'zb'=2,'c'=2,'yp'=2,'y0'=2,'xp'=2,'x0'=2,'zh'=2] {'zq'}, dimensions={0}, use_global_device_ids=true | all-gather | bytes 614400 | tf_op jit(solution)/shard_map/all_gather | solution.py:118
  125.9 4.3 %shard_map.61 = (bf16[16,40,768]{2,1,0:T(8,128)(2,1)}, bf16[16,40,768]{2,1,0:T(8,128)(2,1)S(1)}) custom-call(bf16[4,80,768]{2,1,0:T(8,128)(2,1)S(1)} %bitcast.1, bf16[768,768]{1,0:T(8,128)(2,1)S(1)} %copy-done.4, bf16[768,768]{1,0:T(8,128)(2,1)S(1)} %collective-permute-done.6.w01, bf16[768,768]{1,0:T(8,128)(2,1)} %collective-permute-done.1.w10, ...), custom_call_target="tpu_custom_call" | custom-call | flops 1509949440 | bytes 8388608 | tf_op jit(solution)/shard_map/pallas_call | solution.py:120
  130.2 19.9 %all_to_all.25 = bf16[16,40,768]{2,1,0:T(8,128)(2,1)S(1)} all-to-all(bf16[16,40,768]{2,1,0:T(8,128)(2,1)S(1)} %get-tuple-element.30), channel_id=1, replica_groups=mesh['zq'=4,'zb'=2,'c'=2,'yp'=2,'y0'=2,'xp'=2,'x0'=2,'zh'=2] {'yp','y0',..., dimensions={0} | all-to-all | bytes 1966080 | tf_op jit(solution)/shard_map/all_to_all | solution.py:122
  150.2 7.1 %all-to-all-start.4 = ((bf16[16,40,768]{2,1,0:T(8,128)(2,1)}), bf16[16,40,768]{2,1,0:T(8,128)(2,1)S(1)}, u32[]{:S(2)}, u32[]{:S(2)}) async-start(bf16[16,40,768]{2,1,0:T(8,128)(2,1)} %get-tuple-element.32), calls=%async_computation.4 | async-start | bytes 1966080 | tf_op jit(solution)/shard_map/all_to_all | solution.py:124
  157.4 1.9 %collective-permute-start.8 = (bf16[40,768]{1,0:T(8,128)(2,1)S(1)}, bf16[40,768]{1,0:T(8,128)(2,1)S(1)}, u32[]{:S(2)}, u32[]{:S(2)}) collective-permute-start(bf16[40,768]{1,0:T(8,128)(2,1)S(1)} %reduce_sum.24), channel_id=1, source_target_pairs={{0,1},{1,0},{2,33},{3,32},{8,65},{9,64},{10,97},{11,96},{32,3},{33... | collective-permute-start | bytes 184328 | tf_op jit(solution)/shard_map/ppermute | solution.py:128
  159.4 8.3 %all-to-all-done.4 = bf16[16,40,768]{2,1,0:T(8,128)(2,1)S(1)} async-done(((bf16[16,40,768]{2,1,0:T(8,128)(2,1)}), bf16[16,40,768]{2,1,0:T(8,128)(2,1)S(1)}, u32[]{:S(2)}, u32[]{:S(2)}) %all-to-all-start.4) | async-done | bytes 983072 | tf_op jit(solution)/shard_map/all_to_all | solution.py:124
  167.9 1.9 %collective-permute-start.9 = (bf16[40,768]{1,0:T(8,128)(2,1)S(1)}, bf16[40,768]{1,0:T(8,128)(2,1)S(1)}, u32[]{:S(2)}, u32[]{:S(2)}) collective-permute-start(bf16[40,768]{1,0:T(8,128)(2,1)S(1)} %reduce_sum.25), channel_id=1, source_target_pairs={{0,0},{1,1},{2,32},{3,33},{8,64},{9,65},{10,96},{11,97},{32,2},{33... | collective-permute-start | bytes 184328 | tf_op jit(solution)/shard_map/ppermute | solution.py:128
  169.8 11.8 %collective-permute-done.8 = bf16[40,768]{1,0:T(8,128)(2,1)S(1)} collective-permute-done((bf16[40,768]{1,0:T(8,128)(2,1)S(1)}, bf16[40,768]{1,0:T(8,128)(2,1)S(1)}, u32[]{:S(2)}, u32[]{:S(2)}) %collective-permute-start.8) | collective-permute-done | bytes 61472 | tf_op jit(solution)/shard_map/ppermute | solution.py:128
  (32 shorter events, 7.9 us)
Async XLA Ops:
  0.0 18.8 %collective-permute-start = (bf16[40,768]{1,0:T(8,128)(2,1)}, bf16[40,768]{1,0:T(8,128)(2,1)S(1)}, u32[]{:S(2)}, u32[]{:S(2)}) collective-permute-start(bf16[40,768]{1,0:T(8,128)(2,1)} %param.5), channel_id=1, source_target_pairs={{0,0},{1,1},{2,32},{3,33},{8,8},{9,9},{10,40},{11,41},{32,2},{33,3... | collective-permute-start | bytes 184328 | tf_op jit(solution)/shard_map/ppermute | solution.py:90
  2.2 27.7 %collective-permute-start.2 = (bf16[40,768]{1,0:T(8,128)(2,1)}, bf16[40,768]{1,0:T(8,128)(2,1)S(1)}, u32[]{:S(2)}, u32[]{:S(2)}) collective-permute-start(bf16[40,768]{1,0:T(8,128)(2,1)} %param.5), channel_id=1, source_target_pairs={{0,1},{1,0},{2,33},{3,32},{8,9},{9,8},{10,41},{11,40},{32,3},{33,2... | collective-permute-start | bytes 184328 | tf_op jit(solution)/shard_map/ppermute | solution.py:90
  18.8 32.1 %collective-permute-start.1 = (bf16[768,768]{1,0:T(8,128)(2,1)}, bf16[768,768]{1,0:T(8,128)(2,1)}, u32[]{:S(2)}, u32[]{:S(2)}) collective-permute-start(bf16[768,768]{1,0:T(8,128)(2,1)} %w00.1), channel_id=1, source_target_pairs={{0,64},{64,0},{1,65},{65,1},{2,66},{66,2},{3,67},{67,3},{4,68},{68... | collective-permute-start | bytes 3538952 | tf_op jit(solution)/shard_map/ppermute | solution.py:102
  22.8 20.3 %all-to-all-start = ((bf16[16,40,768]{2,1,0:T(8,128)(2,1)}), bf16[16,40,768]{2,1,0:T(8,128)(2,1)S(1)}, u32[]{:S(2)}, u32[]{:S(2)}) async-start(bf16[16,40,768]{2,1,0:T(8,128)(2,1)} %shard_map.55), calls=%async_computation | async-start | bytes 1966080 | tf_op jit(solution)/shard_map/all_to_all | solution.py:96
  29.8 1.6 copy-start
  29.9 0.9 copy-start.1
  31.5 19.4 %collective-permute-start.3 = (bf16[768,768]{1,0:T(8,128)(2,1)S(1)}, bf16[768,768]{1,0:T(8,128)(2,1)S(1)}, u32[]{:S(2)}, u32[]{:S(2)}) collective-permute-start(bf16[768,768]{1,0:T(8,128)(2,1)S(1)} %copy-done), channel_id=1, source_target_pairs={{0,32},{32,0},{1,33},{33,1},{2,34},{34,2},{3,35},{35,3},{4,36},{36... | collective-permute-start | bytes 3538952 | tf_op jit(solution)/shard_map/ppermute | solution.py:98
  43.1 19.9 %all-to-all-start.1 = ((bf16[16,40,768]{2,1,0:T(8,128)(2,1)}), bf16[16,40,768]{2,1,0:T(8,128)(2,1)}, u32[]{:S(2)}, u32[]{:S(2)}) async-start(bf16[16,40,768]{2,1,0:T(8,128)(2,1)} %copy-done.1), calls=%async_computation.1 | async-start | bytes 1966080 | tf_op jit(solution)/shard_map/all_to_all | solution.py:100
  51.9 0.7 copy-start.2
  52.5 20.6 %copy-start.3 = (bf16[4,40,768]{2,1,0:T(8,128)(2,1)S(1)}, bf16[4,40,768]{2,1,0:T(8,128)(2,1)}, u32[]{:S(2)}) copy-start(bf16[4,40,768]{2,1,0:T(8,128)(2,1)} %copy-done.2) | copy-start | bytes 737284
  52.5 8.8 %collective-permute-start.4 = (bf16[4,40,768]{2,1,0:T(8,128)(2,1)S(1)}, bf16[4,40,768]{2,1,0:T(8,128)(2,1)S(1)}, u32[]{:S(2)}, u32[]{:S(2)}) collective-permute-start(bf16[4,40,768]{2,1,0:T(8,128)(2,1)S(1)} %get-tuple-element.25), channel_id=1, source_target_pairs={{0,64},{64,0},{1,65},{65,1},{2,66},{66,2},{3,67},{67,3},{4,68},{68... | collective-permute-start | bytes 737288 | tf_op jit(solution)/shard_map/ppermute | solution.py:110
  65.1 8.1 %collective-permute-start.5 = (bf16[4,40,768]{2,1,0:T(8,128)(2,1)S(1)}, bf16[4,40,768]{2,1,0:T(8,128)(2,1)S(1)}, u32[]{:S(2)}, u32[]{:S(2)}) collective-permute-start(bf16[4,40,768]{2,1,0:T(8,128)(2,1)S(1)} %get-tuple-element.29), channel_id=1, source_target_pairs={{0,64},{64,0},{1,65},{65,1},{2,66},{66,2},{3,67},{67,3},{4,68},{68... | collective-permute-start | bytes 737288 | tf_op jit(solution)/shard_map/ppermute | solution.py:113
  73.2 5.5 %copy-start.4 = (bf16[768,768]{1,0:T(8,128)(2,1)S(1)}, bf16[768,768]{1,0:T(8,128)(2,1)}, u32[]{:S(2)}) copy-start(bf16[768,768]{1,0:T(8,128)(2,1)} %w00.1) | copy-start | bytes 3538948
  73.2 9.8 %copy-start.6 = (bf16[768]{0:T(1024)(128)(2,1)S(1)}, bf16[768]{0:T(1024)(128)(2,1)}, u32[]{:S(2)}) copy-start(bf16[768]{0:T(1024)(128)(2,1)} %param.7) | copy-start | bytes 4612
  74.1 27.9 %all-to-all-start.2 = ((bf16[4,80,768]{2,1,0:T(8,128)(2,1)}), bf16[4,80,768]{2,1,0:T(8,128)(2,1)S(1)}, u32[]{:S(2)}, u32[]{:S(2)}) async-start(bf16[4,80,768]{2,1,0:T(8,128)(2,1)} %shard_map.59), calls=%async_computation.2 | async-start | bytes 983040 | tf_op jit(solution)/shard_map/all_to_all | solution.py:116
  78.7 47.3 %collective-permute-start.6 = (bf16[768,768]{1,0:T(8,128)(2,1)S(1)}, bf16[768,768]{1,0:T(8,128)(2,1)S(1)}, u32[]{:S(2)}, u32[]{:S(2)}) collective-permute-start(bf16[768,768]{1,0:T(8,128)(2,1)S(1)} %copy-done.4), channel_id=1, source_target_pairs={{0,32},{32,0},{1,33},{33,1},{2,34},{34,2},{3,35},{35,3},{4,36},{36... | collective-permute-start | bytes 3538952 | tf_op jit(solution)/shard_map/ppermute | solution.py:103
  80.6 45.4 %collective-permute-start.7 = (bf16[768,768]{1,0:T(8,128)(2,1)}, bf16[768,768]{1,0:T(8,128)(2,1)}, u32[]{:S(2)}, u32[]{:S(2)}) collective-permute-start(bf16[768,768]{1,0:T(8,128)(2,1)} %collective-permute-done.1.w10), channel_id=1, source_target_pairs={{0,32},{32,0},{1,33},{33,1},{2,34},{34,2},{3,35},{35,3},{4,36},{36... | collective-permute-start | bytes 3538952 | tf_op jit(solution)/shard_map/ppermute | solution.py:103
  150.2 17.6 %all-to-all-start.4 = ((bf16[16,40,768]{2,1,0:T(8,128)(2,1)}), bf16[16,40,768]{2,1,0:T(8,128)(2,1)S(1)}, u32[]{:S(2)}, u32[]{:S(2)}) async-start(bf16[16,40,768]{2,1,0:T(8,128)(2,1)} %get-tuple-element.32), calls=%async_computation.4 | async-start | bytes 1966080 | tf_op jit(solution)/shard_map/all_to_all | solution.py:124
  157.3 12.5 %copy-start.5 = (bf16[768]{0:T(1024)(128)(2,1)S(1)}, bf16[768]{0:T(1024)(128)(2,1)}, u32[]{:S(2)}) copy-start(bf16[768]{0:T(1024)(128)(2,1)} %param.9) | copy-start | bytes 4612
  157.4 24.2 %collective-permute-start.8 = (bf16[40,768]{1,0:T(8,128)(2,1)S(1)}, bf16[40,768]{1,0:T(8,128)(2,1)S(1)}, u32[]{:S(2)}, u32[]{:S(2)}) collective-permute-start(bf16[40,768]{1,0:T(8,128)(2,1)S(1)} %reduce_sum.24), channel_id=1, source_target_pairs={{0,1},{1,0},{2,33},{3,32},{8,65},{9,64},{10,97},{11,96},{32,3},{33... | collective-permute-start | bytes 184328 | tf_op jit(solution)/shard_map/ppermute | solution.py:128
  167.9 13.8 %collective-permute-start.9 = (bf16[40,768]{1,0:T(8,128)(2,1)S(1)}, bf16[40,768]{1,0:T(8,128)(2,1)S(1)}, u32[]{:S(2)}, u32[]{:S(2)}) collective-permute-start(bf16[40,768]{1,0:T(8,128)(2,1)S(1)} %reduce_sum.25), channel_id=1, source_target_pairs={{0,0},{1,1},{2,32},{3,33},{8,64},{9,65},{10,96},{11,97},{32,2},{33... | collective-permute-start | bytes 184328 | tf_op jit(solution)/shard_map/ppermute | solution.py:128
